TPU v7x, 32 devices: a whole 2x2x4 slice. The times are simulated.
32 devices in a mesh: seq: 8 (over z, x), dp: 4 (over y, core).
Axes of the slice: x: 2, y: 2, z: 4, core: 2. Of those that a mesh axis runs over, the one named last changes fastest.
Arguments:
- tokens: bfloat16 [4, 2048, 2048], P('dp', 'seq'), may hold values from -6 to 6
- output_gradient: bfloat16 [4, 2048, 2048], P('dp', 'seq'), may hold values from -6 to 6
- sequence_adapter_index: int32 [4], P('dp'), may hold values from 0 to 7
- time_projection_weights: bfloat16 [4, 2048, 2048], P(None, None, ('seq', 'dp')), may hold values from -0.125 to 0.125
- branch_first_weights: bfloat16 [2048, 448], P(('seq', 'dp')), may hold values from -0.125 to 0.125
- branch_second_weights: bfloat16 [448, 2048], P(None, ('seq', 'dp')), may hold values from -0.375 to 0.375
- vectors: bfloat16 [18, 2048], P(None, ('seq', 'dp')), may hold values from -7.5 to 1.5
- channel_key_weight: bfloat16 [2048, 8192], P(None, ('seq', 'dp')), may hold values from -0.125 to 0.125
- channel_value_weight: bfloat16 [8192, 2048], P(('seq', 'dp')), may hold values from -0.0625 to 0.0625
- model_adapter_rows: bfloat16 [8, 160, 2048], P(None, None, ('seq', 'dp')), may hold values from -0.125 to 0.125
- hidden_adapter_rows: bfloat16 [8, 32, 8192], P(None, None, ('seq', 'dp')), may hold values from -0.0625 to 0.0625
Outputs:
- out: bfloat16 [4, 2048, 2048], P('dp', 'seq')
- grad_tokens: float32 [4, 2048, 2048], P('dp', 'seq')
- grad_adapter_model: float32 [8, 160, 2048], P(None, None, ('seq', 'dp'))
- grad_adapter_hidden: float32 [8, 32, 8192], P(None, None, ('seq', 'dp'))
All inputs are finite; a program needn't handle non-finite values.
Results may differ from a plain program's by a relative error of at most 0.012.
The roundings to bfloat16 on the way count: a program that leaves them out, or rounds other values in their place, can miss the bound.
Values may be sent and summed in bfloat16 or wider, within the bound.
A program may use at most 640 MiB of HBM per device.

v0:
```python
from functools import partial

import jax
import jax.numpy as jnp
from jax import lax
from jax.sharding import PartitionSpec as P

ATTENTION_DIM = 64
DECAY_INNER = 96
RATE_INNER = 96
RANK = 16


PRECISE = lax.Precision.HIGHEST
ADAPT_SCALE = 4.0
NORM_EPS = 1e-05
GROUP_EPS = 0.00064
UNIT_EPS = 1e-06


def shifted(block, axis, distance):
    devices = range(lax.axis_size(axis))
    route = [(i - distance, i) for i in devices if i - distance in devices]
    return lax.ppermute(block, axis, route)


def layer_norm(values, gain_row, shift_row):
    centre = values - jnp.mean(values, axis=-1, keepdims=True)
    spread = jnp.mean(centre * centre, axis=-1, keepdims=True)
    return centre * lax.rsqrt(spread + NORM_EPS) * gain_row + shift_row


def six_mixes(values, edge_row, stacked_parameter_lines):
    change = jnp.concatenate([edge_row, values[:, :-1]], axis=1) - values
    return jnp.stack([values + change * stacked_parameter_lines[2 + number] for number in range(6)])


def chan_mixing(values, edge_row, mix_row):
    change = jnp.concatenate([edge_row, values[:, :-1]], axis=1) - values
    return values + change * mix_row


def adapted(inputs, weight, down_rows, up_rows):
    hidden = jnp.einsum(
        "bpd,brd->bpr", inputs, down_rows, preferred_element_type=jnp.float32
    ).astype(jnp.bfloat16)
    direct = jnp.einsum("bpd,do->bpo", inputs, weight, preferred_element_type=jnp.float32)
    return (
        direct
        + ADAPT_SCALE
        * jnp.einsum("bpr,bro->bpo", hidden, up_rows, preferred_element_type=jnp.float32),
        hidden,
    )


def adapted_back(gradient, inputs, weight, down_rows, up_rows, hidden):
    grad_low = gradient.astype(jnp.bfloat16)
    grad_up = ADAPT_SCALE * jnp.einsum(
        "bpr,bpo->bro", hidden, grad_low, preferred_element_type=jnp.float32
    )
    grad_hidden = (
        ADAPT_SCALE
        * jnp.einsum("bpo,bro->bpr", grad_low, up_rows, preferred_element_type=jnp.float32)
    ).astype(jnp.bfloat16)
    grad_down = jnp.einsum("bpr,bpd->brd", grad_hidden, inputs, preferred_element_type=jnp.float32)
    grad_in = jnp.einsum("bpo,do->bpd", grad_low, weight, preferred_element_type=jnp.float32)
    grad_in = grad_in + jnp.einsum(
        "bpr,brd->bpd", grad_hidden, down_rows, preferred_element_type=jnp.float32
    )
    return (grad_in, grad_down, grad_up)


def to_heads(values):
    return values.reshape(
        values.shape[0], values.shape[1], values.shape[2] // ATTENTION_DIM, ATTENTION_DIM
    )


def flatten_state(values):
    return values.reshape(values.shape[0], -1, 128)


def time_mixer_forward(
    acceptance_entries,
    decay_branch,
    unscaled_keys,
    raw_payload_entries,
    rate_branch,
    stacked_parameter_lines,
    span_length,
):
    sequences_present, piece_length, inner_width = acceptance_entries.shape
    head_count = inner_width // ATTENTION_DIM
    span_count = piece_length // span_length
    logarithm_rate = -jax.nn.softplus(-(stacked_parameter_lines[8] + decay_branch)) - 0.5
    log_decay = -jnp.exp(logarithm_rate)
    context_rate = jax.nn.sigmoid(stacked_parameter_lines[9] + rate_branch)
    unit_key = to_heads(unscaled_keys * stacked_parameter_lines[10])
    unit_key = unit_key * lax.rsqrt(jnp.sum(unit_key * unit_key, axis=-1, keepdims=True) + UNIT_EPS)
    adjusted_lookup_entries = unscaled_keys * (
        1.0 + (context_rate - 1.0) * stacked_parameter_lines[11]
    )

    def blocks(values):
        return values.reshape(
            sequences_present, span_count, span_length, head_count, ATTENTION_DIM
        ).transpose(1, 0, 3, 2, 4)

    pieces_all = (
        blocks(to_heads(acceptance_entries)),
        blocks(to_heads(log_decay)),
        blocks(-unit_key),
        blocks(unit_key * to_heads(context_rate)),
        blocks(to_heads(adjusted_lookup_entries)),
        blocks(to_heads(raw_payload_entries)),
    )
    position = jnp.arange(span_length)
    strict = (position[:, None] > position[None, :]).astype(jnp.float32)
    inclusive = (position[:, None] >= position[None, :]).astype(jnp.float32)
    identity = jnp.eye(span_length, dtype=jnp.float32)
    rounds = max(1, (span_length - 1).bit_length())
    precise_sum = partial(jnp.einsum, precision=PRECISE)

    def one_span(memory, pieces):
        recv_b, logd_b, pull_b, push_b, key_b, value_b = pieces
        cum_log = jnp.cumsum(logd_b, axis=2)
        before = cum_log - logd_b
        last_row = cum_log[:, :, -1:, :]
        pull_q = pull_b * jnp.exp(before)
        recv_q = recv_b * jnp.exp(cum_log)
        push_q = push_b * jnp.exp(-cum_log)
        key_q = key_b * jnp.exp(-cum_log)
        push_c = push_b * jnp.exp(last_row - cum_log)
        key_c = key_b * jnp.exp(last_row - cum_log)
        mat_push = precise_sum("bhtc,bhsc->bhts", pull_q, push_q) * strict
        mat_key = precise_sum("bhtc,bhsc->bhts", pull_q, key_q) * strict
        out_push = precise_sum("bhtc,bhsc->bhts", recv_q, push_q) * inclusive
        out_key = precise_sum("bhtc,bhsc->bhts", recv_q, key_q) * inclusive
        value_pad = jnp.concatenate([value_b, jnp.zeros_like(value_b)], axis=-1)
        right_side = precise_sum("bhtc,bhvc->bhtv", pull_q, memory) + precise_sum(
            "bhts,bhsv->bhtv", mat_key, value_pad
        )
        solver = identity + mat_push
        powered = mat_push
        for _ in range(rounds - 1):
            powered = precise_sum("bhts,bhsu->bhtu", powered, powered)
            solver = solver + precise_sum("bhts,bhsu->bhtu", solver, powered)
        pulled = precise_sum("bhts,bhsv->bhtv", solver, right_side)
        outputs = precise_sum("bhtc,bhvc->bhtv", recv_q, memory)
        outputs = (
            outputs
            + precise_sum("bhts,bhsv->bhtv", out_push, pulled)
            + precise_sum("bhts,bhsv->bhtv", out_key, value_pad)
        )
        memory = memory * jnp.exp(last_row) + precise_sum("bhsv,bhsc->bhvc", pulled, push_c)
        memory = memory + precise_sum("bhsv,bhsc->bhvc", value_pad, key_c)
        return (memory, outputs)

    initial = jnp.concatenate(
        [
            jnp.zeros((ATTENTION_DIM, ATTENTION_DIM), jnp.float32),
            jnp.eye(ATTENTION_DIM, dtype=jnp.float32),
        ],
        axis=0,
    )
    initial = jnp.broadcast_to(
        initial, (sequences_present, head_count, 2 * ATTENTION_DIM, ATTENTION_DIM)
    )
    ending, outputs = lax.scan(one_span, initial, pieces_all)
    outputs = outputs.transpose(1, 2, 0, 3, 4).reshape(
        sequences_present, head_count, piece_length, 2 * ATTENTION_DIM
    )
    return (
        outputs[..., :ATTENTION_DIM],
        outputs[..., ATTENTION_DIM:],
        ending,
        adjusted_lookup_entries,
    )


def mixer_back(
    local_out,
    direction,
    state_in,
    acceptance_entries,
    adjusted_lookup_entries,
    raw_payload_entries,
    sigmoid_filter_entries,
    stacked_parameter_lines,
):
    sequences_present, piece_length, inner_width = acceptance_entries.shape
    head_count = inner_width // ATTENTION_DIM
    whole_out = local_out + jnp.einsum("bhvk,bhtk->bhtv", state_in, direction, precision=PRECISE)
    mixed_out = whole_out.transpose(0, 2, 1, 3)
    centre = mixed_out - jnp.mean(mixed_out, axis=-1, keepdims=True)
    spread = jnp.mean(centre * centre, axis=-1, keepdims=True)
    groupwise_standardized = centre * lax.rsqrt(spread + GROUP_EPS) * stacked_parameter_lines[
        13
    ].reshape(head_count, ATTENTION_DIM) + stacked_parameter_lines[14].reshape(
        head_count, ATTENTION_DIM
    )
    diagonal_reward_addend = jnp.sum(
        to_heads(acceptance_entries)
        * to_heads(adjusted_lookup_entries)
        * stacked_parameter_lines[12].reshape(head_count, ATTENTION_DIM),
        axis=-1,
        keepdims=True,
    ) * to_heads(raw_payload_entries)
    return (groupwise_standardized + diagonal_reward_addend).reshape(
        sequences_present, piece_length, inner_width
    ) * sigmoid_filter_entries


def body(
    tokens,
    output_gradient,
    sequence_adapter_index,
    time_projection_weights,
    branch_first_weights,
    branch_second_weights,
    vectors,
    channel_key_weight,
    channel_value_weight,
    model_adapter_rows,
    hidden_adapter_rows,
):
    sequences_present, piece_length, inner_width = tokens.shape
    span_length = 16
    rate_first_matrix = DECAY_INNER
    gate_first_matrix = DECAY_INNER + RATE_INNER
    mat_all, down_all, up_all, vector_low, model_all = (
        lax.all_gather(time_projection_weights, ("seq", "dp"), axis=2, tiled=True),
        lax.all_gather(branch_first_weights, ("seq", "dp"), axis=0, tiled=True),
        lax.all_gather(branch_second_weights, ("seq", "dp"), axis=1, tiled=True),
        lax.all_gather(vectors, ("seq", "dp"), axis=1, tiled=True),
        lax.all_gather(model_adapter_rows, ("seq", "dp"), axis=2, tiled=True),
    )
    stacked_parameter_lines = vector_low.astype(jnp.float32)
    pick_mask = (
        sequence_adapter_index[:, None] == jnp.arange(model_all.shape[0], dtype=jnp.int32)[None, :]
    )
    pick_low = pick_mask.astype(jnp.bfloat16)
    pick_full = pick_mask.astype(jnp.float32)
    chosen = jnp.einsum(
        "ba,arx->brx", pick_low, model_all, preferred_element_type=jnp.float32
    ).astype(jnp.bfloat16)
    tokens_wide = tokens.astype(jnp.float32)

    def norm_first(values):
        return layer_norm(values, stacked_parameter_lines[0], stacked_parameter_lines[1])

    normed, norm_pull = jax.vjp(norm_first, tokens_wide)
    edge_row = shifted(normed[:, -1:, :], "seq", 1)

    def mixes(values, edge_vals):
        return six_mixes(values, edge_vals, stacked_parameter_lines)

    mixed_wide, mix_pull = jax.vjp(mixes, normed, edge_row)
    mixed = mixed_wide.astype(jnp.bfloat16)
    mix_r, decay_mix_weight, mix_k, mix_v, rate_mix_weight, gate_mix_weight = (
        mixed[number] for number in range(6)
    )
    acceptance_entries, hid_recv = adapted(
        mix_r, mat_all[0], chosen[:, 0:RANK], chosen[:, 5 * RANK : 6 * RANK]
    )
    unscaled_keys, hid_keys = adapted(
        mix_k, mat_all[1], chosen[:, RANK : 2 * RANK], chosen[:, 6 * RANK : 7 * RANK]
    )
    raw_payload_entries, hid_values = adapted(
        mix_v, mat_all[2], chosen[:, 2 * RANK : 3 * RANK], chosen[:, 7 * RANK : 8 * RANK]
    )
    decay_preactivation = jnp.einsum(
        "bpd,dl->bpl",
        decay_mix_weight,
        down_all[:, :rate_first_matrix],
        preferred_element_type=jnp.float32,
    )
    decay_act = jnp.tanh(decay_preactivation)
    decay_branch = jnp.einsum(
        "bpl,ld->bpd",
        decay_act.astype(jnp.bfloat16),
        up_all[:rate_first_matrix],
        preferred_element_type=jnp.float32,
    )
    rate_preactivation = jnp.einsum(
        "bpd,dl->bpl",
        rate_mix_weight,
        down_all[:, rate_first_matrix:gate_first_matrix],
        preferred_element_type=jnp.float32,
    ).astype(jnp.bfloat16)
    rate_branch = jnp.einsum(
        "bpl,ld->bpd",
        rate_preactivation,
        up_all[rate_first_matrix:gate_first_matrix],
        preferred_element_type=jnp.float32,
    )
    gate_preactivation = jnp.einsum(
        "bpd,dl->bpl",
        gate_mix_weight,
        down_all[:, gate_first_matrix:],
        preferred_element_type=jnp.float32,
    )
    gate_act = jax.nn.sigmoid(gate_preactivation)
    sigmoid_filter_entries = jnp.einsum(
        "bpl,ld->bpd",
        gate_act.astype(jnp.bfloat16),
        up_all[gate_first_matrix:],
        preferred_element_type=jnp.float32,
    )

    def leading_part(recv_in, decay_in, keys_in, values_in, rate_in):
        return time_mixer_forward(
            recv_in, decay_in, keys_in, values_in, rate_in, stacked_parameter_lines, span_length
        )

    (local_out, direction, ending, adjusted_lookup_entries), front_pull = jax.vjp(
        leading_part,
        acceptance_entries,
        decay_branch,
        unscaled_keys,
        raw_payload_entries,
        rate_branch,
    )
    add_end = ending[:, :, :ATTENTION_DIM]
    move_end = ending[:, :, ATTENTION_DIM:]
    zero_state = jnp.zeros_like(add_end)

    def pass_on(_, carried):
        state_prev, state_end = carried
        state_prev = shifted(flatten_state(state_end), "seq", 1).reshape(add_end.shape)
        return (
            state_prev,
            jnp.einsum("bhvk,bhkj->bhvj", state_prev, move_end, precision=PRECISE) + add_end,
        )

    state_in, _ = lax.fori_loop(0, lax.axis_size("seq") - 1, pass_on, (zero_state, add_end))

    def back(local_in, direct_in, state_arg, recv_in, keymod_in, values_in, gate_in):
        return mixer_back(
            local_in,
            direct_in,
            state_arg,
            recv_in,
            keymod_in,
            values_in,
            gate_in,
            stacked_parameter_lines,
        )

    gated_wide, back_pull = jax.vjp(
        back,
        local_out,
        direction,
        state_in,
        acceptance_entries,
        adjusted_lookup_entries,
        raw_payload_entries,
        sigmoid_filter_entries,
    )
    gated_low = gated_wide.astype(jnp.bfloat16)
    attended, hid_out = adapted(
        gated_low, mat_all[3], chosen[:, 3 * RANK : 4 * RANK], chosen[:, 8 * RANK : 9 * RANK]
    )
    middle = tokens_wide + attended
    key_full, value_full, hidden_all = (
        lax.all_gather(channel_key_weight, ("seq", "dp"), axis=1, tiled=True),
        lax.all_gather(channel_value_weight, ("seq", "dp"), axis=0, tiled=True),
        lax.all_gather(hidden_adapter_rows, ("seq", "dp"), axis=2, tiled=True),
    )
    chosen_hidden = jnp.einsum(
        "ba,arx->brx", pick_low, hidden_all, preferred_element_type=jnp.float32
    ).astype(jnp.bfloat16)

    def norm_second(values):
        return layer_norm(values, stacked_parameter_lines[15], stacked_parameter_lines[16])

    normed_two, norm2_pull = jax.vjp(norm_second, middle)
    edge_two = shifted(normed_two[:, -1:, :], "seq", 1)

    def chan_mixes(values, edge_vals):
        return chan_mixing(values, edge_vals, stacked_parameter_lines[17])

    chan_wide, chan_pull = jax.vjp(chan_mixes, normed_two, edge_two)
    chan_mix = chan_wide.astype(jnp.bfloat16)
    pre_act, hid_ckey = adapted(
        chan_mix, key_full, chosen[:, 4 * RANK : 5 * RANK], chosen_hidden[:, RANK : 2 * RANK]
    )
    active = jnp.maximum(pre_act, 0.0)
    squared = (active * active).astype(jnp.bfloat16)
    chan_out, hid_cvalue = adapted(
        squared, value_full, chosen_hidden[:, 0:RANK], chosen[:, 9 * RANK : 10 * RANK]
    )
    result = (middle + chan_out).astype(jnp.bfloat16)
    cotangent = output_gradient.astype(jnp.float32)
    key_back, value_back = (
        lax.all_gather(channel_key_weight, ("seq", "dp"), axis=1, tiled=True),
        lax.all_gather(channel_value_weight, ("seq", "dp"), axis=0, tiled=True),
    )
    grad_square, down_cvalue, up_cvalue = adapted_back(
        cotangent,
        squared,
        value_back,
        chosen_hidden[:, 0:RANK],
        chosen[:, 9 * RANK : 10 * RANK],
        hid_cvalue,
    )
    grad_pre = grad_square * 2.0 * active
    grad_chan, down_ckey, up_ckey = adapted_back(
        grad_pre,
        chan_mix,
        key_back,
        chosen[:, 4 * RANK : 5 * RANK],
        chosen_hidden[:, RANK : 2 * RANK],
        hid_ckey,
    )
    grad_normed2, grad_edge2 = chan_pull(grad_chan)
    from_next2 = shifted(grad_edge2, "seq", -1)
    grad_normed2 = jnp.concatenate(
        [grad_normed2[:, :-1], grad_normed2[:, -1:] + from_next2], axis=1
    )
    (grad_middle,) = norm2_pull(grad_normed2)
    grad_middle = grad_middle + cotangent
    mat_back, down_back, up_back = (
        lax.all_gather(time_projection_weights, ("seq", "dp"), axis=2, tiled=True),
        lax.all_gather(branch_first_weights, ("seq", "dp"), axis=0, tiled=True),
        lax.all_gather(branch_second_weights, ("seq", "dp"), axis=1, tiled=True),
    )
    grad_gated, down_out, up_out = adapted_back(
        grad_middle,
        gated_low,
        mat_back[3],
        chosen[:, 3 * RANK : 4 * RANK],
        chosen[:, 8 * RANK : 9 * RANK],
        hid_out,
    )
    grad_local, grad_direct, grad_state, grad_recv2, grad_keymod, grad_value2, grad_gate = (
        back_pull(grad_gated)
    )
    move_turned = jnp.swapaxes(move_end, 2, 3)

    def pass_back(_, carried):
        grad_after, grad_before = carried
        grad_after = shifted(flatten_state(grad_before), "seq", -1).reshape(add_end.shape)
        return (
            grad_after,
            jnp.einsum("bhvk,bhkj->bhvj", grad_after, move_turned, precision=PRECISE) + grad_state,
        )

    grad_end, _ = lax.fori_loop(0, lax.axis_size("seq") - 1, pass_back, (zero_state, grad_state))
    grad_move = jnp.einsum("bhvk,bhvj->bhkj", state_in, grad_end, precision=PRECISE)
    grad_ending = jnp.concatenate([grad_end, grad_move], axis=2)
    grad_recv1, grad_decay, grad_keys, grad_value1, grad_rate = front_pull(
        (grad_local, grad_direct, grad_ending, grad_keymod)
    )
    grad_recv = grad_recv1 + grad_recv2
    grad_value = grad_value1 + grad_value2
    gate_low = grad_gate.astype(jnp.bfloat16)
    grad_gact = jnp.einsum(
        "bpd,ld->bpl", gate_low, up_back[gate_first_matrix:], preferred_element_type=jnp.float32
    )
    grad_gpre = (grad_gact * gate_act * (1.0 - gate_act)).astype(jnp.bfloat16)
    grad_mixg = jnp.einsum(
        "bpl,dl->bpd",
        grad_gpre,
        down_back[:, gate_first_matrix:],
        preferred_element_type=jnp.float32,
    )
    rate_low = grad_rate.astype(jnp.bfloat16)
    grad_rpre = jnp.einsum(
        "bpd,ld->bpl",
        rate_low,
        up_back[rate_first_matrix:gate_first_matrix],
        preferred_element_type=jnp.float32,
    ).astype(jnp.bfloat16)
    grad_mixa = jnp.einsum(
        "bpl,dl->bpd",
        grad_rpre,
        down_back[:, rate_first_matrix:gate_first_matrix],
        preferred_element_type=jnp.float32,
    )
    decay_low = grad_decay.astype(jnp.bfloat16)
    grad_dact = jnp.einsum(
        "bpd,ld->bpl", decay_low, up_back[:rate_first_matrix], preferred_element_type=jnp.float32
    )
    grad_dpre = (grad_dact * (1.0 - decay_act * decay_act)).astype(jnp.bfloat16)
    grad_mixw = jnp.einsum(
        "bpl,dl->bpd",
        grad_dpre,
        down_back[:, :rate_first_matrix],
        preferred_element_type=jnp.float32,
    )
    grad_mixr, down_recv, up_recv = adapted_back(
        grad_recv, mix_r, mat_back[0], chosen[:, 0:RANK], chosen[:, 5 * RANK : 6 * RANK], hid_recv
    )
    grad_mixk, down_keys, up_keys = adapted_back(
        grad_keys,
        mix_k,
        mat_back[1],
        chosen[:, RANK : 2 * RANK],
        chosen[:, 6 * RANK : 7 * RANK],
        hid_keys,
    )
    grad_mixv, down_values, up_values = adapted_back(
        grad_value,
        mix_v,
        mat_back[2],
        chosen[:, 2 * RANK : 3 * RANK],
        chosen[:, 7 * RANK : 8 * RANK],
        hid_values,
    )
    grad_mixes = jnp.stack([grad_mixr, grad_mixw, grad_mixk, grad_mixv, grad_mixa, grad_mixg])
    grad_normed, grad_edge = mix_pull(grad_mixes)
    from_next = shifted(grad_edge, "seq", -1)
    grad_normed = jnp.concatenate([grad_normed[:, :-1], grad_normed[:, -1:] + from_next], axis=1)
    (grad_first,) = norm_pull(grad_normed)
    grad_tokens = grad_first + grad_middle
    per_model = jnp.concatenate(
        [
            down_recv,
            down_keys,
            down_values,
            down_out,
            down_ckey,
            up_recv,
            up_keys,
            up_values,
            up_out,
            up_cvalue,
        ],
        axis=1,
    )
    per_hidden = jnp.concatenate([down_cvalue, up_ckey], axis=1)
    whole_model = jnp.einsum("ba,brx->arx", pick_full, per_model, precision=PRECISE)
    whole_hidden = jnp.einsum("ba,brx->arx", pick_full, per_hidden, precision=PRECISE)
    grad_model, grad_hidden = (
        lax.psum_scatter(whole_model, ("seq", "dp"), scatter_dimension=2, tiled=True),
        lax.psum_scatter(whole_hidden, ("seq", "dp"), scatter_dimension=2, tiled=True),
    )
    return (result, grad_tokens, grad_model, grad_hidden)


def solution(mesh):
    in_specs = (
        P("dp", "seq", None),
        P("dp", "seq", None),
        P("dp"),
        P(None, None, ("seq", "dp")),
        P(("seq", "dp"), None),
        P(None, ("seq", "dp")),
        P(None, ("seq", "dp")),
        P(None, ("seq", "dp")),
        P(("seq", "dp"), None),
        P(None, None, ("seq", "dp")),
        P(None, None, ("seq", "dp")),
    )
    out_specs = (
        P("dp", "seq", None),
        P("dp", "seq", None),
        P(None, None, ("seq", "dp")),
        P(None, None, ("seq", "dp")),
    )
    return jax.shard_map(body, mesh=mesh, in_specs=in_specs, out_specs=out_specs, check_vma=False)
```

profile of v0, /device:TPU:1, one launch (start us, length us, event | category | flops | bytes accessed | tf_op | source)
XLA Modules:
  0.0 3064.7 jit_solution(6331349900250223349)
XLA Ops:
  11.2 43.7 %all-gather = bf16[32,64,18]{1,2,0:T(8,128)(2,1)S(1)} all-gather(bf16[1,64,18]{1,2,0:T(8,128)(2,1)S(1)} %bitcast.1420), channel_id=1, replica_groups=mesh['seq'=8,'dp'=4] {'seq','dp'}, dimensions={0}, use_global_device_ids=true | all-gather | bytes 76032 | tf_op jit(solution)/shard_map/all_gather | solution.py:235
  64.6 5.3 all-gather.11.cloned.1.call-done
  69.9 58.3 %all-gather.9.cloned.1.call-done = bf16[2048,448]{1,0:T(8,128)(2,1)} async-done(((bf16[64,448]{1,0:T(8,128)(2,1)}), bf16[2048,448]{1,0:T(8,128)(2,1)}) %all-gather.9.cloned.1.call-update) | async-done | bytes 1835024 | tf_op jit(solution)/shard_map/all_gather | solution.py:233
  153.1 43.5 %all-gather.19.cloned.1.call-done = bf16[8,32,8192]{2,1,0:T(8,128)(2,1)} async-done(((bf16[8,32,256]{2,1,0:T(8,128)(2,1)}), bf16[8,32,8192]{2,1,0:T(8,128)(2,1)}) %all-gather.19.cloned.1.call-update) | async-done | bytes 4194320 | tf_op jit(solution)/shard_map/all_gather | solution.py:368
  196.5 7.2 fusion.202
  205.1 71.2 %all-gather.15.cloned.1.call-done = bf16[8,160,2048]{1,2,0:T(8,128)(2,1)} async-done(((bf16[8,160,64]{1,2,0:T(8,128)(2,1)}), bf16[8,160,2048]{1,2,0:T(8,128)(2,1)}) %all-gather.15.cloned.1.call-update) | async-done | bytes 5242896 | tf_op jit(solution)/shard_map/all_gather | solution.py:236
  276.3 12.2 copy.412
  295.8 176.4 %all-gather.13.cloned.1.call-done = bf16[4,2048,2048]{1,2,0:T(8,128)(2,1)} async-done(((bf16[4,2048,64]{1,2,0:T(8,128)(2,1)}), bf16[4,2048,2048]{1,2,0:T(8,128)(2,1)}) %all-gather.13.cloned.1.call-update) | async-done | bytes 33554448 | tf_op jit(solution)/shard_map/all_gather | solution.py:232
  472.2 6.1 fusion.195
  479.7 7.3 fusion.199
  499.2 6.1 fusion.197
  511.5 5.1 reshape.2588
  517.1 5.1 reshape.2580
  522.3 7.6 copy.598
  529.9 11.1 copy_bitcast_fusion.22
  541.0 11.1 fusion.204
  552.2 533.8 %while.126 = (s32[]{:T(128)}, f32[1,32,128,64]{2,3,1,0:T(8,128)S(1)}, f32[16,1,32,16,128]{4,3,0,2,1:T(8,128)}, f32[16,1,32,16,64]{4,2,3,1,0:T(8,128)}, f32[16,1,...) while((s32[]{:T(128)}, ...), condition=%wide.region_5.6_spmd.clone.clone, body=%wide.region_3.5_spmd.clone.clone.sunk | while | flops 288400896 | bytes 27879748 | solution.py:169
  1101.3 136.2 %while.124 = (s32[]{:T(128)}, f32[1,32,64,64]{3,2,1,0:T(8,128)}, f32[1,32,64,64]{3,2,1,0:T(8,128)}, f32[1,32,64,64]{3,2,1,0:T(8,128)}, f32[1,32,64,64]{3,2,1,0:T(8,128)}, /*index=5*/s32[]{:T(128)}) while((s32[]{:T(128)}, f32[1,32,64,64]{3,2,1,0:T(8,128)}, f32[1,32,64,64]{3,2,1,0:T(8,128)}, f32[1,32,64,64]{3,2,1,0:T(8,128)}, ...), condition=%wide.region_7.8_spmd, body=%wide.region_6.7_spmd.sunk | while | flops 100794368 | bytes 7340141 | solution.py:336
  1105.7 11.0 collective-permute-done
  1127.3 10.1 collective-permute-done
  1148.1 9.2 collective-permute-done
  1168.6 8.6 collective-permute-done
  1183.7 5.0 collective-permute-start
  1188.8 7.7 collective-permute-done
  1203.0 5.0 collective-permute-start
  1208.0 6.8 collective-permute-done
  1221.3 5.0 collective-permute-start
  1226.3 6.1 collective-permute-done
  1237.5 8.3 bitcast_reduce_fusion
  1257.5 5.8 fusion.201
  1272.4 17.5 fusion.301
  1303.5 17.8 fusion.380
  1337.0 17.0 fusion.381
  1358.9 5.2 convolution_convert_fusion.7
  1378.6 6.1 fusion.200
  1398.6 5.3 fusion.264
  1412.9 134.4 %while.125 = (s32[]{:T(128)}, f32[1,32,64,64]{3,2,1,0:T(8,128)}, f32[1,32,64,64]{3,2,1,0:T(8,128)}, f32[1,32,64,64]{3,2,1,0:T(8,128)}, f32[1,32,64,64]{3,2,1,0:T(8,128)S(1)}, /*index=5*/s32[]{:T(128)}) while((s32[]{:T(128)}, f32[1,32,64,64]{3,2,1,0:T(8,128)}, f32[1,32,64,64]{3,2,1,0:T(8,128)}, f32[1,32,64,64]{3,2,1,0:T(8,128)}, ...), condition=%wide.region_18.19_spmd, body=%wide.region_17.18_spmd.sunk | while | flops 100794368 | bytes 7340141 | solution.py:449
  1415.6 10.4 collective-permute-done.1
  1433.6 12.3 collective-permute-done.1
  1453.5 13.4 collective-permute-done.1
  1474.4 11.1 collective-permute-done.1
  1493.1 12.7 collective-permute-done.1
  1513.4 12.3 collective-permute-done.1
  1533.3 8.7 collective-permute-done.1
  1557.2 5.7 copy.367
  1577.8 1176.2 %while.127 = (s32[]{:T(128)}, f32[1,32,128,64]{2,3,1,0:T(8,128)S(1)}, f32[16,1,32,16,64]{4,3,2,1,0:T(8,128)}, f32[16,1,32,16,64]{4,3,2,1,0:T(8,128)}, f32[16,1,3...) while((s32[]{:T(128)}, ...), condition=%wide.region_24.25_spmd.clone.clone, body=%wide.region_19.24_spmd.clone.clone.sunk | while | flops 576136192 | bytes 39547384 | solution.py:169
  2769.4 5.5 copy.383
  2790.5 5.5 copy.385
  2796.0 5.1 reshape.2609
  2801.2 5.5 copy.397
  2813.6 5.5 copy.386
  2819.0 5.1 reshape.2610
  2824.2 11.6 fusion.248
  2849.8 7.4 broadcast_multiply_fusion
  2857.2 18.5 fusion.368
  2882.7 5.2 neg.198
  2887.9 5.8 fusion.196
  2896.4 5.8 fusion.194
  2904.9 5.8 fusion.198
  2913.4 6.0 fusion.276
  2919.4 7.1 fusion.279
  2926.6 7.3 fusion.278
  2933.9 5.8 fusion.306
  2949.6 108.4 %reduce-scatter.3.cloned.1.call-done = f32[8,160,64]{1,2,0:T(8,128)} async-done(((f32[8,160,2048]{1,2,0:T(8,128)}), f32[8,160,64]{1,2,0:T(8,128)}) %reduce-scatter.3.cloned.1.call-update) | async-done | bytes 327696 | tf_op jit(solution)/shard_map/reduce_scatter | solution.py:536
  (1898 shorter events, 2085.0 us)
Async XLA Ops:
  7.2 47.9 %copy-start.5 = (bf16[1,256,2048]{2,1,0:T(8,128)(2,1)S(1)}, bf16[1,256,2048]{2,1,0:T(8,128)(2,1)}, u32[]{:S(2)}) copy-start(bf16[1,256,2048]{2,1,0:T(8,128)(2,1)} %param.19) | copy-start | bytes 3145732
  7.2 62.7 %all-gather.11.cloned.1.call-start = ((), (), s32[]{:S(2)}) async-start(), calls=%async_computation.3 | async-start | bytes 2162688 | tf_op jit(solution)/shard_map/all_gather | solution.py:234
  7.9 120.3 %all-gather.9.cloned.1.call-start = ((), (), s32[]{:S(2)}) async-start(), calls=%async_computation.2 | async-start | bytes 2162688 | tf_op jit(solution)/shard_map/all_gather | solution.py:233
  8.7 187.9 %all-gather.19.cloned.1.call-start = ((), (), s32[]{:S(2)}) async-start(), calls=%async_computation.7 | async-start | bytes 4325376 | tf_op jit(solution)/shard_map/all_gather | solution.py:368
  9.4 266.9 %all-gather.15.cloned.1.call-start = ((), (), s32[]{:S(2)}) async-start(), calls=%async_computation.5 | async-start | bytes 8650752 | tf_op jit(solution)/shard_map/all_gather | solution.py:236
  10.0 462.2 %all-gather.13.cloned.1.call-start = ((), (), s32[]{:S(2)}) async-start(), calls=%async_computation.4 | async-start | bytes 34603008 | tf_op jit(solution)/shard_map/all_gather | solution.py:232
  10.6 1261.8 %all-gather.21.cloned.1.call-start = ((), (), s32[]{:S(2)}) async-start(), calls=%async_computation.8 | async-start | bytes 34603008 | tf_op jit(solution)/shard_map/all_gather | solution.py:367
  11.1 1292.3 %all-gather.17.cloned.1.call-start = ((), (), s32[]{:S(2)}) async-start(), calls=%async_computation.6 | async-start | bytes 34603008 | tf_op jit(solution)/shard_map/all_gather | solution.py:366
  55.3 81.8 %copy-start.113 = (f32[256]{0:T(256)}, f32[256]{0:T(256)S(1)}, u32[]{:S(2)}) copy-start(f32[256]{0:T(256)S(1)} %broadcast_multiply_fusion.7) | copy-start | bytes 3076
  56.3 80.8 %copy-start.117 = (f32[256]{0:T(256)}, f32[256]{0:T(256)S(1)}, u32[]{:S(2)}) copy-start(f32[256]{0:T(256)S(1)} %fusion.353) | copy-start | bytes 3076
  57.0 71.3 %copy-start.93 = (f32[1,2048]{1,0:T(1,128)}, f32[1,2048]{1,0:T(1,128)S(1)}, u32[]{:S(2)}) copy-start(f32[1,2048]{1,0:T(1,128)S(1)} %get-tuple-element.2396) | copy-start | bytes 24580
  57.0 80.1 %copy-start.95 = (f32[1,2048]{1,0:T(1,128)}, f32[1,2048]{1,0:T(1,128)S(1)}, u32[]{:S(2)}) copy-start(f32[1,2048]{1,0:T(1,128)S(1)} %get-tuple-element.2400) | copy-start | bytes 24580
  57.0 92.8 %copy-start.76 = (f32[1,2048]{1,0:T(1,128)}, f32[1,2048]{1,0:T(1,128)S(1)}, u32[]{:S(2)}) copy-start(f32[1,2048]{1,0:T(1,128)S(1)} %get-tuple-element.2402) | copy-start | bytes 24580
  57.0 92.8 %copy-start.91 = (f32[1,2048]{1,0:T(1,128)}, f32[1,2048]{1,0:T(1,128)S(1)}, u32[]{:S(2)}) copy-start(f32[1,2048]{1,0:T(1,128)S(1)} %get-tuple-element.2388) | copy-start | bytes 24580
  57.0 430.0 %copy-start.86 = (f32[1,2048]{1,0:T(1,128)}, f32[1,2048]{1,0:T(1,128)S(1)}, u32[]{:S(2)}) copy-start(f32[1,2048]{1,0:T(1,128)S(1)} %get-tuple-element.2395) | copy-start | bytes 24580
  57.0 430.0 %copy-start.88 = (f32[1,2048]{1,0:T(1,128)}, f32[1,2048]{1,0:T(1,128)S(1)}, u32[]{:S(2)}) copy-start(f32[1,2048]{1,0:T(1,128)S(1)} %get-tuple-element.2398) | copy-start | bytes 24580
  57.5 7.1 copy-start.61
  57.5 4.4 collective-permute-start.2
  58.9 2890.8 %reduce-scatter.5.cloned.1.call-start = ((), (), s32[]{:S(2)}) async-start(), calls=%async_computation.10 | async-start | bytes 8650752 | tf_op jit(solution)/shard_map/reduce_scatter | solution.py:537
  61.9 75.2 %copy-start.124 = (f32[1,1,2048]{2,1,0:T(1,128)}, f32[1,1,2048]{2,1,0:T(1,128)S(1)}, u32[]{:S(2)}) copy-start(f32[1,1,2048]{2,1,0:T(1,128)S(1)} %collective-permute-done.2) | copy-start | bytes 24580
  132.2 354.9 %copy-start.7 = (f32[256,2048]{1,0:T(8,128)}, f32[256,2048]{1,0:T(8,128)S(1)}, u32[]{:S(2)}) copy-start(f32[256,2048]{1,0:T(8,128)S(1)} %fusion.222) | copy-start | bytes 6291460
  153.0 1099.1 %copy-start.70 = (f32[256,256]{1,0:T(8,128)}, f32[256,256]{1,0:T(8,128)S(1)}, u32[]{:S(2)}) copy-start(f32[256,256]{1,0:T(8,128)S(1)} %fusion.274) | copy-start | bytes 786436
  293.5 184.9 %copy-start.97 = (bf16[256,16]{0,1:T(8,128)(2,1)}, bf16[256,16]{0,1:T(8,128)(2,1)S(1)}, u32[]{:S(2)}) copy-start(bf16[256,16]{0,1:T(8,128)(2,1)S(1)} %convolution_convert_fusion.6) | copy-start | bytes 24580
  294.2 192.9 %copy-start.101 = (bf16[256,16]{0,1:T(8,128)(2,1)}, bf16[256,16]{0,1:T(8,128)(2,1)S(1)}, u32[]{:S(2)}) copy-start(bf16[256,16]{0,1:T(8,128)(2,1)S(1)} %convolution_convert_fusion.4) | copy-start | bytes 24580
  294.8 210.5 %copy-start.99 = (bf16[256,16]{0,1:T(8,128)(2,1)}, bf16[256,16]{0,1:T(8,128)(2,1)S(1)}, u32[]{:S(2)}) copy-start(bf16[256,16]{0,1:T(8,128)(2,1)S(1)} %convolution_convert_fusion.5) | copy-start | bytes 24580
  479.7 7.4 copy-start.15
  522.3 7.6 copy-start.34
  522.3 7.6 copy-start.35
  529.9 11.1 copy-start.32
  529.9 11.1 copy-start.33
  1102.7 14.0 collective-permute-start
  1123.2 14.2 collective-permute-start
  1144.0 13.3 collective-permute-start
  1163.8 13.4 collective-permute-start
  1183.7 12.7 collective-permute-start
  1203.0 11.8 collective-permute-start
  1221.3 11.1 collective-permute-start
  1264.7 110.6 %copy-start.1 = (f32[1,256,2048]{2,1,0:T(8,128)}, f32[1,256,2048]{2,1,0:T(8,128)S(1)}, u32[]{:S(2)}) copy-start(f32[1,256,2048]{2,1,0:T(8,128)S(1)} %get-tuple-element.2411) | copy-start | bytes 6291460
  1267.3 31.5 %collective-permute-start.3 = (f32[1,1,2048]{2,1,0:T(1,128)S(1)}, f32[1,1,2048]{2,1,0:T(1,128)S(1)}, u32[]{:S(2)}, u32[]{:S(2)}) collective-permute-start(f32[1,1,2048]{2,1,0:T(1,128)S(1)} %slice.283), channel_id=1, source_target_pairs={{0,4},{4,8},{8,12},{12,16},{16,20},{20,24},{24,28},{1,5},{5,9},{9,... | collective-permute-start | bytes 24584 | tf_op jit(solution)/shard_map/ppermute | solution.py:24
  1303.5 17.8 copy-start.66
  1337.0 17.0 copy-start.106
  1369.0 1689.0 %reduce-scatter.3.cloned.1.call-start = ((), (), s32[]{:S(2)}) async-start(), calls=%async_computation.9 | async-start | bytes 17301504 | tf_op jit(solution)/shard_map/reduce_scatter | solution.py:536
  1369.1 5.8 collective-permute-start.4
  1377.3 7.4 copy-start.43
  1414.3 11.7 collective-permute-start.1
  1432.3 13.6 collective-permute-start.1
  1452.2 14.7 collective-permute-start.1
  1473.1 12.4 collective-permute-start.1
  1491.8 14.0 collective-permute-start.1
  1512.1 13.6 collective-permute-start.1
  1532.0 10.0 collective-permute-start.1
  2857.2 18.6 copy-start.2
  2919.4 7.1 copy-start.130
  2926.5 7.3 copy-start.19
  2926.5 7.3 copy-start.80
  2926.5 7.3 copy-start.82
  2926.5 7.3 copy-start.84
  2926.6 7.3 copy-start.92
  2926.6 7.3 copy-start.94
  2926.6 7.3 copy-start.96
  2933.9 7.8 copy-start.28
  2933.9 7.8 copy-start.29
  2933.9 7.8 copy-start.64
  2940.1 5.1 collective-permute-start.5
  (94 other events, 310.7 us)
Sparse Core Ops, SparseCore 0:
  10.9 58.9 all-gather.10
  72.8 55.4 all-gather.8
  131.1 65.3 all-gather.18
  199.3 76.9 all-gather.14
  279.1 193.0 all-gather.12
  474.9 193.0 all-gather.20
  669.6 192.4 all-gather.16
  1369.1 157.0 reduce-scatter.4
  2857.3 200.6 reduce-scatter.2
where the time goes:
time: 3100 us; the launch traced here: 3060 us
  matrix products  1550 us (50%)
  waiting for transfers between devices  610 us (20%)
  local copies, waits for them, and re-layouts  521 us (17%)
  other arithmetic  257 us (8%)
  starting transfers between devices  49.6 us (2%)
  blocking collectives  43.7 us (1%)
    dynamic_slice x208, local copies, waits for them, and re-layouts, time_mixer_forward(): ending, outputs = lax.scan(one_span, initial, pieces_all)  202 us
    dot_general x144, matrix products, one_span(): solver = solver + precise_sum('bhts,bhsu->bhtu', solver, powered)  199 us
    dot_general x144, matrix products, one_span(): powered = precise_sum('bhts,bhsu->bhtu', powered, powered)  187 us
    all_gather x1, waiting for transfers between devices, body(): lax.all_gather(time_projection_weights, ('seq', 'dp'), axis=2, tiled=True)  176 us
    ppermute x18, waiting for transfers between devices, shifted(): return lax.ppermute(block, axis, route)  143 us
    dot_general x48, matrix products, one_span(): outputs = precise_sum('bhtc,bhvc->bhtv', recv_q, memory)  117 us
    reduce_scatter x1, waiting for transfers between devices, body(): lax.psum_scatter(whole_model, ('seq', 'dp'), scatter_dimension=2, tiled=T...  108 us
    dot_general x48, matrix products, one_span(): precise_sum('bhsv,bhsc->bhvc', pulled, push_c)  96.4 us
  transfers between devices with their start and end apart: 27, of which 22 were waited for; matrix products, arithmetic and copies ran while one was open for 73% of the time, Pallas kernels for 0%

commit v1 on v0

v1 whole, which is shorter than its diff:
```python
import functools
import math

import jax
import jax.numpy as jnp
from jax import lax
from jax.experimental import pallas as pl
from jax.experimental.pallas import tpu as pltpu
from jax.sharding import PartitionSpec as P

F32, BF = jnp.float32, jnp.bfloat16
MESH = pl.DeviceIdType.MESH
D = 64
C = 64
PW = 2 * D
DECAY_INNER, RATE_INNER, RANK = 96, 96, 16
SCALE = 4.0
NORM_EPS, GROUP_EPS, UNIT_EPS = 1e-05, 0.00064, 1e-06
DECAY_SCALE = math.exp(-0.5)
PRECISE = lax.Precision.HIGHEST
DIMS = {
    "nn": (((1,), (0,)), ((), ())),
    "nt": (((1,), (1,)), ((), ())),
    "tn": (((0,), (0,)), ((), ())),
}


def split(x):
    hi = x.astype(BF)
    return hi, (x - hi.astype(F32)).astype(BF)


def dot1(a, b, m="nn"):
    return lax.dot_general(a.astype(BF), b.astype(BF), DIMS[m], preferred_element_type=F32)


def dot3(a, b, m="nn"):
    ah, al = split(a)
    bh, bl = split(b)
    ka, kb = (0 if m == "tn" else 1), (1 if m == "nt" else 0)
    n = b.shape[1 - kb]
    aa = jnp.concatenate([ah, al], axis=ka)
    bb = jnp.concatenate([jnp.concatenate([bh, bl], axis=1 - kb)] * 2, axis=kb)
    r = lax.dot_general(aa, bb, DIMS[m], preferred_element_type=F32)
    return r[:, :n] + r[:, n:]


def iota(shape, axis):
    return lax.broadcasted_iota(jnp.int32, shape, axis)


def stack2(x):
    lane = iota(x.shape, 1)
    zero = jnp.zeros_like(x)
    return jnp.concatenate([jnp.where(lane < D, x, zero), jnp.where(lane < D, zero, x)], axis=0)


def pack2(x):
    h = x.shape[0] // 2
    return x[:h] + x[h:]


def head_ones():
    r, c = iota((2 * PW, PW), 0) % PW, iota((2 * PW, PW), 1)
    return jnp.where((r // D) == (c // D), 1.0, 0.0).astype(BF)


def headsum(x, ones):
    h, l = split(x)
    return lax.dot_general(
        jnp.concatenate([h, l], axis=1), ones, DIMS["nn"], preferred_element_type=F32
    )


def triangle(upper):
    r, c = iota((C, C), 0), iota((C, C), 1)
    return jnp.where((r <= c) if upper else (r >= c), 1.0, 0.0).astype(BF)


def cums(x, tri):
    h, l = split(x)
    m = (x - h.astype(F32) - l.astype(F32)).astype(BF)
    n = x.shape[1]
    r = lax.dot_general(
        tri, jnp.concatenate([h, l, m], axis=1), DIMS["nn"], preferred_element_type=F32
    )
    return r[:, :n] + r[:, n : 2 * n] + r[:, 2 * n :]


def prelude(kr, wl, al, w0, a0, k_k, k_a, ones):
    s = jax.nn.sigmoid(w0 + wl)
    a = jax.nn.sigmoid(a0 + al)
    kx = kr * k_k
    rn = lax.rsqrt(headsum(kx * kx, ones) + UNIT_EPS)
    return s, -DECAY_SCALE * s, a, rn, kx * rn, kr * (1.0 + (a - 1.0) * k_a)


def grid_ids():
    r, c = iota((PW, PW), 0), iota((PW, PW), 1)
    return r, c, (r // D) == (c // D)


def inverse(a):
    r, c, _ = grid_ids()
    x = jnp.where(r == c, 1.0, 0.0)
    b = 1
    while b < C:
        level = ((r // (2 * b)) == (c // (2 * b))) & ((r // b) % 2 == 1) & ((c // b) % 2 == 0)
        am = jnp.where(level, a, 0.0)
        x = x + am if b == 1 else x + dot3(dot3(x, am), x)
        b *= 2
    return x


def factors(logw, tri):
    run = cums(logw, tri)
    return jnp.exp(run - logw), jnp.exp(run), jnp.exp(-run), jnp.exp(run[C - 1 : C])


def forward_chunk(r, p, q, k, v, logw, tri):
    eb, el, en, last = factors(logw, tri)
    p2, r2, q2, k2, v2 = (
        stack2(p * eb), stack2(r * el), stack2(q * en), stack2(k * en), stack2(v)
    )
    rows, cols, same = grid_ids()
    zero = jnp.zeros((PW, PW), F32)
    strict, incl = (rows > cols) & same, (rows >= cols) & same
    aa = dot3(jnp.concatenate([p2, r2], 0), jnp.concatenate([q2, k2], 0), "nt")
    apq, apk = jnp.where(strict, aa[:PW, :PW], zero), jnp.where(strict, aa[:PW, PW:], zero)
    arq, ark = jnp.where(incl, aa[PW:, :PW], zero), jnp.where(incl, aa[PW:, PW:], zero)
    x = inverse(apq)
    ww = dot3(x, jnp.concatenate([p2, dot3(apk, v2)], 1))
    left = jnp.concatenate(
        [
            jnp.concatenate([arq, ark], 1),
            jnp.concatenate([(q2 * last).T, (k2 * last).T], 1),
        ],
        0,
    )
    right = jnp.concatenate([ww, jnp.concatenate([zero, v2], 1)], 0)
    big = dot3(left, right)
    move = big[PW:, :PW] + jnp.where(rows == cols, jnp.broadcast_to(last, (PW, PW)), zero)
    return (
        pack2(r2 + big[:PW, :PW]),
        pack2(big[:PW, PW:]),
        move,
        big[PW:, PW:],
        pack2(ww[:, :PW]),
        pack2(ww[:, PW:]),
        x,
    )


def backward_chunk(r, p, q, k, v, logw, tri, tri_up, x, u, z0, h, g):
    eb, el, en, last = factors(logw, tri)
    pe, re, qe, ke = p * eb, r * el, q * en, k * en
    qh, kh = qe * last, ke * last
    g2 = stack2(g)
    rows, cols, same = grid_ids()
    zero = jnp.zeros((PW, PW), F32)
    strict, incl = (rows < cols) & same, (rows <= cols) & same
    qk = jnp.concatenate([stack2(qe), stack2(ke)], 0)
    pr = jnp.concatenate([stack2(pe), stack2(re)], 0)
    at = dot3(qk, pr, "nt")
    arq, apk, ark = (
        jnp.where(incl, at[:PW, PW:], zero),
        jnp.where(strict, at[PW:, :PW], zero),
        jnp.where(incl, at[PW:, PW:], zero),
    )
    qkh = dot3(jnp.concatenate([qh, kh], 0), h)
    du = dot3(arq, g2) + stack2(qkh[:C])
    dm = dot3(x, du, "tn")
    dg = jnp.concatenate([dm, g2], 0)
    dv = pack2(dot3(jnp.concatenate([apk, ark], 1), dg)) + qkh[C:]
    dat = dot3(jnp.concatenate([stack2(u), stack2(v)], 0), dg, "nt")
    both = jnp.concatenate([jnp.concatenate([strict, incl], 1)] * 2, 0)
    dat = jnp.where(both, dat, jnp.zeros_like(dat))
    dpr = dot3(dat, qk, "tn")
    sp = dot3(jnp.concatenate([pack2(dm), g], 0), z0, "nt")
    dp, dr = pack2(dpr[:PW]) + sp[:C], pack2(dpr[PW:]) + sp[C:]
    dqk = dot3(dat, pr)
    sq = dot3(jnp.concatenate([u, v], 0), h, "nt")
    dqh, dkh = sq[:C], sq[C:]
    dq, dk = pack2(dqk[:PW]) + dqh * last, pack2(dqk[PW:]) + dkh * last
    tail = jnp.sum(qh * dqh + kh * dkh, axis=0, keepdims=True)
    tail = tail + last * jnp.sum((z0 * h).T, axis=0, keepdims=True)
    gb = pe * dp
    gl = re * dr - qe * dq - ke * dk
    dlogw = cums(gl + gb, tri_up) - gb + tail
    return dr * el, dp * eb, dq * en, dk * en, dv, dlogw


def rec_local(nc, rr, kr, vr, wl, al, vec, reff, oloc, w1, w2, xs, mv, mt, piece):
    ones, tri = head_ones(), triangle(False)
    row = lambda i: vec[i : i + 1, :]
    _, logw, a, _, kk, km = prelude(
        kr[...], wl[...], al[...], row(8), row(9), row(10), row(11), ones
    )
    r, v = rr[...], vr[...]
    q = kk * a
    moves, adds = [], []
    for c in range(nc):
        s = slice(c * C, (c + 1) * C)
        e, o, m, n, y1, y2, x = forward_chunk(r[s], -kk[s], q[s], km[s], v[s], logw[s], tri)
        reff[s, :], oloc[s, :], w1[s, :], w2[s, :] = e, o, y1, y2
        xs[s, :] = pack2(x)
        mp = pack2(m)
        mv[0, s, :], mv[1, s, :], mt[s, :] = mp, pack2(n), pack2(m.T)
        moves.append(mp)
        adds.append(n)
    total = None
    for c in range(nc):
        if c == 0:
            tm, tn = stack2(moves[0]), adds[0]
        else:
            t = dot3(moves[c], jnp.concatenate([tm, tn], 1))
            tm, tn = stack2(t[:, :PW]), stack2(t[:, PW:]) + adds[c]
    piece[0], piece[1], piece[2] = pack2(tm), pack2(tn), pack2(tm.T)


def norm_parts(o, ones):
    centre = o - headsum(o, ones) * (1.0 / D)
    rstd = lax.rsqrt(headsum(centre * centre, ones) * (1.0 / D) + GROUP_EPS)
    return centre * rstd, rstd


def rec_out(nc, zin, rr, kr, vr, al, gg, vec, reff, oloc, w1, w2, mv, z_out, o_out, u_out, zs):
    ones = head_ones()
    row = lambda i: vec[i : i + 1, :]
    state = zin[...]
    for c in range(nc):
        s = slice(c * C, (c + 1) * C)
        zs[s, :] = state
        big = stack2(state)
        t = dot3(jnp.concatenate([reff[s, :], w1[s, :], mv[0, s, :]], 0), big)
        o_out[s, :] = t[:C] + oloc[s, :]
        u_out[s, :] = t[C : 2 * C] + w2[s, :]
        state = t[2 * C :] + mv[1, s, :]
    a = jax.nn.sigmoid(row(9) + al[...])
    km = kr[...] * (1.0 + (a - 1.0) * row(11))
    hat, _ = norm_parts(o_out[...], ones)
    y = hat * row(13) + row(14) + headsum(rr[...] * km * row(12), ones) * vr[...]
    z_out[...] = (y * gg[...]).astype(BF)


def back_local(nc, dz, gg, o, rr, kr, vr, al, vec, reff, mt, do, dgg, es, piece):
    ones = head_ones()
    row = lambda i: vec[i : i + 1, :]
    a = jax.nn.sigmoid(row(9) + al[...])
    km = kr[...] * (1.0 + (a - 1.0) * row(11))
    hat, rstd = norm_parts(o[...], ones)
    y = hat * row(13) + row(14) + headsum(rr[...] * km * row(12), ones) * vr[...]
    dgg[...] = (dz[...] * y).astype(BF)
    dhat = dz[...] * gg[...] * row(13)
    d_o = rstd * (
        dhat
        - headsum(dhat, ones) * (1.0 / D)
        - hat * (headsum(dhat * hat, ones) * (1.0 / D))
    )
    do[...] = d_o
    _, _, same = grid_ids()
    state = None
    for c in reversed(range(nc)):
        s = slice(c * C, (c + 1) * C)
        e = pack2(jnp.where(same, dot3(reff[s, :], d_o[s], "tn"), 0.0))
        es[s, :] = e
        state = e if state is None else e + dot3(mt[s, :], stack2(state))
    piece[...] = state


def rec_back(
    nc, hin, dz, gg, do, rr, kr, vr, wl, al, vec, xs, us, zs, mt, es, drr, dkr, dvr, dwl, dal
):
    ones, tri, tri_up = head_ones(), triangle(False), triangle(True)
    row = lambda i: vec[i : i + 1, :]
    h = hin[...]
    for c in reversed(range(nc)):
        s = slice(c * C, (c + 1) * C)
        r, v, k = rr[s, :], vr[s, :], kr[s, :]
        sg, logw, a, rn, kk, km = prelude(
            k, wl[s, :], al[s, :], row(8), row(9), row(10), row(11), ones
        )
        big = stack2(h)
        dr, dp, dq, dk, dv, dlogw = backward_chunk(
            r, -kk, kk * a, km, v, logw, tri, tri_up,
            stack2(xs[s, :]), us[s, :], stack2(zs[s, :]), big, do[s, :],
        )
        if c:
            h = dot3(mt[s, :], big) + es[s, :]
        dy = dz[s, :] * gg[s, :]
        dv = dv + headsum(r * km * row(12), ones) * dy
        ds = headsum(dy * v, ones) * row(12)
        dr = dr + ds * km
        dkm = dk + ds * r
        dkk = dq * a - dp
        da = dq * kk + dkm * k * row(11)
        dk = dkm * (1.0 + (a - 1.0) * row(11)) + row(10) * rn * (dkk - kk * headsum(dkk * kk, ones))
        drr[s, :], dkr[s, :], dvr[s, :] = dr.astype(BF), dk.astype(BF), dv.astype(BF)
        dwl[s, :] = (dlogw * (-DECAY_SCALE) * sg * (1.0 - sg)).astype(BF)
        dal[s, :] = (da * a * (1.0 - a)).astype(BF)


def over_pairs(body, pairs, ins, outs, name):
    def spec(shape):
        lead = tuple(shape[:-1])
        return pl.BlockSpec(lead + (PW,), lambda i, n=len(lead): (0,) * n + (i,))

    return pl.pallas_call(
        body,
        grid=(pairs,),
        in_specs=[spec(x.shape) for x in ins],
        out_specs=[spec(x.shape) for x in outs],
        out_shape=outs,
        compiler_params=pltpu.CompilerParams(vmem_limit_bytes=48 * 1024 * 1024),
        name=name,
    )(*ins)


def pass_kernel(n, groups, back, move, add, out, here, send, send_sem, recv_sem):
    s, d = lax.axis_index("seq"), lax.axis_index("dp")
    if back:
        first, final, nxt, prv = s == n - 1, s == 0, s - 1, s + 1
    else:
        first, final, nxt, prv = s == 0, s == n - 1, s + 1, s - 1
    barrier = pltpu.get_barrier_semaphore()

    @pl.when(jnp.logical_not(first))
    def _():
        pl.semaphore_signal(barrier, inc=1, device_id=(prv, d), device_id_type=MESH)

    @pl.when(jnp.logical_not(final))
    def _():
        pl.semaphore_wait(barrier, 1)

    def copy(g, to):
        return pltpu.make_async_remote_copy(
            src_ref=send.at[g],
            dst_ref=here.at[g],
            send_sem=send_sem.at[g],
            recv_sem=recv_sem.at[g],
            device_id=(to, d),
            device_id_type=MESH,
        )

    per = out.shape[1] // (groups * PW)
    for g in range(groups):

        @pl.when(first)
        def _():
            here[g] = jnp.zeros(here.shape[1:], F32)

        @pl.when(jnp.logical_not(first))
        def _():
            copy(g, prv).wait_recv()

        out[:, g * per * PW : (g + 1) * per * PW] = here[g]

        @pl.when(jnp.logical_not(final))
        def _():
            for i in range(per):
                at = (g * per + i) * PW
                state = stack2(here[g, :, i * PW : (i + 1) * PW])
                send[g, :, i * PW : (i + 1) * PW] = (
                    dot3(move[:, at : at + PW], state) + add[:, at : at + PW]
                )
            copy(g, nxt).start()

    @pl.when(jnp.logical_not(final))
    def _():
        for g in range(groups):
            copy(g, nxt).wait_send()


def pass_states(n, move, add, back):
    rows, width = move.shape
    groups = 4 if width % (4 * PW) == 0 else 1
    return pl.pallas_call(
        functools.partial(pass_kernel, n, groups, back),
        out_shape=jax.ShapeDtypeStruct((rows, width), F32),
        in_specs=[pl.BlockSpec(memory_space=pltpu.VMEM)] * 2,
        out_specs=pl.BlockSpec(memory_space=pltpu.VMEM),
        scratch_shapes=[
            pltpu.VMEM((groups, rows, width // groups), F32),
            pltpu.VMEM((groups, rows, width // groups), F32),
            pltpu.SemaphoreType.DMA((groups,)),
            pltpu.SemaphoreType.DMA((groups,)),
        ],
        compiler_params=pltpu.CompilerParams(
            collective_id=1 if back else 0, has_side_effects=True
        ),
        name="pass_back" if back else "pass_on",
    )(move, add)


def shifted(block, axis, distance):
    devices = range(lax.axis_size(axis))
    route = [(i - distance, i) for i in devices if i - distance in devices]
    return lax.ppermute(block, axis, route)


def layer_norm(values, gain, shift):
    centre = values - jnp.mean(values, axis=-1, keepdims=True)
    spread = jnp.mean(centre * centre, axis=-1, keepdims=True)
    return centre * lax.rsqrt(spread + NORM_EPS) * gain + shift


def mm(a, b):
    return lax.dot_general(a, b, DIMS["nn"], preferred_element_type=F32)


def mm_nt(a, b):
    return lax.dot_general(a, b, DIMS["nt"], preferred_element_type=F32)


def mm_tn(a, b):
    return lax.dot_general(a, b, DIMS["tn"], preferred_element_type=F32)


def adapted(x, weight, down, up):
    hidden = mm_nt(x, down).astype(BF)
    return mm(x, weight) + SCALE * mm(hidden, up), hidden


def adapted_back(gradient, x, weight, down, up, hidden):
    low = gradient.astype(BF)
    grad_up = SCALE * mm_tn(hidden, low)
    grad_hidden = (SCALE * mm_nt(low, up)).astype(BF)
    return mm_nt(low, weight) + mm(grad_hidden, down), mm_tn(grad_hidden, x), grad_up


def previous(values, edge):
    return jnp.concatenate([edge, values[:-1]], axis=0)


def following(values, edge):
    return jnp.concatenate([values[1:], edge], axis=0)


def body(tokens, output_gradient, index, proj, first, second, vectors, ckey, cvalue, model_rows, hidden_rows):
    axes = ("seq", "dp")
    n_seq = lax.axis_size("seq")
    tokens, output_gradient = tokens[0], output_gradient[0]
    length, width = tokens.shape
    pairs, nc = width // PW, length // C
    lo, hi = DECAY_INNER, DECAY_INNER + RATE_INNER
    vec = lax.all_gather(vectors, axes, axis=1, tiled=True).astype(F32)
    second_all = lax.all_gather(second, axes, axis=1, tiled=True)
    first_all = lax.all_gather(first, axes, axis=0, tiled=True)
    model_all = lax.all_gather(model_rows, axes, axis=2, tiled=True)
    mats = lax.all_gather(proj, axes, axis=2, tiled=True)
    hidden_all = lax.all_gather(hidden_rows, axes, axis=2, tiled=True)
    key_all = lax.all_gather(ckey, axes, axis=1, tiled=True)
    value_all = lax.all_gather(cvalue, axes, axis=0, tiled=True)
    pick = index[0] == jnp.arange(model_all.shape[0], dtype=jnp.int32)
    chosen = jnp.einsum("a,arx->rx", pick.astype(BF), model_all, preferred_element_type=F32).astype(BF)
    chosen_hidden = jnp.einsum("a,arx->rx", pick.astype(BF), hidden_all, preferred_element_type=F32).astype(BF)
    down = lambda i: chosen[i * RANK : (i + 1) * RANK]
    up = lambda i: chosen[(5 + i) * RANK : (6 + i) * RANK]

    wide = tokens.astype(F32)
    normed, norm_pull = jax.vjp(lambda t: layer_norm(t, vec[0:1], vec[1:2]), wide)
    change = previous(normed, shifted(normed[-1:], "seq", 1)) - normed
    mix = [(normed + change * vec[2 + i : 3 + i]).astype(BF) for i in range(6)]
    m_r, m_w, m_k, m_v, m_a, m_g = mix
    rr, h_r = adapted(m_r, mats[0], down(0), up(0))
    kr, h_k = adapted(m_k, mats[1], down(1), up(1))
    vr, h_v = adapted(m_v, mats[2], down(2), up(2))
    act_w = jnp.tanh(mm(m_w, first_all[:, :lo]))
    wl = mm(act_w.astype(BF), second_all[:lo])
    pre_a = mm(m_a, first_all[:, lo:hi]).astype(BF)
    al = mm(pre_a, second_all[lo:hi])
    act_g = jax.nn.sigmoid(mm(m_g, first_all[:, hi:]))
    gg = mm(act_g.astype(BF), second_all[hi:])

    full = jax.ShapeDtypeStruct((length, width), F32)
    low = jax.ShapeDtypeStruct((length, width), BF)
    small = jax.ShapeDtypeStruct((D, width), F32)
    reff, oloc, w1, w2, xs, mv, mt, piece = over_pairs(
        functools.partial(rec_local, nc), pairs, (rr, kr, vr, wl, al, vec),
        [full] * 5 + [jax.ShapeDtypeStruct((2, length, width), F32), full, jax.ShapeDtypeStruct((3, D, width), F32)],
        "rec_local",
    )
    zin = pass_states(n_seq, piece[0], piece[1], False)
    gated, o, us, zs = over_pairs(
        functools.partial(rec_out, nc), pairs,
        (zin, rr, kr, vr, al, gg, vec, reff, oloc, w1, w2, mv),
        [low, full, full, full], "rec_out",
    )
    attended, h_o = adapted(gated, mats[3], down(3), up(3))
    middle = wide + attended
    normed2, norm2_pull = jax.vjp(lambda t: layer_norm(t, vec[15:16], vec[16:17]), middle)
    mu = vec[17:18]
    m_c = (normed2 + (previous(normed2, shifted(normed2[-1:], "seq", 1)) - normed2) * mu).astype(BF)
    pre, h_c = adapted(m_c, key_all, down(4), chosen_hidden[RANK:])
    active = jnp.maximum(pre, 0.0)
    squared = (active * active).astype(BF)
    chan, h_f = adapted(squared, value_all, chosen_hidden[:RANK], up(4))
    result = (middle + chan).astype(BF)

    cot = output_gradient.astype(F32)
    d_sq, down_f, up_f = adapted_back(cot, squared, value_all, chosen_hidden[:RANK], up(4), h_f)
    d_mc, down_c, up_c = adapted_back(d_sq * 2.0 * active, m_c, key_all, down(4), chosen_hidden[RANK:], h_c)
    moved = d_mc * mu
    d_n2 = d_mc - moved + following(moved, shifted(moved[:1], "seq", -1))
    d_mid = norm2_pull(d_n2)[0] + cot
    d_gated, down_o, up_o = adapted_back(d_mid, gated, mats[3], down(3), up(3), h_o)
    do, dgg, es, eloc = over_pairs(
        functools.partial(back_local, nc), pairs,
        (d_gated, gg, o, rr, kr, vr, al, vec, reff, mt), [full, low, full, small], "back_local",
    )
    hin = pass_states(n_seq, piece[2], eloc, True)
    drr, dkr, dvr, dwl, dal = over_pairs(
        functools.partial(rec_back, nc), pairs,
        (hin, d_gated, gg, do, rr, kr, vr, wl, al, vec, xs, us, zs, mt, es), [low] * 5, "rec_back",
    )
    d_tg = (mm_nt(dgg, second_all[hi:]) * act_g * (1.0 - act_g)).astype(BF)
    d_ta = mm_nt(dal, second_all[lo:hi]).astype(BF)
    d_tw = (mm_nt(dwl, second_all[:lo]) * (1.0 - act_w * act_w)).astype(BF)
    d_mr, down_r, up_r = adapted_back(drr, m_r, mats[0], down(0), up(0), h_r)
    d_mk, down_k, up_k = adapted_back(dkr, m_k, mats[1], down(1), up(1), h_k)
    d_mv, down_v, up_v = adapted_back(dvr, m_v, mats[2], down(2), up(2), h_v)
    grads = [
        d_mr, mm_nt(d_tw, first_all[:, :lo]), d_mk, d_mv,
        mm_nt(d_ta, first_all[:, lo:hi]), mm_nt(d_tg, first_all[:, hi:]),
    ]
    stay = sum(g * (1.0 - vec[2 + i : 3 + i]) for i, g in enumerate(grads))
    go = sum(g * vec[2 + i : 3 + i] for i, g in enumerate(grads))
    d_n1 = stay + following(go, shifted(go[:1], "seq", -1))
    grad_tokens = norm_pull(d_n1)[0] + d_mid
    per_model = jnp.concatenate([down_r, down_k, down_v, down_o, down_c, up_r, up_k, up_v, up_o, up_f], axis=0)
    per_hidden = jnp.concatenate([down_f, up_c], axis=0)
    pick_f = pick.astype(F32)[:, None, None]
    grad_model = lax.psum_scatter(pick_f * per_model, axes, scatter_dimension=2, tiled=True)
    grad_hidden = lax.psum_scatter(pick_f * per_hidden, axes, scatter_dimension=2, tiled=True)
    return result[None], grad_tokens[None], grad_model, grad_hidden


def solution(mesh):
    cols = P(None, ("seq", "dp"))
    rows = P(("seq", "dp"), None)
    deep = P(None, None, ("seq", "dp"))
    act = P("dp", "seq", None)
    return jax.shard_map(
        body,
        mesh=mesh,
        in_specs=(act, act, P("dp"), deep, rows, cols, cols, cols, rows, deep, deep),
        out_specs=(act, act, deep, deep),
        check_vma=False,
    )
```

time: 3100 us -> 1370 us (0.44)
  matrix products: 1550 us -> 229 us
  local copies, waits for them, and re-layouts: 521 us -> 43.5 us
  Pallas kernels: 0 us -> 353 us
  other arithmetic: 257 us -> 29.6 us
    dot_general x940 -> x58, matrix products: 1550 us -> 229 us  [the longest x23 112 us: mm(): return lax.dot_general(a, b, DIMS['nn'], preferred_element_type=F32)]
    pallas_call x0 -> x6, Pallas kernels: none -> 353 us  [the longest x4 282 us: over_pairs(): pl.pallas_call(body, grid=(pairs,), in_specs=[spec(x.shape) for x in ins]...]
    dynamic_slice x208 -> x0, local copies, waits for them, and re-layouts: 202 us -> none  [time_mixer_forward(): ending, outputs = lax.scan(one_span, initial, pieces_all)]
    all_gather x7, waiting for transfers between devices: 355 us -> 509 us  [the longest x1 177 us: body(): mats = lax.all_gather(proj, axes, axis=2, tiled=True)]
    ppermute x18 -> x4, waiting for transfers between devices: 143 us -> 1.04 us  [shifted(): return lax.ppermute(block, axis, route)]
    reshape x41 -> x0, local copies, waits for them, and re-layouts: 98 us -> none  [the longest x7 35.6 us: blocks(): values.reshape(sequences_present, span_count, span_length, head_count, AT...]
    dynamic_update_slice x32 -> x0, other arithmetic: 77.1 us -> none  [time_mixer_forward(): ending, outputs = lax.scan(one_span, initial, pieces_all)]
    another operation x78 -> x0, other arithmetic: 55.1 us -> none  [the longest x48 48.9 us: one_span(): cum_log = jnp.cumsum(logd_b, axis=2)]
  transfers between devices with their start and end apart: 27 -> 13, of which waited for: 22 -> 8; matrix products, arithmetic and copies ran while one was open for 73% -> 18% of each run, Pallas kernels for 0% -> 26%
where the time goes in v1:
time: 1370 us; the launch traced here: 1360 us
  waiting for transfers between devices  618 us (45%)
  Pallas kernels  353 us (26%)
  matrix products  229 us (17%)
  blocking collectives  43.7 us (3%)
  local copies, waits for them, and re-layouts  43.5 us (3%)
  other arithmetic  29.6 us (2%)
  starting transfers between devices  23.2 us (2%)
  between operations  16 us (1%)
    pallas_call x4, Pallas kernels, over_pairs(): pl.pallas_call(body, grid=(pairs,), in_specs=[spec(x.shape) for x in ins]...  282 us
    all_gather x1, waiting for transfers between devices, body(): mats = lax.all_gather(proj, axes, axis=2, tiled=True)  177 us
    all_gather x1, waiting for transfers between devices, body(): key_all = lax.all_gather(ckey, axes, axis=1, tiled=True)  146 us
    dot_general x23, matrix products, mm(): return lax.dot_general(a, b, DIMS['nn'], preferred_element_type=F32)  112 us
    reduce_scatter x1, waiting for transfers between devices, body(): lax.psum_scatter(pick_f * per_model, axes, scatter_dimension=2, tiled=True)  103 us
    dot_general x21, matrix products, mm_nt(): return lax.dot_general(a, b, DIMS['nt'], preferred_element_type=F32)  94.7 us
    pallas_call x2, Pallas kernels, pass_states(): pl.pallas_call(functools.partial(pass_kernel, n, groups, back), out_shape...  71.7 us
    all_gather x1, waiting for transfers between devices, body(): model_all = lax.all_gather(model_rows, axes, axis=2, tiled=True)  70.9 us
  transfers between devices with their start and end apart: 13, of which 8 were waited for; matrix products, arithmetic and copies ran while one was open for 18% of the time, Pallas kernels for 26%

profile of v1, /device:TPU:1, one launch (start us, length us, event | category | flops | bytes accessed | tf_op | source)
XLA Modules:
  0.0 1355.7 jit_solution(6413339547950991279)
XLA Ops:
  11.9 43.7 %all-gather = bf16[32,64,18]{1,2,0:T(8,128)(2,1)S(1)} all-gather(bf16[1,64,18]{1,2,0:T(8,128)(2,1)S(1)} %bitcast.271), channel_id=1, replica_groups=mesh['seq'=8,'dp'=4] {'seq','dp'}, dimensions={0}, use_global_device_ids=true | all-gather | bytes 76032 | tf_op jit(solution)/shard_map/all_gather | solution.py:446
  60.2 1.6 fusion.171
  63.1 2.3 add_convert_fusion.3
  65.4 4.5 all-gather.13.cloned.1.call-done
  69.9 2.7 convolution_tanh_fusion
  72.6 55.6 %all-gather.15.cloned.1.call-done = bf16[448,2048]{0,1:T(8,128)(2,1)} async-done(((bf16[448,64]{0,1:T(8,128)(2,1)}), bf16[448,2048]{0,1:T(8,128)(2,1)}) %all-gather.15.cloned.1.call-update) | async-done | bytes 1835024 | tf_op jit(solution)/shard_map/all_gather | solution.py:447
  128.2 3.0 fusion.111.wl
  131.2 2.8 fusion.57
  134.1 1.9 fusion.99.gg
  136.0 5.2 fusion.60.al
  141.2 55.3 %all-gather.19.cloned.1.call-done = bf16[8,32,8192]{2,1,0:T(8,128)(2,1)} async-done(((bf16[8,32,256]{2,1,0:T(8,128)(2,1)}), bf16[8,32,8192]{2,1,0:T(8,128)(2,1)}) %all-gather.19.cloned.1.call-update) | async-done | bytes 4194320 | tf_op jit(solution)/shard_map/all_gather | solution.py:451
  196.5 7.2 fusion.13
  203.7 1.7 copy.31
  205.4 70.9 %all-gather.11.cloned.1.call-done = bf16[8,160,2048]{1,2,0:T(8,128)(2,1)} async-done(((bf16[8,160,64]{1,2,0:T(8,128)(2,1)}), bf16[8,160,2048]{1,2,0:T(8,128)(2,1)}) %all-gather.11.cloned.1.call-update) | async-done | bytes 5242896 | tf_op jit(solution)/shard_map/all_gather | solution.py:449
  276.3 12.1 copy.21
  288.4 4.1 fusion.150
  294.8 177.5 %all-gather.9.cloned.1.call-done = bf16[4,2048,2048]{1,2,0:T(8,128)(2,1)} async-done(((bf16[4,2048,64]{1,2,0:T(8,128)(2,1)}), bf16[4,2048,2048]{1,2,0:T(8,128)(2,1)}) %all-gather.9.cloned.1.call-update) | async-done | bytes 33554448 | tf_op jit(solution)/shard_map/all_gather | solution.py:450
  472.2 6.7 fusion.6
  478.9 2.8 fusion.21.rr
  481.7 6.6 fusion.8
  488.3 2.6 fusion.20.kr
  490.9 6.2 fusion.10
  497.1 2.6 fusion.19.vr
  499.7 132.5 %rec_local.1 = (f32[256,2048]{1,0:T(8,128)S(1)}, f32[256,2048]{1,0:T(8,128)S(1)}, f32[256,2048]{1,0:T(8,128)}, f32[256,2048]{1,0:T(8,128)}, f32[256,2048]{1,0:T(...) custom-call(f32[256,2048]{1,0:T(8,128)} %fusion.21.rr, f32[256,2048]{1,0:T(8,128)} %fusion.20.kr, ...), custom_call_target="tpu_custom_call" | custom-call | tf_op jit(solution)/shard_map/rec_local/pallas_call | solution.py:308
  636.1 14.6 %pass_on.1.zin = f32[64,2048]{1,0:T(8,128)} custom-call(f32[64,2048]{1,0:T(8,128)} %get-tuple-element.57.move, f32[64,2048]{1,0:T(8,128)} %get-tuple-element.56.add), custom_call_target="tpu_custom_call" | custom-call | tf_op jit(solution)/shard_map/pass_on/pallas_call | solution.py:377
  651.7 22.5 %rec_out.1 = (bf16[256,2048]{1,0:T(8,128)(2,1)S(1)}, f32[256,2048]{1,0:T(8,128)S(1)}, f32[256,2048]{1,0:T(8,128)S(1)}, f32[256,2048]{1,0:T(8,128)}) custom-call(f32[64,2048]{1,0:T(8,128)S(1)} %copy-done.6, f32[256,2048]{1,0:T(8,128)} %fusion.21.rr, f32[256,2048]{1,0:T(8,128)} %fusion.20.kr, f32[256,2048]{1,0:T(8,128)} %fusion.19.vr, f32[256,2048]{1,0:T(8,128)} %fusion.60.al, ...), custom_call_target="tpu_custom_call" | custom-call | tf_op jit(solution)/shard_map/rec_out/pallas_call | solution.py:308
  675.5 5.9 fusion.12
  685.0 18.3 %collective-permute-start.1 = (f32[1,2048]{1,0:T(1,128)S(1)}, f32[1,2048]{1,0:T(1,128)S(1)}, u32[]{:S(2)}, u32[]{:S(2)}) collective-permute-start(f32[1,2048]{1,0:T(1,128)S(1)} %slice.240), channel_id=1, source_target_pairs={{0,4},{4,8},{8,12},{12,16},{16,20},{20,24},{24,28},{1,5},{5,9},{9,... | collective-permute-start | bytes 24584 | tf_op jit(solution)/shard_map/ppermute | solution.py:398
  703.4 18.8 %fusion.76 = f32[256,8192]{1,0:T(8,128)} fusion(bf16[8192,2048]{1,0:T(8,128)(2,1)} %all-gather.21.cloned.1.call-done, bf16[1,256,2048]{2,1,0:T(8,128)(2,1)} %param.12), kind=kOutput, calls=%fused_computation.143 | convolution fusion | flops 8589934592 | bytes 42991616 | tf_op jit(solution)/shard_map/dot_general | solution.py:412
  722.2 2.5 fusion.50
  726.9 145.7 %all-gather.17.cloned.1.call-done = bf16[2048,8192]{1,0:T(8,128)(2,1)} async-done(((bf16[2048,256]{1,0:T(8,128)(2,1)}), bf16[2048,8192]{1,0:T(8,128)(2,1)}) %all-gather.17.cloned.1.call-update) | async-done | bytes 33554448 | tf_op jit(solution)/shard_map/all_gather | solution.py:452
  872.6 17.4 %fusion.175 = f32[256,8192]{1,0:T(8,128)} fusion(bf16[256,2048]{1,0:T(8,128)(2,1)} %copy-done.33, bf16[2048,8192]{1,0:T(8,128)(2,1)} %all-gather.17.cloned.1.call-done), kind=kOutput, calls=%fused_computation.247 | convolution fusion | flops 8589934592 | bytes 42991616 | tf_op jit(solution)/shard_map/dot_general | solution.py:408
  890.1 4.7 fusion.3
  895.4 2.6 copy-done.16
  898.0 4.7 fusion.4
  904.7 4.3 broadcast_multiply_fusion.1
  909.5 3.4 fusion.67
  912.9 17.2 %fusion.176 = f32[256,2048]{1,0:T(8,128)} fusion(bf16[256,8192]{1,0:T(8,128)(2,1)} %copy-done.22, bf16[2048,8192]{1,0:T(8,128)(2,1)} %all-gather.17.cloned.1.call-done), kind=kOutput, calls=%fused_computation.248 | convolution fusion | flops 8589934592 | bytes 39845888 | tf_op jit(solution)/shard_map/dot_general | solution.py:412
  930.1 2.1 broadcast_multiply_fusion.2
  933.6 4.7 convolution_convert_fusion.7
  943.5 5.9 fusion.11
  949.4 2.6 convolution_add_fusion.4.dz
  952.0 21.4 %back_local.1 = (f32[256,2048]{1,0:T(8,128)S(1)}, bf16[256,2048]{1,0:T(8,128)(2,1)S(1)}, f32[256,2048]{1,0:T(8,128)S(1)}, f32[64,2048]{1,0:T(8,128)S(1)}) custom-call(f32[256,2048]{1,0:T(8,128)} %convolution_add_fusion.4.dz, f32[256,2048]{1,0:T(8,128)} %fusion.99.gg, f32[256,2048]{1,0:T(8,128)} %copy-done.3, f32[256,2048]{1,0:T(8,128)} %fusion.21.rr, ...), custom_call_target="tpu_custom_call" | custom-call | tf_op jit(solution)/shard_map/back_local/pallas_call | solution.py:308
  977.9 57.2 %pass_back.1.hin = f32[64,2048]{1,0:T(8,128)} custom-call(f32[64,2048]{1,0:T(8,128)} %get-tuple-element.55.move, f32[64,2048]{1,0:T(8,128)} %copy-done.15), custom_call_target="tpu_custom_call" | custom-call | tf_op jit(solution)/shard_map/pass_back/pallas_call | solution.py:377
  1036.1 105.3 %rec_back.1 = (bf16[256,2048]{1,0:T(8,128)(2,1)S(1)}, bf16[256,2048]{1,0:T(8,128)(2,1)S(1)}, bf16[256,2048]{1,0:T(8,128)(2,1)S(1)}, bf16[256,2048]{1,0:T(8,128)(2,1)S(1)}, bf16[256,2048]{1,0:T(8,128)(2,1)S(1)}) custom-call(f32[64,2048]{1,0:T(8,128)S(1)} %copy-done.5, f32[256,2048]{1,0:T(8,128)} %convolution_add_fusion.4.dz, f32[256,2048]{1,0:T(8,128)} %fusion.99.gg, ...), custom_call_target="tpu_custom_call" | custom-call | tf_op jit(solution)/shard_map/rec_back/pallas_call | solution.py:308
  1142.9 1.5 fusion.65
  1154.8 2.7 copy.20
  1157.5 9.0 broadcast_multiply_fusion
  1166.5 19.2 %fusion.161 = f32[256,2048]{1,0:T(8,128)} fusion(bf16[8192,2048]{1,0:T(8,128)(2,1)} %all-gather.21.cloned.1.call-done, f32[256,8192]{1,0:T(8,128)} %copy-done.16), kind=kOutput, calls=%fused_computation.243 | convolution fusion | flops 8594128896 | bytes 44040192 | tf_op jit(solution)/shard_map/dot_general | solution.py:408
  1185.7 4.8 fusion.61
  1190.4 5.9 fusion.9
  1196.3 2.6 convolution_add_fusion.1
  1198.9 5.9 fusion.7
  1204.8 2.6 convolution_add_fusion.2
  1207.3 5.8 fusion.5
  1213.2 2.7 convolution_add_fusion.3
  1215.9 4.0 fusion.113
  1220.0 9.0 multiply_add_fusion
  1229.9 1.5 collective-permute-start.3
  1231.5 3.2 fusion.28
  1234.8 2.0 slice.249
  1237.5 4.2 fusion.37
  1243.6 2.2 add_bitcast_fusion
  1245.8 102.9 %reduce-scatter.3.cloned.1.call-done = f32[8,160,64]{1,2,0:T(8,128)} async-done(((f32[8,160,2048]{1,2,0:T(8,128)}), f32[8,160,64]{1,2,0:T(8,128)}) %reduce-scatter.3.cloned.1.call-update) | async-done | bytes 327696 | tf_op jit(solution)/shard_map/reduce_scatter | solution.py:533
  (240 shorter events, 54.4 us)
Async XLA Ops:
  7.2 4.8 copy-start.81
  7.2 62.8 %all-gather.13.cloned.1.call-start = ((), (), s32[]{:S(2)}) async-start(), calls=%async_computation.4 | async-start | bytes 2162688 | tf_op jit(solution)/shard_map/all_gather | solution.py:448
  7.9 120.3 %all-gather.15.cloned.1.call-start = ((), (), s32[]{:S(2)}) async-start(), calls=%async_computation.5 | async-start | bytes 2162688 | tf_op jit(solution)/shard_map/all_gather | solution.py:447
  8.7 187.9 %all-gather.19.cloned.1.call-start = ((), (), s32[]{:S(2)}) async-start(), calls=%async_computation.7 | async-start | bytes 4325376 | tf_op jit(solution)/shard_map/all_gather | solution.py:451
  9.4 266.9 %all-gather.11.cloned.1.call-start = ((), (), s32[]{:S(2)}) async-start(), calls=%async_computation.3 | async-start | bytes 8650752 | tf_op jit(solution)/shard_map/all_gather | solution.py:449
  10.0 45.8 %copy-start.19 = (bf16[1,256,2048]{2,1,0:T(8,128)(2,1)S(1)}, bf16[1,256,2048]{2,1,0:T(8,128)(2,1)}, u32[]{:S(2)}) copy-start(bf16[1,256,2048]{2,1,0:T(8,128)(2,1)} %param.11) | copy-start | bytes 3145732
  10.0 462.2 %all-gather.9.cloned.1.call-start = ((), (), s32[]{:S(2)}) async-start(), calls=%async_computation.2 | async-start | bytes 34603008 | tf_op jit(solution)/shard_map/all_gather | solution.py:450
  10.6 692.8 %all-gather.21.cloned.1.call-start = ((), (), s32[]{:S(2)}) async-start(), calls=%async_computation.8 | async-start | bytes 34603008 | tf_op jit(solution)/shard_map/all_gather | solution.py:453
  11.1 861.5 %all-gather.17.cloned.1.call-start = ((), (), s32[]{:S(2)}) async-start(), calls=%async_computation.6 | async-start | bytes 34603008 | tf_op jit(solution)/shard_map/all_gather | solution.py:452
  11.9 1233.9 %reduce-scatter.5.cloned.1.call-start = ((), (), s32[]{:S(2)}) async-start(), calls=%async_computation.10 | async-start | bytes 8650752 | tf_op jit(solution)/shard_map/reduce_scatter | solution.py:534
  56.0 434.9 %copy-start.63 = (f32[256]{0:T(256)}, f32[256]{0:T(256)S(1)}, u32[]{:S(2)}) copy-start(f32[256]{0:T(256)S(1)} %broadcast_multiply_fusion.4) | copy-start | bytes 3076
  57.0 433.9 %copy-start.77 = (f32[256]{0:T(256)}, f32[256]{0:T(256)S(1)}, u32[]{:S(2)}) copy-start(f32[256]{0:T(256)S(1)} %fusion.152) | copy-start | bytes 3076
  57.8 12.2 copy-start.69
  57.8 73.5 %copy-start.65 = (f32[1,2048]{1,0:T(1,128)}, f32[1,2048]{1,0:T(1,128)S(1)}, u32[]{:S(2)}) copy-start(f32[1,2048]{1,0:T(1,128)S(1)} %get-tuple-element.67) | copy-start | bytes 24580
  57.8 78.2 %copy-start.67 = (f32[1,2048]{1,0:T(1,128)}, f32[1,2048]{1,0:T(1,128)S(1)}, u32[]{:S(2)}) copy-start(f32[1,2048]{1,0:T(1,128)S(1)} %get-tuple-element.68) | copy-start | bytes 24580
  57.8 414.5 %copy-start.61 = (f32[1,2048]{1,0:T(1,128)}, f32[1,2048]{1,0:T(1,128)S(1)}, u32[]{:S(2)}) copy-start(f32[1,2048]{1,0:T(1,128)S(1)} %get-tuple-element.72) | copy-start | bytes 24580
  57.8 423.9 %copy-start.59 = (f32[1,2048]{1,0:T(1,128)}, f32[1,2048]{1,0:T(1,128)S(1)}, u32[]{:S(2)}) copy-start(f32[1,2048]{1,0:T(1,128)S(1)} %get-tuple-element.71) | copy-start | bytes 24580
  57.8 433.1 %copy-start.55 = (f32[1,2048]{1,0:T(1,128)}, f32[1,2048]{1,0:T(1,128)S(1)}, u32[]{:S(2)}) copy-start(f32[1,2048]{1,0:T(1,128)S(1)} %get-tuple-element.74) | copy-start | bytes 24580
  57.8 433.1 %copy-start.57 = (f32[1,2048]{1,0:T(1,128)}, f32[1,2048]{1,0:T(1,128)S(1)}, u32[]{:S(2)}) copy-start(f32[1,2048]{1,0:T(1,128)S(1)} %get-tuple-element.70) | copy-start | bytes 24580
  58.3 3.5 collective-permute-start
  65.4 227.9 %copy-start.39 = (bf16[256,2048]{1,0:T(8,128)(2,1)}, bf16[256,2048]{1,0:T(8,128)(2,1)S(1)}, u32[]{:S(2)}) copy-start(bf16[256,2048]{1,0:T(8,128)(2,1)S(1)} %get-tuple-element.52) | copy-start | bytes 3145732
  65.4 228.3 %copy-start.37 = (bf16[256,2048]{1,0:T(8,128)(2,1)}, bf16[256,2048]{1,0:T(8,128)(2,1)S(1)}, u32[]{:S(2)}) copy-start(bf16[256,2048]{1,0:T(8,128)(2,1)S(1)} %get-tuple-element.50) | copy-start | bytes 3145732
  72.6 61.4 %copy-start.53 = (f32[256,96]{0,1:T(8,128)}, f32[256,96]{0,1:T(8,128)S(1)}, u32[]{:S(2)}) copy-start(f32[256,96]{0,1:T(8,128)S(1)} %convolution_tanh_fusion) | copy-start | bytes 294916
  128.2 3.0 copy-start.45
  131.2 2.8 copy-start.46
  288.4 4.5 copy-start.41
  478.9 2.8 copy-start.50
  674.2 7.2 copy-start.3
  674.2 7.2 copy-start.7
  675.5 5.9 copy-start.20
  682.9 257.3 %copy-start.17 = (f32[256,2048]{1,0:T(8,128)}, f32[256,2048]{1,0:T(8,128)S(1)}, u32[]{:S(2)}) copy-start(f32[256,2048]{1,0:T(8,128)S(1)} %get-tuple-element.76) | copy-start | bytes 6291460
  685.0 37.2 %collective-permute-start.1 = (f32[1,2048]{1,0:T(1,128)S(1)}, f32[1,2048]{1,0:T(1,128)S(1)}, u32[]{:S(2)}, u32[]{:S(2)}) collective-permute-start(f32[1,2048]{1,0:T(1,128)S(1)} %slice.240), channel_id=1, source_target_pairs={{0,4},{4,8},{8,12},{12,16},{16,20},{20,24},{24,28},{1,5},{5,9},{9,... | collective-permute-start | bytes 24584 | tf_op jit(solution)/shard_map/ppermute | solution.py:398
  872.6 17.4 %copy-start.48 = (bf16[1,32,8192]{2,1,0:T(8,128)(2,1)S(1)}, bf16[1,32,8192]{2,1,0:T(8,128)(2,1)}, u32[]{:S(2)}) copy-start(bf16[1,32,8192]{2,1,0:T(8,128)(2,1)} %copy.31) | copy-start | bytes 1572868
  894.7 3.3 copy-start.16
  909.1 439.6 %reduce-scatter.3.cloned.1.call-start = ((), (), s32[]{:S(2)}) async-start(), calls=%async_computation.9 | async-start | bytes 17301504 | tf_op jit(solution)/shard_map/reduce_scatter | solution.py:533
  930.1 3.5 copy-start.49
  932.3 7.2 collective-permute-start.2
  942.3 7.1 copy-start.35
  1141.4 5.2 copy-start.12
  1141.4 5.2 copy-start.14
  1141.4 10.6 copy-start.1
  1141.4 4.2 copy-start.42
  1141.4 5.2 copy-start.40
  1142.9 4.6 copy-start.38
  1145.7 3.7 copy-start.34
  1149.3 3.6 copy-start.36
  1150.2 3.6 copy-start.31
  1185.6 4.8 copy-start.2
  1215.9 4.1 copy-start.11
  1215.9 4.1 copy-start.52
  1215.9 4.1 copy-start.58
  1215.9 4.1 copy-start.60
  1215.9 4.1 copy-start.62
  1215.9 4.1 copy-start.66
  1215.9 4.1 copy-start.68
  1215.9 4.1 copy-start.70
  1220.0 11.4 copy-start.18
  1229.9 6.9 collective-permute-start.3
  1231.4 5.3 copy-start.24
  1231.4 5.3 copy-start.25
  1231.4 5.3 copy-start.26
  1234.7 2.7 copy-start.64
  1237.5 4.2 copy-start.80
  1237.5 4.3 copy-start.78
  (31 other events, 55.3 us)
Sparse Core Ops, SparseCore 0:
  10.9 59.0 all-gather.12
  72.8 55.4 all-gather.14
  131.1 65.3 all-gather.18
  199.3 76.9 all-gather.10
  279.1 193.0 all-gather.8
  474.9 193.3 all-gather.20
  669.8 202.7 all-gather.16
  909.2 143.3 reduce-scatter.4
  1166.6 182.0 reduce-scatter.2

commit v2 on v1

v2 whole, which is shorter than its diff:
```python
import functools
import math

import jax
import jax.numpy as jnp
from jax import lax
from jax.experimental import pallas as pl
from jax.experimental.pallas import tpu as pltpu
from jax.sharding import PartitionSpec as P

F32, BF = jnp.float32, jnp.bfloat16
MESH = pl.DeviceIdType.MESH
D = 64
C = 64
PW = 2 * D
DECAY_INNER, RATE_INNER, GATE_INNER, RANK = 96, 96, 256, 16
SCALE = 4.0
NORM_EPS, GROUP_EPS, UNIT_EPS = 1e-05, 0.00064, 1e-06
DECAY_SCALE = math.exp(-0.5)
PRECISE = lax.Precision.HIGHEST
DIMS = {
    "nn": (((1,), (0,)), ((), ())),
    "nt": (((1,), (1,)), ((), ())),
    "tn": (((0,), (0,)), ((), ())),
}


def split(x):
    hi = x.astype(BF)
    return hi, (x - hi.astype(F32)).astype(BF)


def dot1(a, b, m="nn"):
    return lax.dot_general(a.astype(BF), b.astype(BF), DIMS[m], preferred_element_type=F32)


def dot3(a, b, m="nn"):
    ah, al = split(a)
    bh, bl = split(b)
    ka, kb = (0 if m == "tn" else 1), (1 if m == "nt" else 0)
    n = b.shape[1 - kb]
    aa = jnp.concatenate([ah, al], axis=ka)
    bb = jnp.concatenate([jnp.concatenate([bh, bl], axis=1 - kb)] * 2, axis=kb)
    r = lax.dot_general(aa, bb, DIMS[m], preferred_element_type=F32)
    return r[:, :n] + r[:, n:]


dot_inv = dot_a = dot_w = dot_b = dot_g = dot3


def iota(shape, axis):
    return lax.broadcasted_iota(jnp.int32, shape, axis)


def stack2(x):
    lane = iota(x.shape, 1)
    zero = jnp.zeros_like(x)
    return jnp.concatenate([jnp.where(lane < D, x, zero), jnp.where(lane < D, zero, x)], axis=0)


def pack2(x):
    h = x.shape[0] // 2
    return x[:h] + x[h:]


def head_ones():
    r, c = iota((2 * PW, PW), 0) % PW, iota((2 * PW, PW), 1)
    return jnp.where((r // D) == (c // D), 1.0, 0.0).astype(BF)


def headsum(x, ones):
    h, l = split(x)
    return lax.dot_general(
        jnp.concatenate([h, l], axis=1), ones, DIMS["nn"], preferred_element_type=F32
    )


def triangle(upper):
    r, c = iota((C, C), 0), iota((C, C), 1)
    return jnp.where((r <= c) if upper else (r >= c), 1.0, 0.0).astype(BF)


def cums(x, tri):
    h, l = split(x)
    m = (x - h.astype(F32) - l.astype(F32)).astype(BF)
    n = x.shape[1]
    r = lax.dot_general(
        tri, jnp.concatenate([h, l, m], axis=1), DIMS["nn"], preferred_element_type=F32
    )
    return r[:, :n] + r[:, n : 2 * n] + r[:, 2 * n :]


def prelude(kr, wl, al, w0, a0, k_k, k_a, ones):
    s = jax.nn.sigmoid(w0 + wl)
    a = jax.nn.sigmoid(a0 + al)
    kx = kr * k_k
    rn = lax.rsqrt(headsum(kx * kx, ones) + UNIT_EPS)
    return s, -DECAY_SCALE * s, a, rn, kx * rn, kr * (1.0 + (a - 1.0) * k_a)


def grid_ids():
    r, c = iota((PW, PW), 0), iota((PW, PW), 1)
    return r, c, (r // D) == (c // D)


def inverses(many):
    r, c, _ = grid_ids()
    eye = jnp.where(r == c, 1.0, 0.0)
    b = 1
    while b < C:
        level = ((r // (2 * b)) == (c // (2 * b))) & ((r // b) % 2 == 1) & ((c // b) % 2 == 0)
        parts = [jnp.where(level, a, 0.0) for a in many]
        if b == 1:
            xs = [eye + p for p in parts]
        else:
            half = [dot_inv(x, p) for x, p in zip(xs, parts)]
            xs = [x + dot_inv(h, x) for h, x in zip(half, xs)]
        b *= 2
    return xs


def factors(logw, tri):
    run = cums(logw, tri)
    return jnp.exp(run - logw), jnp.exp(run), jnp.exp(-run), jnp.exp(run[C - 1 : C])


def forward_chunks(units, tri):
    rows, cols, same = grid_ids()
    zero = jnp.zeros((PW, PW), F32)
    strict, incl = (rows > cols) & same, (rows >= cols) & same
    fs = [factors(u[5], tri) for u in units]
    p2 = [stack2(u[1] * f[0]) for u, f in zip(units, fs)]
    r2 = [stack2(u[0] * f[1]) for u, f in zip(units, fs)]
    q2 = [stack2(u[2] * f[2]) for u, f in zip(units, fs)]
    k2 = [stack2(u[3] * f[2]) for u, f in zip(units, fs)]
    v2 = [stack2(u[4]) for u in units]
    aa = [
        dot_a(jnp.concatenate([p, r], 0), jnp.concatenate([q, k], 0), "nt")
        for p, r, q, k in zip(p2, r2, q2, k2)
    ]
    apk = [jnp.where(strict, a[:PW, PW:], zero) for a in aa]
    y = [dot_w(a, v) for a, v in zip(apk, v2)]
    xs = inverses([jnp.where(strict, a[:PW, :PW], zero) for a in aa])
    ww = [dot_w(x, jnp.concatenate([p, t], 1)) for x, p, t in zip(xs, p2, y)]
    left = [
        jnp.concatenate(
            [
                jnp.concatenate(
                    [jnp.where(incl, a[PW:, :PW], zero), jnp.where(incl, a[PW:, PW:], zero)], 1
                ),
                jnp.concatenate([(q * f[3]).T, (k * f[3]).T], 1),
            ],
            0,
        )
        for a, q, k, f in zip(aa, q2, k2, fs)
    ]
    right = [
        jnp.concatenate([w, jnp.concatenate([zero, v], 1)], 0) for w, v in zip(ww, v2)
    ]
    big = [dot_b(l, r) for l, r in zip(left, right)]
    move = [
        b[PW:, :PW] + jnp.where(rows == cols, jnp.broadcast_to(f[3], (PW, PW)), zero)
        for b, f in zip(big, fs)
    ]
    return [
        (pack2(r + b[:PW, :PW]), pack2(b[:PW, PW:]), m, b[PW:, PW:], pack2(w[:, :PW]), pack2(w[:, PW:]), x)
        for r, b, m, w, x in zip(r2, big, move, ww, xs)
    ]


def backward_chunks(units, tri, tri_up):
    rows, cols, same = grid_ids()
    zero = jnp.zeros((PW, PW), F32)
    strict, incl = (rows < cols) & same, (rows <= cols) & same
    both = jnp.concatenate([jnp.concatenate([strict, incl], 1)] * 2, 0)
    fs = [factors(t[5], tri) for t in units]
    pe = [t[1] * f[0] for t, f in zip(units, fs)]
    re = [t[0] * f[1] for t, f in zip(units, fs)]
    qe = [t[2] * f[2] for t, f in zip(units, fs)]
    ke = [t[3] * f[2] for t, f in zip(units, fs)]
    g2 = [stack2(t[10]) for t in units]
    qk = [jnp.concatenate([stack2(q), stack2(k)], 0) for q, k in zip(qe, ke)]
    pr = [jnp.concatenate([stack2(p), stack2(r)], 0) for p, r in zip(pe, re)]
    at = [dot_a(a, b, "nt") for a, b in zip(qk, pr)]
    qkh = [
        dot_g(jnp.concatenate([q * f[3], k * f[3]], 0), t[9])
        for q, k, f, t in zip(qe, ke, fs, units)
    ]
    sq = [dot_g(jnp.concatenate([t[7], t[4]], 0), t[9], "nt") for t in units]
    du = [
        dot_g(jnp.where(incl, a[:PW, PW:], zero), g) + stack2(h[:C])
        for a, g, h in zip(at, g2, qkh)
    ]
    dm = [dot_g(t[6], d, "tn") for t, d in zip(units, du)]
    dg = [jnp.concatenate([d, g], 0) for d, g in zip(dm, g2)]
    dv = [
        pack2(
            dot_g(
                jnp.concatenate(
                    [jnp.where(strict, a[PW:, :PW], zero), jnp.where(incl, a[PW:, PW:], zero)], 1
                ),
                d,
            )
        )
        + h[C:]
        for a, d, h in zip(at, dg, qkh)
    ]
    dat = [
        dot_g(jnp.concatenate([stack2(t[7]), stack2(t[4])], 0), d, "nt")
        for t, d in zip(units, dg)
    ]
    dat = [jnp.where(both, d, jnp.zeros_like(d)) for d in dat]
    dpr = [dot_g(d, a, "tn") for d, a in zip(dat, qk)]
    dqk = [dot_g(d, a) for d, a in zip(dat, pr)]
    sp = [dot_g(jnp.concatenate([pack2(d), t[10]], 0), t[8], "nt") for d, t in zip(dm, units)]
    outs = []
    for i, t in enumerate(units):
        eb, el, en, last = fs[i]
        dp, dr = pack2(dpr[i][:PW]) + sp[i][:C], pack2(dpr[i][PW:]) + sp[i][C:]
        dqh, dkh = sq[i][:C], sq[i][C:]
        dq, dk = pack2(dqk[i][:PW]) + dqh * last, pack2(dqk[i][PW:]) + dkh * last
        tail = jnp.sum((qe[i] * dqh + ke[i] * dkh) * last, axis=0, keepdims=True)
        tail = tail + last * jnp.sum((t[8] * t[9]).T, axis=0, keepdims=True)
        gb = pe[i] * dp
        gl = re[i] * dr - qe[i] * dq - ke[i] * dk
        dlogw = cums(gl + gb, tri_up) - gb + tail
        outs.append((dr * el, dp * eb, dq * en, dk * en, dv[i], dlogw))
    return outs


def lanes(ref):
    return [slice(i * PW, (i + 1) * PW) for i in range(ref.shape[-1] // PW)]


def rec_local(nc, rr, kr, vr, wl, al, vec, reff, oloc, w1, w2, xs, mv, mt, piece):
    ones, tri = head_ones(), triangle(False)
    units, where = [], []
    for ln in lanes(rr):
        row = lambda i: vec[i : i + 1, ln]
        _, logw, a, _, kk, km = prelude(
            kr[:, ln], wl[:, ln], al[:, ln], row(8), row(9), row(10), row(11), ones
        )
        r, v, q = rr[:, ln], vr[:, ln], kk * a
        for c in range(nc):
            s = slice(c * C, (c + 1) * C)
            units.append((r[s], -kk[s], q[s], km[s], v[s], logw[s]))
            where.append((s, ln))
    done = forward_chunks(units, tri)
    packed = []
    for (s, ln), (e, o, m, n, y1, y2, x) in zip(where, done):
        reff[s, ln], oloc[s, ln], w1[s, ln], w2[s, ln] = e, o, y1, y2
        xs[s, ln] = pack2(x)
        mp = pack2(m)
        mv[0, s, ln], mv[1, s, ln], mt[s, ln] = mp, pack2(n), pack2(m.T)
        packed.append(mp)
    for i, ln in enumerate(lanes(rr)):
        tm, tn = stack2(packed[i * nc]), done[i * nc][3]
        for c in range(1, nc):
            t = dot3(packed[i * nc + c], jnp.concatenate([tm, tn], 1))
            tm, tn = stack2(t[:, :PW]), stack2(t[:, PW:]) + done[i * nc + c][3]
        piece[0, :, ln], piece[1, :, ln], piece[2, :, ln] = pack2(tm), pack2(tn), pack2(tm.T)


def norm_parts(o, ones):
    centre = o - headsum(o, ones) * (1.0 / D)
    rstd = lax.rsqrt(headsum(centre * centre, ones) * (1.0 / D) + GROUP_EPS)
    return centre * rstd, rstd


def rec_out(
    nc, zin, rr, kr, vr, al, gg, vec, reff, oloc, w1, w2, mv, tokens, wo, down, up, norm,
    z_out, o_out, u_out, zs, middle, normed, h_out, acc_h,
):
    step, last = pl.program_id(0), pl.num_programs(0) - 1
    ones = head_ones()
    state = [zin[:, ln] for ln in lanes(rr)]
    for c in range(nc):
        s = slice(c * C, (c + 1) * C)
        ts = [
            dot3(jnp.concatenate([mv[0, s, ln], reff[s, ln], w1[s, ln]], 0), stack2(z))
            for z, ln in zip(state, lanes(rr))
        ]
        for i, (t, ln) in enumerate(zip(ts, lanes(rr))):
            zs[s, ln] = state[i]
            o_out[s, ln] = t[C : 2 * C] + oloc[s, ln]
            u_out[s, ln] = t[2 * C :] + w2[s, ln]
            state[i] = t[:C] + mv[1, s, ln]
    for ln in lanes(rr):
        row = lambda i: vec[i : i + 1, ln]
        a = jax.nn.sigmoid(row(9) + al[:, ln])
        km = kr[:, ln] * (1.0 + (a - 1.0) * row(11))
        hat, _ = norm_parts(o_out[:, ln], ones)
        y = hat * row(13) + row(14) + headsum(rr[:, ln] * km * row(12), ones) * vr[:, ln]
        z_out[:, ln] = (y * gg[:, ln]).astype(BF)

    @pl.when(step == 0)
    def _():
        acc_h[...] = jnp.zeros_like(acc_h)
        middle[...] = tokens[...].astype(F32)

    acc_h[...] += mm_nt(z_out[...], down[...])
    middle[...] += mm_nt(z_out[...], wo[...])

    @pl.when(step == last)
    def _():
        h_out[...] = acc_h[...].astype(BF)
        x1 = middle[...] + SCALE * mm(h_out[...], up[...])
        middle[...] = x1
        centre = x1 - jnp.mean(x1, axis=-1, keepdims=True)
        rstd = lax.rsqrt(jnp.mean(centre * centre, axis=-1, keepdims=True) + NORM_EPS)
        normed[...] = centre * rstd * norm[15:16, :] + norm[16:17, :]


def back_local(
    nc, d_mc, edge, gy, middle, norm, wo, down, down_all, up, h_o, gated,
    gg, o, rr, kr, vr, al, vec, reff, mt,
    d_mid, dz, do, dgg, es, piece, g_down, g_up, low, dh,
):
    @pl.when(pl.program_id(0) == 0)
    def _():
        moved = d_mc[...] * norm[17:18, :]
        n = moved.shape[0]
        up_one = pltpu.roll(moved, n - 1, axis=0)
        up_one = jnp.where(iota(moved.shape, 0) == n - 1, edge[...], up_one)
        dn = d_mc[...] - moved + up_one
        x1 = middle[...]
        centre = x1 - jnp.mean(x1, axis=-1, keepdims=True)
        rstd = lax.rsqrt(jnp.mean(centre * centre, axis=-1, keepdims=True) + NORM_EPS)
        hat = centre * rstd
        dhat = dn * norm[15:16, :]
        d = rstd * (
            dhat
            - jnp.mean(dhat, axis=-1, keepdims=True)
            - hat * jnp.mean(dhat * hat, axis=-1, keepdims=True)
        )
        d = d + gy[...].astype(F32)
        d_mid[...] = d
        low[...] = d.astype(BF)
        dh[...] = (SCALE * mm_nt(low[...], up[...])).astype(BF)
        g_up[...] = SCALE * mm_tn(h_o[...], low[...])

    dz[...] = mm(low[...], wo[...]) + mm(dh[...], down[...])
    g_down[...] = mm_tn(dh[...], gated[...])
    ones = head_ones()
    _, _, same = grid_ids()
    for ln in lanes(rr):
        row = lambda i: vec[i : i + 1, ln]
        a = jax.nn.sigmoid(row(9) + al[:, ln])
        km = kr[:, ln] * (1.0 + (a - 1.0) * row(11))
        hat, rstd = norm_parts(o[:, ln], ones)
        y = hat * row(13) + row(14) + headsum(rr[:, ln] * km * row(12), ones) * vr[:, ln]
        dgg[:, ln] = (dz[:, ln] * y).astype(BF)
        dhat = dz[:, ln] * gg[:, ln] * row(13)
        do[:, ln] = rstd * (
            dhat
            - headsum(dhat, ones) * (1.0 / D)
            - hat * (headsum(dhat * hat, ones) * (1.0 / D))
        )
    for c in range(nc):
        s = slice(c * C, (c + 1) * C)
        for ln in lanes(rr):
            es[s, ln] = pack2(jnp.where(same, dot3(reff[s, ln], do[s, ln], "tn"), 0.0))
    state = [es[(nc - 1) * C : nc * C, ln] for ln in lanes(rr)]
    for c in reversed(range(nc - 1)):
        s = slice(c * C, (c + 1) * C)
        state = [es[s, ln] + dot3(mt[s, ln], stack2(h)) for h, ln in zip(state, lanes(rr))]
    for h, ln in zip(state, lanes(rr)):
        piece[:, ln] = h


def rec_back(
    nc, hin, dz, gg, do, rr, kr, vr, wl, al, vec, xs, us, zs, mt, es, drr, dkr, dvr, dwl, dal
):
    ones, tri, tri_up = head_ones(), triangle(False), triangle(True)
    units, where, pre = [], [], []
    hs = {}
    for ln in lanes(rr):
        h = hin[:, ln]
        for c in reversed(range(nc)):
            s = slice(c * C, (c + 1) * C)
            hs[c, ln.start] = stack2(h)
            if c:
                h = dot3(mt[s, ln], hs[c, ln.start]) + es[s, ln]
    for ln in lanes(rr):
        row = lambda i: vec[i : i + 1, ln]
        for c in range(nc):
            s = slice(c * C, (c + 1) * C)
            r, v, k = rr[s, ln], vr[s, ln], kr[s, ln]
            sg, logw, a, rn, kk, km = prelude(
                k, wl[s, ln], al[s, ln], row(8), row(9), row(10), row(11), ones
            )
            units.append(
                (r, -kk, kk * a, km, v, logw, stack2(xs[s, ln]), us[s, ln], stack2(zs[s, ln]),
                 hs[c, ln.start], do[s, ln])
            )
            where.append((s, ln))
            pre.append((sg, a, rn, kk, km))
    done = backward_chunks(units, tri, tri_up)
    for (s, ln), (sg, a, rn, kk, km), (dr, dp, dq, dk, dv, dlogw) in zip(where, pre, done):
        row = lambda i: vec[i : i + 1, ln]
        r, v, k = rr[s, ln], vr[s, ln], kr[s, ln]
        dy = dz[s, ln] * gg[s, ln]
        dv = dv + headsum(r * km * row(12), ones) * dy
        ds = headsum(dy * v, ones) * row(12)
        dr = dr + ds * km
        dkm = dk + ds * r
        dkk = dq * a - dp
        da = dq * kk + dkm * k * row(11)
        dk = dkm * (1.0 + (a - 1.0) * row(11)) + row(10) * rn * (dkk - kk * headsum(dkk * kk, ones))
        drr[s, ln], dkr[s, ln], dvr[s, ln] = dr.astype(BF), dk.astype(BF), dv.astype(BF)
        dwl[s, ln] = (dlogw * (-DECAY_SCALE) * sg * (1.0 - sg)).astype(BF)
        dal[s, ln] = (da * a * (1.0 - a)).astype(BF)


TILE = 2 * PW


def cut(shape):
    lead = tuple(shape[:-1])
    return pl.BlockSpec(lead + (TILE,), lambda i, n=len(lead): (0,) * n + (i,))


def whole(shape):
    return pl.BlockSpec(tuple(shape), lambda i, n=len(shape): (0,) * n)


def tile_rows(shape):
    return pl.BlockSpec((TILE, shape[1]), lambda i: (i, 0))


def over_tiles(body, steps, ins, outs, name, scratch=(), **params):
    made = lambda spec, shape: spec if isinstance(spec, pl.BlockSpec) else spec(shape)
    return pl.pallas_call(
        body,
        grid=(steps,),
        in_specs=[made(spec, x.shape) for spec, x in ins],
        out_specs=[made(spec, x.shape) for spec, x in outs],
        out_shape=[x for _, x in outs],
        scratch_shapes=list(scratch),
        compiler_params=pltpu.CompilerParams(vmem_limit_bytes=60 * 1024 * 1024, **params),
        name=name,
    )(*[x for _, x in ins])


def pass_kernel(n, groups, back, move, add, out, here, send, send_sem, recv_sem):
    s, d = lax.axis_index("seq"), lax.axis_index("dp")
    if back:
        first, final, nxt, prv = s == n - 1, s == 0, s - 1, s + 1
    else:
        first, final, nxt, prv = s == 0, s == n - 1, s + 1, s - 1
    barrier = pltpu.get_barrier_semaphore()

    @pl.when(jnp.logical_not(first))
    def _():
        pl.semaphore_signal(barrier, inc=1, device_id=(prv, d), device_id_type=MESH)

    @pl.when(jnp.logical_not(final))
    def _():
        pl.semaphore_wait(barrier, 1)

    def copy(g, to):
        return pltpu.make_async_remote_copy(
            src_ref=send.at[g],
            dst_ref=here.at[g],
            send_sem=send_sem.at[g],
            recv_sem=recv_sem.at[g],
            device_id=(to, d),
            device_id_type=MESH,
        )

    per = out.shape[1] // (groups * PW)
    for g in range(groups):

        @pl.when(first)
        def _():
            here[g] = jnp.zeros(here.shape[1:], F32)

        @pl.when(jnp.logical_not(first))
        def _():
            copy(g, prv).wait_recv()

        out[:, g * per * PW : (g + 1) * per * PW] = here[g]

        @pl.when(jnp.logical_not(final))
        def _():
            for i in range(per):
                at = (g * per + i) * PW
                state = stack2(here[g, :, i * PW : (i + 1) * PW])
                send[g, :, i * PW : (i + 1) * PW] = (
                    dot3(move[:, at : at + PW], state) + add[:, at : at + PW]
                )
            copy(g, nxt).start()

    @pl.when(jnp.logical_not(final))
    def _():
        for g in range(groups):
            copy(g, nxt).wait_send()


def pass_states(n, move, add, back):
    rows, width = move.shape
    groups = width // PW
    return pl.pallas_call(
        functools.partial(pass_kernel, n, groups, back),
        out_shape=jax.ShapeDtypeStruct((rows, width), F32),
        in_specs=[pl.BlockSpec(memory_space=pltpu.VMEM)] * 2,
        out_specs=pl.BlockSpec(memory_space=pltpu.VMEM),
        scratch_shapes=[
            pltpu.VMEM((groups, rows, width // groups), F32),
            pltpu.VMEM((groups, rows, width // groups), F32),
            pltpu.SemaphoreType.DMA((groups,)),
            pltpu.SemaphoreType.DMA((groups,)),
        ],
        compiler_params=pltpu.CompilerParams(
            collective_id=1 if back else 0, has_side_effects=True
        ),
        name="pass_back" if back else "pass_on",
    )(move, add)


ORDERS = ("zxy", "zyx", "xzy", "yzx")
DIRS = "xyuds"


def gather_events(order, z, x, y):
    other = {"x": lambda q: (q, 1 - x, y), "y": lambda q: (q, x, 1 - y), "z": lambda q: (q, x, y)}
    inside = lambda k: None if k == 0 else jnp.logical_and(z + k >= 0, z + k <= 3)
    if order[0] == "z":
        a, b = order[1], order[2]
        events = [(0, (z, x, y), None, None, [a, b, "u", "d", "s"])]
        for k in (1, 2, 3):
            events.append((k, (z - k, x, y), "u", z >= k, ["u", a, b, "s"]))
            events.append((k, (z + k, x, y), "d", z + k <= 3, ["d", a, b, "s"]))
        for k in range(-3, 4):
            events.append((abs(k) + 1, other[a](z + k), a, inside(k), [b, "s"]))
    else:
        a, b = order[0], order[2]
        events = [(0, (z, x, y), None, None, [a, "u", "d", b, "s"])]
        events.append((1, other[a](z), a, None, ["u", "d", b, "s"]))
        for k in (1, 2, 3):
            for late, at in ((0, other["z"]), (1, other[a])):
                events.append((k + late, at(z - k), "u", z >= k, ["u", b, "s"]))
                events.append((k + late, at(z + k), "d", z + k <= 3, ["d", b, "s"]))
    for k in range(-3, 4):
        events.append((abs(k) + 1, other[b](z + k), b, inside(k), ["s"]))
        events.append((abs(k) + 2, (z + k, 1 - x, 1 - y), b, inside(k), ["s"]))
    return events


def maybe(condition, run):
    if condition is None:
        run()
    else:
        pl.when(condition)(run)


def gather_kernel(orders, *refs):
    n = len(orders)
    shards, whole = refs[:n], refs[n : 2 * n]
    send, recv, near = refs[2 * n :]
    seq, dp = lax.axis_index("seq"), lax.axis_index("dp")
    z, x, y, c = seq // 2, seq % 2, dp // 2, dp % 2
    to = {
        "x": (z * 2 + 1 - x, dp),
        "y": (seq, (1 - y) * 2 + c),
        "u": (seq + 2, dp),
        "d": (seq - 2, dp),
        "s": (seq, y * 2 + 1 - c),
    }
    exists = {"u": z < 3, "d": z > 0}
    barrier = pltpu.get_barrier_semaphore()
    for k in DIRS:
        maybe(
            exists.get(k),
            lambda k=k: pl.semaphore_signal(barrier, inc=1, device_id=to[k], device_id_type=MESH),
        )
    pl.semaphore_wait(barrier, 3 + (z + 2) // 3 + (5 - z) // 3)

    chip = lambda b: b[0] * 4 + b[1] * 2 + b[2]

    def copy(t, own, b, k):
        slot = whole[t].at[chip(b) * 2 + c]
        return pltpu.make_async_remote_copy(
            src_ref=shards[t] if own else slot,
            dst_ref=slot,
            send_sem=send.at[DIRS.index(k), t, chip(b)],
            recv_sem=recv.at[1 if k == "s" else 0, t, chip(b)],
            device_id=to[k],
            device_id_type=MESH,
        )

    todo = [(e[0], t, i, e) for t, o in enumerate(orders) for i, e in enumerate(gather_events(o, z, x, y))]
    todo.sort(key=lambda q: q[0])
    sent, own = [], []
    for _, t, _, (_, b, came, condition, goes) in todo:
        if came is None:
            own.append(pltpu.make_async_copy(shards[t], whole[t].at[chip(b) * 2 + c], near.at[t]))
            own[-1].start()
        else:
            maybe(condition, lambda: copy(t, False, b, came).wait_recv())
        for k in goes:
            both = exists.get(k) if condition is None else condition
            if condition is not None and k in exists:
                both = jnp.logical_and(condition, exists[k])
            maybe(both, lambda: copy(t, came is None, b, k).start())
            sent.append((t, came is None, b, k, both))
    for t in range(n):
        for i in range(16):
            pltpu.make_async_remote_copy(
                src_ref=shards[t],
                dst_ref=whole[t].at[i * 2 + 1 - c],
                send_sem=send.at[4, t, i],
                recv_sem=recv.at[1, t, i],
                device_id=to["s"],
                device_id_type=MESH,
            ).wait_recv()
    for t, mine, b, k, both in sent:
        maybe(both, lambda: copy(t, mine, b, k).wait_send())
    for o in own:
        o.wait()


def gather(shards):
    n_seq, n_dp, n = lax.axis_size("seq"), lax.axis_size("dp"), len(shards)
    if (n_seq, n_dp) != (8, 4):
        return [lax.all_gather(s, ("seq", "dp"), axis=0) for s in shards]
    return pl.pallas_call(
        functools.partial(gather_kernel, [ORDERS[i % len(ORDERS)] for i in range(n)]),
        out_shape=[jax.ShapeDtypeStruct((n_seq * n_dp,) + s.shape, s.dtype) for s in shards],
        in_specs=[pl.BlockSpec(memory_space=pl.ANY)] * n,
        out_specs=[pl.BlockSpec(memory_space=pl.ANY)] * n,
        scratch_shapes=[
            pltpu.SemaphoreType.DMA((5, n, 16)),
            pltpu.SemaphoreType.DMA((2, n, 16)),
            pltpu.SemaphoreType.DMA((n,)),
        ],
        compiler_params=pltpu.CompilerParams(collective_id=2, has_side_effects=True),
        name="gather_time",
    )(*shards)


def channel_kernel(
    n2, edge, norm, gy, middle, down_c, up_f, kv, hidden,
    out, dmc, first, g_hidden, g_up_f, g_down_c, mc, ffo, h_c, dh_f, acc_f, acc_c,
):
    step, last = pl.program_id(0), pl.num_programs(0) - 1
    per, ff = kv.shape[0], kv.shape[1] // 2

    @pl.when(step == 0)
    def _():
        x = n2[...]
        before = jnp.where(iota(x.shape, 0) == 0, edge[...], pltpu.roll(x, 1, axis=0))
        mc[...] = (x + (before - x) * norm[17:18, :]).astype(BF)
        h_c[...] = mm_nt(mc[...], down_c[...]).astype(BF)
        dh_f[...] = (SCALE * mm_nt(gy[...], up_f[...])).astype(BF)
        acc_f[...] = jnp.zeros_like(acc_f)
        acc_c[...] = jnp.zeros_like(acc_c)
        ffo[...] = jnp.zeros_like(ffo)
        dmc[...] = jnp.zeros_like(dmc)

    hqs, dps = [], []
    for b in range(per):
        down_f, up_c = hidden[b, :RANK], hidden[b, RANK:]
        pre = mm_nt(mc[...], kv[b, :ff]) + SCALE * mm(h_c[...], up_c)
        dsq = mm_nt(gy[...], kv[b, ff:]) + mm(dh_f[...], down_f)
        active = jnp.maximum(pre, 0.0)
        hq = (active * active).astype(BF)
        dpre = (dsq * (2.0 * active)).astype(BF)
        g_hidden[b, :RANK] = mm_tn(dh_f[...], hq)
        g_hidden[b, RANK:] = SCALE * mm_tn(h_c[...], dpre)
        acc_f[...] += mm_nt(hq, down_f)
        acc_c[...] += mm_nt(dpre, up_c)
        hqs.append(hq)
        dps.append(dpre)
    hq, dpre = jnp.concatenate(hqs, 1), jnp.concatenate(dps, 1)
    ffo[...] += mm(hq, jnp.concatenate([kv[b, ff:] for b in range(per)], 0))
    dmc[...] += mm(dpre, jnp.concatenate([kv[b, :ff] for b in range(per)], 0))

    @pl.when(step == last)
    def _():
        h_f = acc_f[...].astype(BF)
        out[...] = (middle[...] + ffo[...] + SCALE * mm(h_f, up_f[...])).astype(BF)
        g_up_f[...] = SCALE * mm_tn(h_f, gy[...])
        dh_c = (SCALE * acc_c[...]).astype(BF)
        d = dmc[...] + mm(dh_c, down_c[...])
        dmc[...] = d
        first[...] = d[:8] * norm[17:18, :]
        g_down_c[...] = mm_tn(dh_c, mc[...])


def channel(n2, edge, norm, gy, middle, down_c, up_f, kv, hidden):
    n, both, width = kv.shape
    ff, length = both // 2, n2.shape[0]
    per = max(1, min(n, 512 // ff))
    block = lambda shape: pl.BlockSpec((per,) + tuple(shape[1:]), lambda i: (i, 0, 0))
    rank = jax.ShapeDtypeStruct((RANK, width), F32)
    return over_tiles(
        channel_kernel,
        n // per,
        [(whole, a) for a in (n2, edge, norm, gy, middle, down_c, up_f)] + [(block, kv), (block, hidden)],
        [
            (whole, jax.ShapeDtypeStruct((length, width), BF)),
            (whole, jax.ShapeDtypeStruct((length, width), F32)),
            (whole, jax.ShapeDtypeStruct((8, width), F32)),
            (block, jax.ShapeDtypeStruct((n, 2 * RANK, ff), F32)),
            (whole, rank),
            (whole, rank),
        ],
        "channel",
        [
            pltpu.VMEM((length, width), BF),
            pltpu.VMEM((length, width), F32),
            pltpu.VMEM((length, RANK), BF),
            pltpu.VMEM((length, RANK), BF),
            pltpu.VMEM((length, RANK), F32),
            pltpu.VMEM((length, RANK), F32),
        ],
    )


HALF = 512


def branch_masks(shape):
    lane = iota(shape, 1)
    lo, hi = DECAY_INNER, DECAY_INNER + RATE_INNER
    return lane < lo, (lane >= lo) & (lane < hi), (lane >= hi) & (lane < hi + GATE_INNER)


def project_kernel(
    hat, hat_prev, valid, vec, first, chosen, second, w_r, w_k, w_v, up,
    rr, kr, vr, wl, al, gg, m_r, m_k, m_v, hs, act, act_low,
):
    @pl.when(pl.program_id(0) == 0)
    def _():
        n1 = hat[...] * vec[0:1, :] + vec[1:2, :]
        change = (hat_prev[...] * vec[0:1, :] + vec[1:2, :]) * valid[...] - n1
        mixed = lambda i: (n1 + change * vec[2 + i : 3 + i, :]).astype(BF)
        m_r[...], m_k[...], m_v[...] = mixed(0), mixed(2), mixed(3)
        for i, m in enumerate((m_r, m_k, m_v)):
            hs[i] = mm_nt(m[...], chosen[i * RANK : (i + 1) * RANK, :]).astype(BF)
        t_w = mm(mixed(1), first[...])
        t_a = mm(mixed(4), first[...])
        t_g = mm(mixed(5), first[...])
        is_w, is_a, is_g = branch_masks(t_w.shape)
        zero = jnp.zeros_like(t_w)
        t_w = jnp.where(is_w, jnp.tanh(t_w), zero)
        t_a = jnp.where(is_a, t_a, zero)
        t_g = jnp.where(is_g, jax.nn.sigmoid(t_g), zero)
        act[...] = t_w + t_a + t_g
        act_low[0], act_low[1], act_low[2] = t_w.astype(BF), t_a.astype(BF), t_g.astype(BF)

    for i, (m, w, out) in enumerate(((m_r, w_r, rr), (m_k, w_k, kr), (m_v, w_v, vr))):
        out[...] = mm_nt(m[...], w[...]) + SCALE * mm(hs[i], up[(5 + i) * RANK : (6 + i) * RANK, :])
    for i, out in enumerate((wl, al, gg)):
        out[...] = mm_nt(act_low[i], second[...])


def late_kernel(drr, dkr, dvr, dwl, dal, dgg, m_r, m_k, m_v, hs, act, chosen, second, dhs, d_act, grads):
    for i, (d, m) in enumerate(((drr, m_r), (dkr, m_k), (dvr, m_v))):
        dh = (SCALE * mm_nt(d[...], chosen[(5 + i) * RANK : (6 + i) * RANK, :])).astype(BF)
        dhs[i] = dh
        down, up = mm_tn(dh, m[...]), SCALE * mm_tn(hs[i], d[...])
        wide = grads.shape[2]
        for p in range(grads.shape[0]):
            part = slice(p * wide, (p + 1) * wide)
            grads[p, i * RANK : (i + 1) * RANK, :] = down[:, part]
            grads[p, (3 + i) * RANK : (4 + i) * RANK, :] = up[:, part]
    is_w, is_a, is_g = branch_masks(act.shape)
    a = act[...]
    zero = jnp.zeros_like(a)
    d_act[0] = jnp.where(is_w, mm(dwl[...], second[...]) * (1.0 - a * a), zero).astype(BF)
    d_act[1] = jnp.where(is_a, mm(dal[...], second[...]), zero).astype(BF)
    d_act[2] = jnp.where(is_g, mm(dgg[...], second[...]) * a * (1.0 - a), zero).astype(BF)


def final_kernel(
    n, drr, dkr, dvr, w_r, w_k, w_v, dhs, down, d_act, first, vec, parts,
    stay, go, summed, here, send_sem, recv_sem,
):
    step, last = pl.program_id(0), pl.num_programs(0) - 1
    me, dp = lax.axis_index("seq"), lax.axis_index("dp")

    def copy(k):
        peer = lax.rem(me + k, n)
        return pltpu.make_async_remote_copy(
            src_ref=parts.at[peer],
            dst_ref=here.at[k - 1],
            send_sem=send_sem.at[k - 1],
            recv_sem=recv_sem.at[k - 1],
            device_id=(peer, dp),
            device_id_type=MESH,
        )

    @pl.when(step == 0)
    def _():
        barrier = pltpu.get_barrier_semaphore()
        for k in range(1, n):
            pl.semaphore_signal(
                barrier, inc=1, device_id=(lax.rem(me + k, n), dp), device_id_type=MESH
            )
        pl.semaphore_wait(barrier, n - 1)
        for k in range(1, n):
            copy(k).start()

    total, moved = None, None
    for i, (d, w, at) in enumerate(((drr, w_r, 2), (dkr, w_k, 4), (dvr, w_v, 5))):
        g = mm(d[...], w[...]) + mm(dhs[i], down[i * RANK : (i + 1) * RANK, :])
        move = g * vec[at : at + 1, :]
        total, moved = (g, move) if total is None else (total + g, moved + move)
    for i, at in enumerate((3, 6, 7)):
        g = mm_nt(d_act[i], first[...])
        total, moved = total + g, moved + g * vec[at : at + 1, :]
    stay[...] = total - moved
    go[...] = moved

    @pl.when(step == last)
    def _():
        for k in range(1, n):
            copy(k).wait()
        t = parts[me]
        for k in range(1, n):
            t = t + here[k - 1]
        summed[...] = t


def shifted(block, axis, distance):
    devices = range(lax.axis_size(axis))
    route = [(i - distance, i) for i in devices if i - distance in devices]
    return lax.ppermute(block, axis, route)


def mm(a, b):
    return lax.dot_general(a, b, DIMS["nn"], preferred_element_type=F32)


def mm_nt(a, b):
    return lax.dot_general(a, b, DIMS["nt"], preferred_element_type=F32)


def mm_tn(a, b):
    return lax.dot_general(a, b, DIMS["tn"], preferred_element_type=F32)


def body(tokens, output_gradient, index, proj, first, second, vectors, ckey, cvalue, model_rows, hidden_rows):
    axes = ("seq", "dp")
    n_seq, n_dp = lax.axis_size("seq"), lax.axis_size("dp")
    n = n_seq * n_dp
    tokens, gy = tokens[0], output_gradient[0]
    length, width = tokens.shape
    nc, tiles = length // C, width // TILE
    adapters, kinds, cols = model_rows.shape
    ff, inner, nvec = ckey.shape[1], first.shape[1], vectors.shape[0]

    kv = lax.all_gather(jnp.concatenate([ckey.T, cvalue], 0), axes, axis=0)

    index_all = lax.all_gather(index, "dp", axis=0, tiled=True)
    pick = index_all[:, None] == jnp.arange(adapters, dtype=jnp.int32)[None, :]
    few = jnp.concatenate([model_rows.reshape(adapters, -1), hidden_rows.reshape(adapters, -1)], 1)
    few = jnp.einsum("sa,ax->sx", pick.astype(BF), few, preferred_element_type=F32).astype(BF)
    pad = lambda k: jnp.zeros((cols, k), BF)
    misc = jnp.concatenate(
        [first, pad(HALF - inner), second.T, vectors.T, pad(HALF - inner - nvec)], axis=1
    )
    turned = jnp.swapaxes(proj, 1, 2)

    wide = tokens.astype(F32)
    ahead = shifted(tokens[-1:], "seq", 1).astype(F32)
    rows = jnp.concatenate([ahead, wide], 0)
    centre = rows - jnp.mean(rows, axis=-1, keepdims=True)
    rstd = lax.rsqrt(jnp.mean(centre * centre, axis=-1, keepdims=True) + NORM_EPS)
    hat = centre * rstd
    start = (jnp.arange(length)[:, None] == 0) & (lax.axis_index("seq") == 0)
    valid = jnp.where(start, 0.0, 1.0).astype(F32)
    hat_prev, hat, rstd = hat[:-1], hat[1:], rstd[1:]

    *mats, misc, few_all = gather([turned[0], turned[1], turned[2], turned[3], misc, few.reshape(-1, 128)])
    mats = [m.reshape(width, width) for m in mats]
    misc = misc.reshape(width, -1)
    vec = misc[:, HALF + inner : HALF + inner + nvec].T.astype(F32)
    own = lax.dynamic_index_in_dim(few_all.reshape(n, n_dp, -1, 128), lax.axis_index("dp"), 1, False)
    own = own.reshape(n, -1)
    chosen = own[:, : kinds * cols].reshape(n, kinds, cols).transpose(1, 0, 2).reshape(kinds, width)
    hidden = own[:, kinds * cols :].reshape(n, 2 * RANK, ff)
    down = lambda i: chosen[i * RANK : (i + 1) * RANK]
    up = lambda i: chosen[(5 + i) * RANK : (6 + i) * RANK]

    shape = jax.ShapeDtypeStruct
    full, low = shape((length, width), F32), shape((length, width), BF)
    small, rank = shape((D, width), F32), shape((RANK, width), F32)
    firsts = pl.BlockSpec((width, HALF), lambda i: (0, 0))
    seconds = pl.BlockSpec((width, HALF), lambda i: (0, 1))
    first_rows = pl.BlockSpec((TILE, HALF), lambda i: (i, 0))
    second_rows = pl.BlockSpec((TILE, HALF), lambda i: (i, 1))
    rr, kr, vr, wl, al, gg, m_r, m_k, m_v, hs, act = over_tiles(
        project_kernel, tiles,
        [
            (whole, hat), (whole, hat_prev), (whole, valid), (whole, vec), (firsts, misc), (whole, chosen),
            (second_rows, misc), (tile_rows, mats[0]), (tile_rows, mats[1]), (tile_rows, mats[2]), (cut, chosen),
        ],
        [(cut, full)] * 6
        + [(whole, low)] * 3
        + [(whole, shape((3, length, RANK), BF)), (whole, shape((length, HALF), F32))],
        "project",
        [pltpu.VMEM((3, length, HALF), BF)],
    )
    reff, oloc, w1, w2, xs, mv, mt, piece = over_tiles(
        functools.partial(rec_local, nc), tiles,
        [(cut, a) for a in (rr, kr, vr, wl, al, vec)],
        [(cut, full)] * 5 + [(cut, shape((2, length, width), F32)), (cut, full), (cut, shape((3, D, width), F32))],
        "rec_local",
    )
    zin = pass_states(n_seq, piece[0], piece[1], False)
    gated, o, us, zs, middle, n2, h_o = over_tiles(
        functools.partial(rec_out, nc), tiles,
        [(cut, a) for a in (zin, rr, kr, vr, al, gg, vec, reff, oloc, w1, w2, mv)]
        + [(whole, tokens), (cut, mats[3]), (cut, down(3)), (whole, up(3)), (whole, vec)],
        [(cut, low), (cut, full), (cut, full), (cut, full), (whole, full), (whole, full), (whole, shape((length, RANK), BF))],
        "rec_out",
        [pltpu.VMEM((length, RANK), F32)],
    )
    result, d_mc, moved, g_hidden, up_f, down_c = channel(
        n2, shifted(n2[-1:], "seq", 1), vec, gy, middle, down(4), up(4), kv, hidden
    )
    d_mid, dz, do, dgg, es, eloc, down_o, up_o = over_tiles(
        functools.partial(back_local, nc), tiles,
        [
            (whole, d_mc), (whole, shifted(moved[:1], "seq", -1)), (whole, gy), (whole, middle), (whole, vec),
            (cut, mats[3]), (cut, down(3)), (whole, down(3)), (whole, up(3)), (whole, h_o),
        ]
        + [(cut, a) for a in (gated, gg, o, rr, kr, vr, al, vec, reff, mt)],
        [(whole, full), (cut, full), (cut, full), (cut, low), (cut, full), (cut, small), (cut, rank), (whole, rank)],
        "back_local",
        [pltpu.VMEM((length, width), BF), pltpu.VMEM((length, RANK), BF)],
    )
    wide = n_dp * cols
    early = jnp.concatenate([down_o, down_c, up_o, up_f], 0)
    early = jnp.swapaxes(early.reshape(4 * RANK, n_seq, wide), 0, 1)
    early = jnp.concatenate([early, g_hidden.reshape(n_seq, -1, wide)], 1)
    early = lax.psum_scatter(early, "seq", scatter_dimension=0, tiled=True)[0]
    hin = pass_states(n_seq, piece[2], eloc, True)
    drr, dkr, dvr, dwl, dal = over_tiles(
        functools.partial(rec_back, nc), tiles,
        [(cut, a) for a in (hin, dz, gg, do, rr, kr, vr, wl, al, vec, xs, us, zs, mt, es)],
        [(cut, low)] * 5, "rec_back",
    )
    early, drr = lax.optimization_barrier((early, drr))
    dhs, d_act, late = over_tiles(
        late_kernel, 1,
        [(whole, a) for a in (drr, dkr, dvr, dwl, dal, dgg, m_r, m_k, m_v, hs, act, chosen)] + [(seconds, misc)],
        [
            (whole, shape((3, length, RANK), BF)),
            (whole, shape((3, length, HALF), BF)),
            (whole, shape((n_seq, 6 * RANK, wide), F32)),
        ],
        "late",
    )
    stay, go, late = over_tiles(
        functools.partial(final_kernel, n_seq), tiles,
        [
            (whole, drr), (whole, dkr), (whole, dvr), (cut, mats[0]), (cut, mats[1]), (cut, mats[2]),
            (whole, dhs), (cut, chosen), (whole, d_act), (first_rows, misc), (cut, vec), (whole, late),
        ],
        [(cut, full)] * 2 + [(whole, shape((6 * RANK, wide), F32))], "final",
        [
            pltpu.VMEM((n_seq - 1, 6 * RANK, wide), F32),
            pltpu.SemaphoreType.DMA((n_seq - 1,)),
            pltpu.SemaphoreType.DMA((n_seq - 1,)),
        ],
        collective_id=3, has_side_effects=True,
    )
    d_n1 = stay + jnp.concatenate([go[1:], shifted(go[:1], "seq", -1)], 0)
    dhat = d_n1 * vec[0:1]
    grad_tokens = d_mid + rstd * (
        dhat
        - jnp.mean(dhat, axis=-1, keepdims=True)
        - hat * jnp.mean(dhat * hat, axis=-1, keepdims=True)
    )

    columns = jnp.concatenate([early[: 4 * RANK], late], 0).reshape(10 * RANK, n_dp, cols)
    both = jnp.concatenate(
        [jnp.swapaxes(columns, 0, 1).reshape(n_dp, -1), early[4 * RANK :].reshape(n_dp, -1)], 1
    )
    both = lax.all_to_all(both, "dp", split_axis=0, concat_axis=0, tiled=True)
    both = jnp.einsum("sa,sx->ax", pick.astype(F32), both, precision=PRECISE)
    at = 10 * RANK * cols
    a = both[:, :at].reshape(adapters, 10 * RANK, cols)
    h = both[:, at:].reshape(adapters, 2 * RANK, ff)
    grad_model = jnp.concatenate(
        [a[:, 4 * RANK : 7 * RANK], a[:, : 2 * RANK], a[:, 7 * RANK :], a[:, 2 * RANK : 4 * RANK]], axis=1
    )
    return result[None], grad_tokens[None], grad_model, h


def solution(mesh):
    cols = P(None, ("seq", "dp"))
    rows = P(("seq", "dp"), None)
    deep = P(None, None, ("seq", "dp"))
    act = P("dp", "seq", None)
    return jax.shard_map(
        body,
        mesh=mesh,
        in_specs=(act, act, P("dp"), deep, rows, cols, cols, cols, rows, deep, deep),
        out_specs=(act, act, deep, deep),
        check_vma=False,
    )
```

time: 1370 us -> 739 us (0.54)
  waiting for transfers between devices: 618 us -> 50.2 us
  Pallas kernels: 353 us -> 583 us
  matrix products: 229 us -> 0.85 us
  blocking collectives: 43.7 us -> 4.57 us
  other arithmetic: 29.6 us -> 12.7 us
    all_gather x7 -> x1, waiting for transfers between devices: 509 us -> 46.5 us  [body(): kv = lax.all_gather(jnp.concatenate([ckey.T, cvalue], 0), axes, axis=0)]
    pallas_call x4 -> x9, Pallas kernels: 282 us -> 517 us  [the longest x1 269 us: gather(): pl.pallas_call(functools.partial(gather_kernel, [ORDERS[i % len(ORDERS)]...]
    dot_general x58 -> x2, matrix products: 229 us -> 0.85 us  [the longest x1 0.56 us: body(): both = jnp.einsum('sa,sx->ax', pick.astype(F32), both, precision=PRECISE)]
    reduce_scatter x2 -> x1, waiting for transfers between devices: 103 us -> 0.02 us  [body(): early = lax.psum_scatter(early, 'seq', scatter_dimension=0, tiled=True)[0]]
    all_gather x1 -> x0, blocking collectives: 43.7 us -> none  [body(): vec = lax.all_gather(vectors, axes, axis=1, tiled=True).astype(F32)]
  transfers between devices with their start and end apart: 13 -> 7, of which waited for: 8 -> 3; matrix products, arithmetic and copies ran while one was open for 18% -> 5% of each run, Pallas kernels for 26% -> 65%
where the time goes in v2:
time: 739 us; the launch traced here: 729 us
  Pallas kernels  583 us (79%)
  waiting for transfers between devices  50.2 us (7%)
  local copies, waits for them, and re-layouts  39.5 us (5%)
  starting transfers between devices  22.6 us (3%)
  between operations  15.6 us (2%)
  other arithmetic  12.7 us (2%)
    pallas_call x1, Pallas kernels, gather(): pl.pallas_call(functools.partial(gather_kernel, [ORDERS[i % len(ORDERS)]...  269 us
    pallas_call x8, Pallas kernels, over_tiles(): pl.pallas_call(body, grid=(steps,), in_specs=[made(spec, x.shape) for spe...  248 us
    pallas_call x2, Pallas kernels, pass_states(): pl.pallas_call(functools.partial(pass_kernel, n, groups, back), out_shape...  66 us
    all_gather x1, waiting for transfers between devices, body(): kv = lax.all_gather(jnp.concatenate([ckey.T, cvalue], 0), axes, axis=0)  46.5 us
  transfers between devices with their start and end apart: 7, of which 3 were waited for; matrix products, arithmetic and copies ran while one was open for 5% of the time, Pallas kernels for 65%

profile of v2, /device:TPU:1, one launch (start us, length us, event | category | flops | bytes accessed | tf_op | source)
XLA Modules:
  0.0 728.8 jit_solution(3239399577824743850)
XLA Ops:
  7.2 1.6 copy.49
  8.8 1.5 pad_maximum_fusion
  11.2 0.6 dynamic-slice
  11.8 0.8 dynamic-update-slice
  12.6 3.9 collective-permute-start
  16.6 4.6 all-reduce
  21.3 0.3 reshape.128
  22.1 0.7 reshape.130.refs_5_
  22.9 0.8 concatenate.35.refs_4_
  23.7 1.0 slice_bitcast_fusion.3
  24.7 268.9 %gather_time.1 = (bf16[32,64,2048]{2,1,0:T(8,128)(2,1)}, bf16[32,64,2048]{2,1,0:T(8,128)(2,1)}, bf16[32,64,2048]{2,1,0:T(8,128)(2,1)}, bf16[32,64,2048]{2,1,0:T(...) custom-call(bf16[64,2048]{1,0:T(8,128)(2,1)} %get-tuple-element.149.refs_0_, ...), custom_call_target="tpu_custom_call" | custom-call | tf_op jit(solution)/shard_map/gather_time/pallas_call | solution.py:627
  293.6 1.7 constant_dynamic-slice_fusion
  295.4 0.3 copy.68
  295.7 1.0 copy-done.1
  296.8 1.3 reshape.134
  298.1 1.3 slice.154
  299.6 0.7 convert_bitcast_fusion.vec.norm
  300.3 0.7 fusion.11.valid
  301.0 1.6 copy.44
  302.5 3.2 reshape.135.chosen.up.down
  305.7 0.8 slice.125.down.down_all
  306.6 0.8 slice.127.up
  307.4 0.4 convert_reduce_fusion
  307.8 0.7 fusion.2
  308.5 0.5 fusion
  309.0 2.4 fusion.17
  311.4 25.1 %project.1 = (f32[256,2048]{1,0:T(8,128)}, f32[256,2048]{1,0:T(8,128)}, f32[256,2048]{1,0:T(8,128)}, f32[256,2048]{1,0:T(8,128)}, f32[256,2048]{1,0:T(8,128)}, /...) custom-call(f32[256,2048]{1,0:T(8,128)} %get-tuple-element.138.hat, ...), custom_call_target="tpu_custom_call" | custom-call | tf_op jit(solution)/shard_map/project/pallas_call | solution.py:433
  336.5 43.6 %rec_local.1 = (f32[256,2048]{1,0:T(8,128)}, f32[256,2048]{1,0:T(8,128)}, f32[256,2048]{1,0:T(8,128)}, f32[256,2048]{1,0:T(8,128)}, f32[256,2048]{1,0:T(8,128)},...) custom-call(f32[256,2048]{1,0:T(8,128)} %get-tuple-element.68.rr, ...), custom_call_target="tpu_custom_call" | custom-call | tf_op jit(solution)/shard_map/rec_local/pallas_call | solution.py:433
  380.1 2.6 slice_bitcast_fusion
  382.6 25.3 %pass_on.1.zin = f32[64,2048]{1,0:T(8,128)} custom-call(f32[64,2048]{1,0:T(8,128)} %get-tuple-element.141.move, f32[64,2048]{1,0:T(8,128)} %get-tuple-element.140.add), custom_call_target="tpu_custom_call" | custom-call | tf_op jit(solution)/shard_map/pass_on/pallas_call | solution.py:503
  407.9 23.1 %rec_out.1 = (bf16[256,2048]{1,0:T(8,128)(2,1)}, f32[256,2048]{1,0:T(8,128)}, f32[256,2048]{1,0:T(8,128)}, f32[256,2048]{1,0:T(8,128)}, f32[256,2048]{1,0:T(8,12...) custom-call(f32[64,2048]{1,0:T(8,128)} %pass_on.1.zin, f32[256,2048]{1,0:T(8,128)} %get-tuple-element.68.rr, ...), custom_call_target="tpu_custom_call" | custom-call | tf_op jit(solution)/shard_map/rec_out/pallas_call | solution.py:433
  431.1 0.8 slice.128
  431.9 6.1 collective-permute-start.1
  438.1 1.2 slice.160
  439.4 0.8 slice.130.down_c
  440.2 0.8 slice.132.up_f
  441.0 0.9 copy.61
  442.0 46.5 %all-gather.3.cloned.1.call-done = bf16[16384,2048]{1,0:T(8,128)(2,1)} async-done(((bf16[512,2048]{1,0:T(8,128)(2,1)}), bf16[16384,2048]{1,0:T(8,128)(2,1)}) %all-gather.3.cloned.1.call-update) | async-done | bytes 67108880 | tf_op jit(solution)/shard_map/all_gather | solution.py:855
  488.4 56.4 %channel.1 = (bf16[256,2048]{1,0:T(8,128)(2,1)}, f32[256,2048]{1,0:T(8,128)}, f32[8,2048]{1,0:T(8,128)}, f32[32,32,256]{2,1,0:T(8,128)}, f32[16,2048]{1,0:T(8,128)}, /*index=5*/f32[16,2048]{1,0:T(8,128)}) custom-call(f32[256,2048]{1,0:T(8,128)} %get-tuple-element.81.n2, f32[1,2048]{1,0:T(1,128)} %copy-done.12, f32[18,2048]{1,0:T(8,128)} %convert_bitcast_fusion.vec.norm, ...), custom_call_target="tpu_custom_call" | custom-call | tf_op jit(solution)/shard_map/channel/pallas_call | solution.py:433
  544.8 0.8 slice.134
  545.7 1.3 collective-permute-start.2
  546.9 3.1 collective-permute-done.2.edge
  550.0 0.6 copy-done.13
  550.6 23.8 %back_local.1 = (f32[256,2048]{1,0:T(8,128)}, f32[256,2048]{1,0:T(8,128)}, f32[256,2048]{1,0:T(8,128)}, bf16[256,2048]{1,0:T(8,128)(2,1)}, f32[256,2048]{1,0:T(8...) custom-call(f32[256,2048]{1,0:T(8,128)} %get-tuple-element.84.d_mc, f32[1,2048]{1,0:T(1,128)} %copy-done.13, ...), custom_call_target="tpu_custom_call" | custom-call | tf_op jit(solution)/shard_map/back_local/pallas_call | solution.py:433
  574.5 1.1 pad_maximum_fusion.4
  575.8 1.2 pad_maximum_fusion.1
  577.2 40.7 %pass_back.1.hin = f32[64,2048]{1,0:T(8,128)} custom-call(f32[64,2048]{1,0:T(8,128)} %get-tuple-element.139.move, f32[64,2048]{1,0:T(8,128)} %get-tuple-element.96.add), custom_call_target="tpu_custom_call" | custom-call | tf_op jit(solution)/shard_map/pass_back/pallas_call | solution.py:503
  617.9 47.0 %rec_back.1 = (bf16[256,2048]{1,0:T(8,128)(2,1)}, bf16[256,2048]{1,0:T(8,128)(2,1)}, bf16[256,2048]{1,0:T(8,128)(2,1)}, bf16[256,2048]{1,0:T(8,128)(2,1)}, bf16[256,2048]{1,0:T(8,128)(2,1)}) custom-call(f32[64,2048]{1,0:T(8,128)} %pass_back.1.hin, f32[256,2048]{1,0:T(8,128)} %get-tuple-element.97.dz, f32[256,2048]{1,0:T(8,128)} %get-tuple-element.74.gg, ...), custom_call_target="tpu_custom_call" | custom-call | tf_op jit(solution)/shard_map/rec_back/pallas_call | solution.py:433
  665.0 0.8 slice.140
  665.8 0.9 slice.141
  666.7 10.3 %late.1 = (bf16[3,256,16]{2,1,0:T(8,128)(2,1)}, bf16[3,256,512]{2,1,0:T(8,128)(2,1)}, f32[8,96,256]{2,1,0:T(8,128)}) custom-call(bf16[256,2048]{1,0:T(8,128)(2,1)} %get-tuple-element.104.drr, bf16[256,2048]{1,0:T(8,128)(2,1)} %get-tuple-element.105.dkr, bf16[256,2048]{1,0:T(8,128)(2,1)} %get-tuple-element.106.dvr, bf16[256,2048]{1,0:T(8,128)(2,1)} %get-tuple-element.107.dwl, ...), custom_call_target="tpu_custom_call" | custom-call | tf_op jit(solution)/shard_map/late/pallas_call | solution.py:433
  677.0 18.5 %final.1 = (f32[256,2048]{1,0:T(8,128)}, f32[256,2048]{1,0:T(8,128)}, f32[96,256]{1,0:T(8,128)}) custom-call(bf16[256,2048]{1,0:T(8,128)(2,1)} %get-tuple-element.104.drr, bf16[256,2048]{1,0:T(8,128)(2,1)} %get-tuple-element.105.dkr, bf16[256,2048]{1,0:T(8,128)(2,1)} %get-tuple-element.106.dvr, bf16[2048,2048]{1,0:T(8,128)(2,1)} %bitcast.70, ...), custom_call_target="tpu_custom_call" | custom-call | tf_op jit(solution)/shard_map/final/pallas_call | solution.py:433
  695.6 0.9 pad_maximum_fusion.5
  697.0 0.8 slice.138
  697.9 1.3 collective-permute-start.3
  699.2 3.2 slice.137
  702.4 1.0 copy.53
  703.5 9.9 %all-to-all-start = ((f32[4,1,18432]{2,1,0:T(1,128)}), f32[4,1,18432]{2,1,0:T(1,128)S(1)}, u32[]{:S(2)}, u32[]{:S(2)}) async-start(f32[4,1,18432]{2,1,0:T(1,128)} %copy.53), calls=%async_computation.1 | async-start | bytes 589824 | tf_op jit(solution)/shard_map/all_to_all | solution.py:984
  713.4 3.0 fusion.15
  716.4 1.9 add_bitcast_fusion
  718.2 0.6 all-to-all-done
  718.8 0.6 fusion.7
  719.8 1.1 copy.54
  720.9 0.8 copy.55
  (71 shorter events, 2.7 us)
Async XLA Ops:
  7.2 1.6 copy-start.5
  7.2 481.3 %all-gather.3.cloned.1.call-start = ((), (), s32[]{:S(2)}) async-start(), calls=%async_computation.3 | async-start | bytes 69206016 | tf_op jit(solution)/shard_map/all_gather | solution.py:855
  10.3 0.9 copy-start.15
  10.3 2.3 copy-start
  10.3 10.8 %copy-start.6 = (bf16[8,160,64]{1,2,0:T(8,128)(2,1)S(1)}, bf16[8,160,64]{1,2,0:T(8,128)(2,1)}, u32[]{:S(2)}) copy-start(bf16[8,160,64]{1,2,0:T(8,128)(2,1)} %param.20) | copy-start | bytes 491524
  10.3 11.4 %copy-start.7 = (bf16[8,32,256]{2,1,0:T(8,128)(2,1)S(1)}, bf16[8,32,256]{2,1,0:T(8,128)(2,1)}, u32[]{:S(2)}) copy-start(bf16[8,32,256]{2,1,0:T(8,128)(2,1)} %param.21) | copy-start | bytes 393220
  10.3 12.5 %copy-start.14 = (bf16[18,64]{1,0:T(8,128)(2,1)S(1)}, bf16[18,64]{1,0:T(8,128)(2,1)}, u32[]{:S(2)}) copy-start(bf16[18,64]{1,0:T(8,128)(2,1)} %param.17) | copy-start | bytes 6916
  10.3 12.6 %copy-start.10 = (bf16[64,448]{1,0:T(8,128)(2,1)S(1)}, bf16[64,448]{1,0:T(8,128)(2,1)}, u32[]{:S(2)}) copy-start(bf16[64,448]{1,0:T(8,128)(2,1)} %param.15) | copy-start | bytes 172036
  10.3 12.6 %copy-start.11 = (bf16[448,64]{0,1:T(8,128)(2,1)S(1)}, bf16[448,64]{0,1:T(8,128)(2,1)}, u32[]{:S(2)}) copy-start(bf16[448,64]{0,1:T(8,128)(2,1)} %param.16) | copy-start | bytes 172036
  10.3 13.4 %copy-start.4 = (bf16[4,2048,64]{1,2,0:T(8,128)(2,1)S(1)}, bf16[4,2048,64]{1,2,0:T(8,128)(2,1)}, u32[]{:S(2)}) copy-start(bf16[4,2048,64]{1,2,0:T(8,128)(2,1)} %param.14) | copy-start | bytes 3145732
  10.4 654.6 %reduce-scatter.2.cloned.1.call-start = ((), (), s32[]{:S(2)}) async-start(), calls=%async_computation.2 | async-start | bytes 1769472 | tf_op jit(solution)/shard_map/reduce_scatter | solution.py:940
  12.6 294.8 %collective-permute-start = (bf16[1,2048]{1,0:T(2,128)(2,1)S(1)}, bf16[1,2048]{1,0:T(2,128)(2,1)S(1)}, u32[]{:S(2)}, u32[]{:S(2)}) collective-permute-start(bf16[1,2048]{1,0:T(2,128)(2,1)S(1)} %slice_bitcast_fusion.7), channel_id=1, source_target_pairs={{0,4},{4,8},{8,12},{12,16},{16,20},{20,24},{24,28},{1,5},{5,9},{9,... | collective-permute-start | bytes 12296 | tf_op jit(solution)/shard_map/ppermute | solution.py:830
  295.7 1.0 copy-start.1
  431.9 10.0 %collective-permute-start.1 = (f32[1,2048]{1,0:T(1,128)S(1)}, f32[1,2048]{1,0:T(1,128)S(1)}, u32[]{:S(2)}, u32[]{:S(2)}) collective-permute-start(f32[1,2048]{1,0:T(1,128)S(1)} %slice.128), channel_id=1, source_target_pairs={{0,4},{4,8},{8,12},{12,16},{16,20},{20,24},{24,28},{1,5},{5,9},{9,... | collective-permute-start | bytes 24584 | tf_op jit(solution)/shard_map/ppermute | solution.py:830
  441.9 46.5 %copy-start.12 = (f32[1,2048]{1,0:T(1,128)}, f32[1,2048]{1,0:T(1,128)S(1)}, u32[]{:S(2)}) copy-start(f32[1,2048]{1,0:T(1,128)S(1)} %collective-permute-done.1.edge) | copy-start | bytes 24580
  545.7 4.4 collective-permute-start.2
  550.0 0.6 copy-start.13
  550.6 23.9 %copy-start.8 = (f32[16,2048]{1,0:T(8,128)S(1)}, f32[16,2048]{1,0:T(8,128)}, u32[]{:S(2)}) copy-start(f32[16,2048]{1,0:T(8,128)} %get-tuple-element.94) | copy-start | bytes 393220
  550.6 23.9 %copy-start.9 = (f32[16,2048]{1,0:T(8,128)S(1)}, f32[16,2048]{1,0:T(8,128)}, u32[]{:S(2)}) copy-start(f32[16,2048]{1,0:T(8,128)} %get-tuple-element.92) | copy-start | bytes 393220
  574.5 1.4 copy-start.3
  697.9 15.5 %collective-permute-start.3 = (f32[1,2048]{1,0:T(1,128)S(1)}, f32[1,2048]{1,0:T(1,128)S(1)}, u32[]{:S(2)}, u32[]{:S(2)}) collective-permute-start(f32[1,2048]{1,0:T(1,128)S(1)} %slice.138), channel_id=1, source_target_pairs={{4,0},{8,4},{12,8},{16,12},{20,16},{24,20},{28,24},{5,1},{9,5},{13... | collective-permute-start | bytes 24584 | tf_op jit(solution)/shard_map/ppermute | solution.py:830
  699.2 14.1 %slice-start = ((f32[18,2048]{1,0:T(8,128)}), f32[1,2048]{1,0:T(1,128)S(1)}, s32[]{:S(2)}) async-start(f32[18,2048]{1,0:T(8,128)} %convert_bitcast_fusion.vec.norm), calls=%async_computation.4 | async-start | bytes 16384 | tf_op jit(solution)/shard_map/slice | solution.py:973
  703.5 15.4 %all-to-all-start = ((f32[4,1,18432]{2,1,0:T(1,128)}), f32[4,1,18432]{2,1,0:T(1,128)S(1)}, u32[]{:S(2)}, u32[]{:S(2)}) async-start(f32[4,1,18432]{2,1,0:T(1,128)} %copy.53), calls=%async_computation.1 | async-start | bytes 589824 | tf_op jit(solution)/shard_map/all_to_all | solution.py:984
  713.4 3.0 copy-start.2
Sparse Core Ops, SparseCore 0:
  10.9 477.5 all-gather.2
  577.2 65.1 reduce-scatter.1

commit v3 on v2

v3 whole, which is shorter than its diff:
```python
import functools
import math

import jax
import jax.numpy as jnp
from jax import lax
from jax.experimental import pallas as pl
from jax.experimental.pallas import tpu as pltpu
from jax.sharding import PartitionSpec as P

F32, BF = jnp.float32, jnp.bfloat16
MESH = pl.DeviceIdType.MESH
D = 64
C = 64
PW = 2 * D
DECAY_INNER, RATE_INNER, GATE_INNER, RANK = 96, 96, 256, 16
SCALE = 4.0
NORM_EPS, GROUP_EPS, UNIT_EPS = 1e-05, 0.00064, 1e-06
DECAY_SCALE = math.exp(-0.5)
PRECISE = lax.Precision.HIGHEST
DIMS = {
    "nn": (((1,), (0,)), ((), ())),
    "nt": (((1,), (1,)), ((), ())),
    "tn": (((0,), (0,)), ((), ())),
}


def split(x):
    hi = x.astype(BF)
    return hi, (x - hi.astype(F32)).astype(BF)


def dot1(a, b, m="nn"):
    return lax.dot_general(a.astype(BF), b.astype(BF), DIMS[m], preferred_element_type=F32)


def dot3(a, b, m="nn"):
    ah, al = split(a)
    bh, bl = split(b)
    ka, kb = (0 if m == "tn" else 1), (1 if m == "nt" else 0)
    n = b.shape[1 - kb]
    aa = jnp.concatenate([ah, al], axis=ka)
    bb = jnp.concatenate([jnp.concatenate([bh, bl], axis=1 - kb)] * 2, axis=kb)
    r = lax.dot_general(aa, bb, DIMS[m], preferred_element_type=F32)
    return r[:, :n] + r[:, n:]


dot_inv = dot_a = dot_w = dot_b = dot_g = dot3


def iota(shape, axis):
    return lax.broadcasted_iota(jnp.int32, shape, axis)


def stack2(x):
    lane = iota(x.shape, 1)
    zero = jnp.zeros_like(x)
    return jnp.concatenate([jnp.where(lane < D, x, zero), jnp.where(lane < D, zero, x)], axis=0)


def pack2(x):
    h = x.shape[0] // 2
    return x[:h] + x[h:]


def head_ones():
    r, c = iota((2 * PW, PW), 0) % PW, iota((2 * PW, PW), 1)
    return jnp.where((r // D) == (c // D), 1.0, 0.0).astype(BF)


def headsum(x, ones):
    h, l = split(x)
    return lax.dot_general(
        jnp.concatenate([h, l], axis=1), ones, DIMS["nn"], preferred_element_type=F32
    )


def triangle(upper):
    r, c = iota((C, C), 0), iota((C, C), 1)
    return jnp.where((r <= c) if upper else (r >= c), 1.0, 0.0).astype(BF)


def cums(x, tri):
    h, l = split(x)
    m = (x - h.astype(F32) - l.astype(F32)).astype(BF)
    n = x.shape[1]
    r = lax.dot_general(
        tri, jnp.concatenate([h, l, m], axis=1), DIMS["nn"], preferred_element_type=F32
    )
    return r[:, :n] + r[:, n : 2 * n] + r[:, 2 * n :]


def prelude(kr, wl, al, w0, a0, k_k, k_a, ones):
    s = jax.nn.sigmoid(w0 + wl)
    a = jax.nn.sigmoid(a0 + al)
    kx = kr * k_k
    rn = lax.rsqrt(headsum(kx * kx, ones) + UNIT_EPS)
    return s, -DECAY_SCALE * s, a, rn, kx * rn, kr * (1.0 + (a - 1.0) * k_a)


def grid_ids():
    r, c = iota((PW, PW), 0), iota((PW, PW), 1)
    return r, c, (r // D) == (c // D)


def inverses(many):
    r, c, _ = grid_ids()
    eye = jnp.where(r == c, 1.0, 0.0)
    b = 1
    while b < C:
        level = ((r // (2 * b)) == (c // (2 * b))) & ((r // b) % 2 == 1) & ((c // b) % 2 == 0)
        parts = [jnp.where(level, a, 0.0) for a in many]
        if b == 1:
            xs = [eye + p for p in parts]
        else:
            half = [dot_inv(x, p) for x, p in zip(xs, parts)]
            xs = [x + dot_inv(h, x) for h, x in zip(half, xs)]
        b *= 2
    return xs


def factors(logw, tri):
    run = cums(logw, tri)
    return jnp.exp(run - logw), jnp.exp(run), jnp.exp(-run), jnp.exp(run[C - 1 : C])


def forward_chunks(units, tri):
    rows, cols, same = grid_ids()
    zero = jnp.zeros((PW, PW), F32)
    strict, incl = (rows > cols) & same, (rows >= cols) & same
    fs = [factors(u[5], tri) for u in units]
    p2 = [stack2(u[1] * f[0]) for u, f in zip(units, fs)]
    r2 = [stack2(u[0] * f[1]) for u, f in zip(units, fs)]
    q2 = [stack2(u[2] * f[2]) for u, f in zip(units, fs)]
    k2 = [stack2(u[3] * f[2]) for u, f in zip(units, fs)]
    v2 = [stack2(u[4]) for u in units]
    aa = [
        dot_a(jnp.concatenate([p, r], 0), jnp.concatenate([q, k], 0), "nt")
        for p, r, q, k in zip(p2, r2, q2, k2)
    ]
    apk = [jnp.where(strict, a[:PW, PW:], zero) for a in aa]
    y = [dot_w(a, v) for a, v in zip(apk, v2)]
    xs = inverses([jnp.where(strict, a[:PW, :PW], zero) for a in aa])
    ww = [dot_w(x, jnp.concatenate([p, t], 1)) for x, p, t in zip(xs, p2, y)]
    left = [
        jnp.concatenate(
            [
                jnp.concatenate(
                    [jnp.where(incl, a[PW:, :PW], zero), jnp.where(incl, a[PW:, PW:], zero)], 1
                ),
                jnp.concatenate([(q * f[3]).T, (k * f[3]).T], 1),
            ],
            0,
        )
        for a, q, k, f in zip(aa, q2, k2, fs)
    ]
    right = [
        jnp.concatenate([w, jnp.concatenate([zero, v], 1)], 0) for w, v in zip(ww, v2)
    ]
    big = [dot_b(l, r) for l, r in zip(left, right)]
    move = [
        b[PW:, :PW] + jnp.where(rows == cols, jnp.broadcast_to(f[3], (PW, PW)), zero)
        for b, f in zip(big, fs)
    ]
    return [
        (pack2(r + b[:PW, :PW]), pack2(b[:PW, PW:]), m, b[PW:, PW:], pack2(w[:, :PW]), pack2(w[:, PW:]), x)
        for r, b, m, w, x in zip(r2, big, move, ww, xs)
    ]


def backward_chunks(units, tri, tri_up):
    rows, cols, same = grid_ids()
    zero = jnp.zeros((PW, PW), F32)
    strict, incl = (rows < cols) & same, (rows <= cols) & same
    both = jnp.concatenate([jnp.concatenate([strict, incl], 1)] * 2, 0)
    fs = [factors(t[5], tri) for t in units]
    pe = [t[1] * f[0] for t, f in zip(units, fs)]
    re = [t[0] * f[1] for t, f in zip(units, fs)]
    qe = [t[2] * f[2] for t, f in zip(units, fs)]
    ke = [t[3] * f[2] for t, f in zip(units, fs)]
    g2 = [stack2(t[10]) for t in units]
    qk = [jnp.concatenate([stack2(q), stack2(k)], 0) for q, k in zip(qe, ke)]
    pr = [jnp.concatenate([stack2(p), stack2(r)], 0) for p, r in zip(pe, re)]
    at = [dot_a(a, b, "nt") for a, b in zip(qk, pr)]
    qkh = [
        dot_g(jnp.concatenate([q * f[3], k * f[3]], 0), t[9])
        for q, k, f, t in zip(qe, ke, fs, units)
    ]
    sq = [dot_g(jnp.concatenate([t[7], t[4]], 0), t[9], "nt") for t in units]
    du = [
        dot_g(jnp.where(incl, a[:PW, PW:], zero), g) + stack2(h[:C])
        for a, g, h in zip(at, g2, qkh)
    ]
    dm = [dot_g(t[6], d, "tn") for t, d in zip(units, du)]
    dg = [jnp.concatenate([d, g], 0) for d, g in zip(dm, g2)]
    dv = [
        pack2(
            dot_g(
                jnp.concatenate(
                    [jnp.where(strict, a[PW:, :PW], zero), jnp.where(incl, a[PW:, PW:], zero)], 1
                ),
                d,
            )
        )
        + h[C:]
        for a, d, h in zip(at, dg, qkh)
    ]
    dat = [
        dot_g(jnp.concatenate([stack2(t[7]), stack2(t[4])], 0), d, "nt")
        for t, d in zip(units, dg)
    ]
    dat = [jnp.where(both, d, jnp.zeros_like(d)) for d in dat]
    dpr = [dot_g(d, a, "tn") for d, a in zip(dat, qk)]
    dqk = [dot_g(d, a) for d, a in zip(dat, pr)]
    sp = [dot_g(jnp.concatenate([pack2(d), t[10]], 0), t[8], "nt") for d, t in zip(dm, units)]
    outs = []
    for i, t in enumerate(units):
        eb, el, en, last = fs[i]
        dp, dr = pack2(dpr[i][:PW]) + sp[i][:C], pack2(dpr[i][PW:]) + sp[i][C:]
        dqh, dkh = sq[i][:C], sq[i][C:]
        dq, dk = pack2(dqk[i][:PW]) + dqh * last, pack2(dqk[i][PW:]) + dkh * last
        tail = jnp.sum((qe[i] * dqh + ke[i] * dkh) * last, axis=0, keepdims=True)
        tail = tail + last * jnp.sum((t[8] * t[9]).T, axis=0, keepdims=True)
        gb = pe[i] * dp
        gl = re[i] * dr - qe[i] * dq - ke[i] * dk
        dlogw = cums(gl + gb, tri_up) - gb + tail
        outs.append((dr * el, dp * eb, dq * en, dk * en, dv[i], dlogw))
    return outs


def lanes(ref):
    return [slice(i * PW, (i + 1) * PW) for i in range(ref.shape[-1] // PW)]


def norm_parts(o, ones):
    centre = o - headsum(o, ones) * (1.0 / D)
    rstd = lax.rsqrt(headsum(centre * centre, ones) * (1.0 / D) + GROUP_EPS)
    return centre * rstd, rstd


def hand_on(n, half, back, move, add, here, send, send_sem, recv_sem):
    step, last = pl.program_id(0), pl.num_programs(0) - 1
    s, d = lax.axis_index("seq"), lax.axis_index("dp")
    at = n - 1 - s if back else s
    first, final = at == 0, at == n - 1
    nxt, prv = (s - 1, s + 1) if back else (s + 1, s - 1)
    begins, goes = jnp.logical_not(first), jnp.logical_not(final)
    tile = step - jnp.minimum(at, half)
    now = jnp.logical_and(tile >= 0, tile < half)

    def copy(i, to):
        return pltpu.make_async_remote_copy(
            src_ref=send.at[i],
            dst_ref=here.at[i],
            send_sem=send_sem.at[i],
            recv_sem=recv_sem.at[i],
            device_id=(to, d),
            device_id_type=MESH,
        )

    @pl.when(jnp.logical_and(step == 0, begins))
    def _():
        pl.semaphore_signal(
            pltpu.get_barrier_semaphore(), inc=1, device_id=(prv, d), device_id_type=MESH
        )

    @pl.when(jnp.logical_and(step == 0, goes))
    def _():
        pl.semaphore_wait(pltpu.get_barrier_semaphore(), 1)

    @pl.when(jnp.logical_and(now, first))
    def _():
        here[tile] = jnp.zeros(here.shape[1:], F32)

    @pl.when(jnp.logical_and(now, begins))
    def _():
        copy(tile, prv).wait_recv()

    @pl.when(jnp.logical_and(now, goes))
    def _():
        for ln in lanes(here):
            send[tile, :, ln] = dot3(move[tile, :, ln], stack2(here[tile, :, ln])) + add[tile, :, ln]
        copy(tile, nxt).start()

    @pl.when(jnp.logical_and(step == last, goes))
    def _():
        for i in range(half):
            copy(i, nxt).wait_send()


def hand_scratch(steps):
    return [
        pltpu.VMEM((steps, D, TILE), F32),
        pltpu.VMEM((steps, D, TILE), F32),
        pltpu.SemaphoreType.DMA((steps,)),
        pltpu.SemaphoreType.DMA((steps,)),
    ]


def rec_forward(
    nc, n, half, rr, kr, vr, wl, al, gg, vec, tokens, wo, down, up, norm,
    reff, xs, mt, turned, z_out, o_out, u_out, zs, middle, normed, h_out,
    k_reff, k_oloc, k_w1, k_w2, k_m, k_n, move, add, acc_h, *hand,
):
    step, last = pl.program_id(0), pl.num_programs(0) - 1
    ones = head_ones()

    @pl.when(step < half)
    def _():
        tri = triangle(False)
        units, where = [], []
        for ln in lanes(rr):
            row = lambda i: vec[i : i + 1, ln]
            _, logw, a, _, kk, km = prelude(
                kr[:, ln], wl[:, ln], al[:, ln], row(8), row(9), row(10), row(11), ones
            )
            r, v, q = rr[:, ln], vr[:, ln], kk * a
            for c in range(nc):
                s = slice(c * C, (c + 1) * C)
                units.append((r[s], -kk[s], q[s], km[s], v[s], logw[s]))
                where.append((s, ln))
        done = forward_chunks(units, tri)
        packed = []
        for (s, ln), (e, o, m, z, y1, y2, x) in zip(where, done):
            reff[s, ln] = e
            k_reff[step, s, ln], k_oloc[step, s, ln] = e, o
            k_w1[step, s, ln], k_w2[step, s, ln] = y1, y2
            xs[s, ln] = pack2(x)
            mp = pack2(m)
            k_m[step, s, ln], k_n[step, s, ln], mt[s, ln] = mp, pack2(z), pack2(m.T)
            packed.append(mp)
        for i, ln in enumerate(lanes(rr)):
            tm, tn = stack2(packed[i * nc]), done[i * nc][3]
            for c in range(1, nc):
                t = dot3(packed[i * nc + c], jnp.concatenate([tm, tn], 1))
                tm, tn = stack2(t[:, :PW]), stack2(t[:, PW:]) + done[i * nc + c][3]
            move[step, :, ln], add[step, :, ln], turned[:, ln] = pack2(tm), pack2(tn), pack2(tm.T)

    hand_on(n, half, False, move, add, *hand)

    @pl.when(step >= half)
    def _():
        t = step - half
        here = hand[0]
        state = [here[t, :, ln] for ln in lanes(rr)]
        for c in range(nc):
            s = slice(c * C, (c + 1) * C)
            ts = [
                dot3(jnp.concatenate([k_m[t, s, ln], k_reff[t, s, ln], k_w1[t, s, ln]], 0), stack2(z))
                for z, ln in zip(state, lanes(rr))
            ]
            for i, (y, ln) in enumerate(zip(ts, lanes(rr))):
                zs[s, ln] = state[i]
                o_out[s, ln] = y[C : 2 * C] + k_oloc[t, s, ln]
                u_out[s, ln] = y[2 * C :] + k_w2[t, s, ln]
                state[i] = y[:C] + k_n[t, s, ln]
        for ln in lanes(rr):
            row = lambda i: vec[i : i + 1, ln]
            a = jax.nn.sigmoid(row(9) + al[:, ln])
            km = kr[:, ln] * (1.0 + (a - 1.0) * row(11))
            hat, _ = norm_parts(o_out[:, ln], ones)
            y = hat * row(13) + row(14) + headsum(rr[:, ln] * km * row(12), ones) * vr[:, ln]
            z_out[:, ln] = (y * gg[:, ln]).astype(BF)

        @pl.when(step == half)
        def _():
            acc_h[...] = jnp.zeros_like(acc_h)
            middle[...] = tokens[...].astype(F32)

        acc_h[...] += mm_nt(z_out[...], down[...])
        middle[...] += mm_nt(z_out[...], wo[...])

    @pl.when(step == last)
    def _():
        h_out[...] = acc_h[...].astype(BF)
        x1 = middle[...] + SCALE * mm(h_out[...], up[...])
        middle[...] = x1
        centre = x1 - jnp.mean(x1, axis=-1, keepdims=True)
        rstd = lax.rsqrt(jnp.mean(centre * centre, axis=-1, keepdims=True) + NORM_EPS)
        normed[...] = centre * rstd * norm[15:16, :] + norm[16:17, :]


def rec_backward(
    nc, n, half, d_mc, edge, gy, middle, norm, wo, down, up, h_o, gated, gg, o, rr, kr, vr, wl, al, vec,
    reff, mt, turned, xs, us, zs,
    d_mid, dgg, g_down, g_up, drr, dkr, dvr, dwl, dal,
    low, dh, k_dy, k_do, k_es, move, add, *hand,
):
    step = pl.program_id(0)
    ones = head_ones()

    @pl.when(step == 0)
    def _():
        moved = d_mc[...] * norm[17:18, :]
        size = moved.shape[0]
        up_one = pltpu.roll(moved, size - 1, axis=0)
        up_one = jnp.where(iota(moved.shape, 0) == size - 1, edge[0:1, :], up_one)
        dn = d_mc[...] - moved + up_one
        x1 = middle[...]
        centre = x1 - jnp.mean(x1, axis=-1, keepdims=True)
        rstd = lax.rsqrt(jnp.mean(centre * centre, axis=-1, keepdims=True) + NORM_EPS)
        hat = centre * rstd
        dhat = dn * norm[15:16, :]
        d = rstd * (
            dhat
            - jnp.mean(dhat, axis=-1, keepdims=True)
            - hat * jnp.mean(dhat * hat, axis=-1, keepdims=True)
        )
        d = d + gy[...].astype(F32)
        d_mid[...] = d
        low[...] = d.astype(BF)
        dh[...] = (SCALE * mm_nt(low[...], up[...])).astype(BF)
        g_up[...] = SCALE * mm_tn(h_o[...], low[...])

    @pl.when(step < half)
    def _():
        dz = mm(low[...], wo[...]) + mm(dh[...], down[...])
        g_down[...] = mm_tn(dh[...], gated[...])
        _, _, same = grid_ids()
        for ln in lanes(rr):
            row = lambda i: vec[i : i + 1, ln]
            a = jax.nn.sigmoid(row(9) + al[:, ln])
            km = kr[:, ln] * (1.0 + (a - 1.0) * row(11))
            hat, rstd = norm_parts(o[:, ln], ones)
            y = hat * row(13) + row(14) + headsum(rr[:, ln] * km * row(12), ones) * vr[:, ln]
            dgg[:, ln] = (dz[:, ln] * y).astype(BF)
            dy = dz[:, ln] * gg[:, ln]
            k_dy[step, :, ln] = dy
            dhat = dy * row(13)
            k_do[step, :, ln] = rstd * (
                dhat
                - headsum(dhat, ones) * (1.0 / D)
                - hat * (headsum(dhat * hat, ones) * (1.0 / D))
            )
        es = {}
        for c in range(nc):
            s = slice(c * C, (c + 1) * C)
            for ln in lanes(rr):
                e = pack2(jnp.where(same, dot3(reff[s, ln], k_do[step, s, ln], "tn"), 0.0))
                k_es[step, s, ln] = e
                es[c, ln.start] = e
        state = [es[nc - 1, ln.start] for ln in lanes(rr)]
        for c in reversed(range(nc - 1)):
            s = slice(c * C, (c + 1) * C)
            state = [es[c, ln.start] + dot3(mt[s, ln], stack2(h)) for h, ln in zip(state, lanes(rr))]
        for h, ln in zip(state, lanes(rr)):
            add[step, :, ln] = h
            move[step, :, ln] = turned[:, ln]

    hand_on(n, half, True, move, add, *hand)

    @pl.when(step >= half)
    def _():
        t = step - half
        tri, tri_up = triangle(False), triangle(True)
        units, where, pre = [], [], []
        hs = {}
        for ln in lanes(rr):
            h = hand[0][t, :, ln]
            for c in reversed(range(nc)):
                s = slice(c * C, (c + 1) * C)
                hs[c, ln.start] = stack2(h)
                if c:
                    h = dot3(mt[s, ln], hs[c, ln.start]) + k_es[t, s, ln]
        for ln in lanes(rr):
            row = lambda i: vec[i : i + 1, ln]
            for c in range(nc):
                s = slice(c * C, (c + 1) * C)
                r, v, k = rr[s, ln], vr[s, ln], kr[s, ln]
                sg, logw, a, rn, kk, km = prelude(
                    k, wl[s, ln], al[s, ln], row(8), row(9), row(10), row(11), ones
                )
                units.append(
                    (r, -kk, kk * a, km, v, logw, stack2(xs[s, ln]), us[s, ln], stack2(zs[s, ln]),
                     hs[c, ln.start], k_do[t, s, ln])
                )
                where.append((s, ln))
                pre.append((sg, a, rn, kk, km))
        done = backward_chunks(units, tri, tri_up)
        for (s, ln), (sg, a, rn, kk, km), (dr, dp, dq, dk, dv, dlogw) in zip(where, pre, done):
            row = lambda i: vec[i : i + 1, ln]
            r, v, k = rr[s, ln], vr[s, ln], kr[s, ln]
            dy = k_dy[t, s, ln]
            dv = dv + headsum(r * km * row(12), ones) * dy
            ds = headsum(dy * v, ones) * row(12)
            dr = dr + ds * km
            dkm = dk + ds * r
            dkk = dq * a - dp
            da = dq * kk + dkm * k * row(11)
            dk = dkm * (1.0 + (a - 1.0) * row(11)) + row(10) * rn * (dkk - kk * headsum(dkk * kk, ones))
            drr[s, ln], dkr[s, ln], dvr[s, ln] = dr.astype(BF), dk.astype(BF), dv.astype(BF)
            dwl[s, ln] = (dlogw * (-DECAY_SCALE) * sg * (1.0 - sg)).astype(BF)
            dal[s, ln] = (da * a * (1.0 - a)).astype(BF)


TILE = 2 * PW


def cut(shape):
    lead = tuple(shape[:-1])
    return pl.BlockSpec(lead + (TILE,), lambda i, n=len(lead): (0,) * n + (i,))


def whole(shape):
    return pl.BlockSpec(tuple(shape), lambda i, n=len(shape): (0,) * n, pipeline_mode=pl.Buffered(1))


def result(shape):
    return pl.BlockSpec(tuple(shape), lambda i, n=len(shape): (0,) * n)


def in_turn(half, which):
    def spec(shape):
        lead = tuple(shape[:-1])
        place = {
            "first": lambda i: jnp.minimum(i, half - 1),
            "second": lambda i: jnp.maximum(i - half, 0),
            "both": lambda i: lax.rem(i, half),
        }[which]
        return pl.BlockSpec(lead + (TILE,), lambda i: (0,) * len(lead) + (place(i),))

    return spec


def tile_rows(shape):
    return pl.BlockSpec((TILE, shape[1]), lambda i: (i, 0))


def over_tiles(body, steps, ins, outs, name, scratch=(), **params):
    made = lambda spec, shape: spec if isinstance(spec, pl.BlockSpec) else spec(shape)
    return pl.pallas_call(
        body,
        grid=(steps,),
        in_specs=[made(spec, x.shape) for spec, x in ins],
        out_specs=[made(spec, x.shape) for spec, x in outs],
        out_shape=[x for _, x in outs],
        scratch_shapes=list(scratch),
        compiler_params=pltpu.CompilerParams(vmem_limit_bytes=60 * 1024 * 1024, **params),
        name=name,
    )(*[x for _, x in ins])


ORDERS = ("zxy", "zyx", "xzy", "yzx")
DIRS = "xyuds"


def gather_events(order, z, x, y):
    other = {"x": lambda q: (q, 1 - x, y), "y": lambda q: (q, x, 1 - y), "z": lambda q: (q, x, y)}
    inside = lambda k: None if k == 0 else jnp.logical_and(z + k >= 0, z + k <= 3)
    if order[0] == "z":
        a, b = order[1], order[2]
        events = [(0, (z, x, y), None, None, [a, b, "u", "d", "s"])]
        for k in (1, 2, 3):
            events.append((k, (z - k, x, y), "u", z >= k, ["u", a, b, "s"]))
            events.append((k, (z + k, x, y), "d", z + k <= 3, ["d", a, b, "s"]))
        for k in range(-3, 4):
            events.append((abs(k) + 1, other[a](z + k), a, inside(k), [b, "s"]))
    else:
        a, b = order[0], order[2]
        events = [(0, (z, x, y), None, None, [a, "u", "d", b, "s"])]
        events.append((1, other[a](z), a, None, ["u", "d", b, "s"]))
        for k in (1, 2, 3):
            for late, at in ((0, other["z"]), (1, other[a])):
                events.append((k + late, at(z - k), "u", z >= k, ["u", b, "s"]))
                events.append((k + late, at(z + k), "d", z + k <= 3, ["d", b, "s"]))
    for k in range(-3, 4):
        events.append((abs(k) + 1, other[b](z + k), b, inside(k), ["s"]))
        events.append((abs(k) + 2, (z + k, 1 - x, 1 - y), b, inside(k), ["s"]))
    return events


def maybe(condition, run):
    if condition is None:
        run()
    else:
        pl.when(condition)(run)


class Gathering:
    def __init__(self, orders, steps, shards, whole, send, recv, near):
        self.shards, self.whole, self.send, self.recv, self.near = shards, whole, send, recv, near
        seq, dp = lax.axis_index("seq"), lax.axis_index("dp")
        z, x, y, self.c = seq // 2, seq % 2, dp // 2, dp % 2
        self.z = z
        self.to = {
            "x": (z * 2 + 1 - x, dp),
            "y": (seq, (1 - y) * 2 + self.c),
            "u": (seq + 2, dp),
            "d": (seq - 2, dp),
            "s": (seq, y * 2 + 1 - self.c),
        }
        self.exists = {"u": z < 3, "d": z > 0}
        todo = [
            (steps[t][i] if steps else e[0], t, e)
            for t, o in enumerate(orders)
            for i, e in enumerate(gather_events(o, z, x, y))
        ]
        todo.sort(key=lambda q: q[0])
        self.todo = todo
        self.times = sorted({q[0] for q in todo})

    def enter(self, beside=None, count=0):
        barrier = pltpu.get_barrier_semaphore()
        if beside is not None:
            pl.when(count == 1)(
                lambda: pl.semaphore_signal(barrier, inc=1, device_id=beside, device_id_type=MESH)
            )
        for k in DIRS:
            maybe(
                self.exists.get(k),
                lambda k=k: pl.semaphore_signal(
                    barrier, inc=1, device_id=self.to[k], device_id_type=MESH
                ),
            )
        pl.semaphore_wait(barrier, 3 + (self.z + 2) // 3 + (5 - self.z) // 3 + count)

    def chip(self, b):
        return b[0] * 4 + b[1] * 2 + b[2]

    def copy(self, t, own, b, k):
        slot = self.whole[t].at[self.chip(b) * 2 + self.c]
        return pltpu.make_async_remote_copy(
            src_ref=self.shards[t] if own else slot,
            dst_ref=slot,
            send_sem=self.send.at[DIRS.index(k), t, self.chip(b)],
            recv_sem=self.recv.at[1 if k == "s" else 0, t, self.chip(b)],
            device_id=self.to[k],
            device_id_type=MESH,
        )

    def local(self, t, b):
        return pltpu.make_async_copy(
            self.shards[t], self.whole[t].at[self.chip(b) * 2 + self.c], self.near.at[t]
        )

    def goes(self, event):
        _, b, came, condition, ways = event
        for k in ways:
            both = self.exists.get(k) if condition is None else condition
            if condition is not None and k in self.exists:
                both = jnp.logical_and(condition, self.exists[k])
            yield b, came is None, k, both

    def take(self, time):
        for at, t, event in self.todo:
            if at != time:
                continue
            _, b, came, condition, _ = event
            if came is None:
                self.local(t, b).start()
            else:
                maybe(condition, lambda: self.copy(t, False, b, came).wait_recv())
            for _, own, k, both in self.goes(event):
                maybe(both, lambda: self.copy(t, own, b, k).start())

    def finish(self):
        for t in range(len(self.shards)):
            for i in range(16):
                pltpu.make_async_remote_copy(
                    src_ref=self.shards[t],
                    dst_ref=self.whole[t].at[i * 2 + 1 - self.c],
                    send_sem=self.send.at[4, t, i],
                    recv_sem=self.recv.at[1, t, i],
                    device_id=self.to["s"],
                    device_id_type=MESH,
                ).wait_recv()
        for _, t, event in self.todo:
            for b, own, k, both in self.goes(event):
                maybe(both, lambda: self.copy(t, own, b, k).wait_send())
            if event[2] is None:
                self.local(t, event[1]).wait()


def gather_scratch(n):
    return [
        pltpu.SemaphoreType.DMA((5, n, 16)),
        pltpu.SemaphoreType.DMA((2, n, 16)),
        pltpu.SemaphoreType.DMA((n,)),
    ]


def gather_kernel(orders, *refs):
    n = len(orders)
    g = Gathering(orders, None, refs[:n], refs[n : 2 * n], *refs[2 * n :])
    g.enter()
    for time in g.times:
        g.take(time)
    g.finish()


def gather(shards):
    n_seq, n_dp, n = lax.axis_size("seq"), lax.axis_size("dp"), len(shards)
    if (n_seq, n_dp) != (8, 4):
        return [lax.all_gather(s, ("seq", "dp"), axis=0) for s in shards]
    return pl.pallas_call(
        functools.partial(gather_kernel, [ORDERS[i % len(ORDERS)] for i in range(n)]),
        out_shape=[jax.ShapeDtypeStruct((n_seq * n_dp,) + s.shape, s.dtype) for s in shards],
        in_specs=[pl.BlockSpec(memory_space=pl.ANY)] * n,
        out_specs=[pl.BlockSpec(memory_space=pl.ANY)] * n,
        scratch_shapes=gather_scratch(n),
        compiler_params=pltpu.CompilerParams(collective_id=2, has_side_effects=True),
        name="gather_time",
    )(*shards)


LATE_ORDERS = ("zxy", "yzx")
LATE_STEPS = (
    (0, 2, 2, 4, 4, 7, 7, 11, 9, 4, 2, 5, 9, 11, 9, 13, 7, 11, 4, 8, 2, 6, 5, 9, 7, 11, 9, 13),
    (0, 3, 3, 3, 5, 5, 6, 6, 8, 8, 9, 9, 11, 11, 13, 14, 13, 14, 7, 11, 3, 6, 8, 12, 13, 14, 13, 14),
)


def channel_kernel(
    late, n2, edge, norm, gy, middle, down_c, up_f, kv, hidden, *refs,
):
    if late:
        key_shard, value_shard, hidden_late, *refs = refs
    out, dmc, first, g_hidden, g_up_f, g_down_c, *refs = refs
    if late:
        g_late, d_edge, *refs = refs
    mc, mct, gyt, ffo, h_c, dh_f, acc_f, acc_c, *refs = refs
    step, last = pl.program_id(0), pl.num_programs(0) - 1
    per, ff = kv.shape[0], kv.shape[1] // 2
    if late:
        key_late, value_late, mine, came, edge_sem, *sems = refs
        g = Gathering(LATE_ORDERS, LATE_STEPS, (key_shard, value_shard), (key_late, value_late), *sems)
        seq, dp = lax.axis_index("seq"), lax.axis_index("dp")
        x, z = seq % 2, seq // 2
        beside = seq + 2 * x - 1
        count = (1 - x) * ((z + 2) // 3) + x * ((5 - z) // 3)
        starts, ends = seq == 0, seq == 7

        def edges(i, to):
            return pltpu.make_async_remote_copy(
                src_ref=mine.at[i],
                dst_ref=came.at[i],
                send_sem=edge_sem.at[0, i],
                recv_sem=edge_sem.at[1, i],
                device_id=(to, dp),
                device_id_type=MESH,
            )

        def trade(i, has_from, has_to, shift):
            pl.when(has_to)(lambda: edges(i, seq + shift).start())
            pl.when(has_from)(lambda: edges(i, seq - shift).wait_recv())
            pl.when(has_to)(lambda: edges(i, seq + shift).wait_send())

        @pl.when(step == 0)
        def _():
            came[...] = jnp.zeros_like(came)
            g.enter((beside, dp), count)
            size = n2.shape[0]
            mine[0] = n2[size - 8 :, :]

        for time in g.times:

            @pl.when(step == time)
            def _():
                g.take(time)

        @pl.when(step == 0)
        def _():
            trade(0, jnp.logical_not(starts), jnp.logical_not(ends), 1)

    @pl.when(step == 0)
    def _():
        x = n2[...]
        row = came[0, 7:8, :] if late else edge[...]
        before = jnp.where(iota(x.shape, 0) == 0, row, pltpu.roll(x, 1, axis=0))
        m = x + (before - x) * norm[17:18, :]
        mc[...] = m.astype(BF)
        mct[...] = m.T.astype(BF)
        gyt[...] = gy[...].astype(F32).T.astype(BF)
        h_c[...] = mm_nt(down_c[...], mc[...]).astype(BF)
        dh_f[...] = (SCALE * mm_nt(up_f[...], gy[...])).astype(BF)
        acc_f[...] = jnp.zeros_like(acc_f)
        acc_c[...] = jnp.zeros_like(acc_c)
        ffo[...] = jnp.zeros_like(ffo)
        dmc[...] = jnp.zeros_like(dmc)

    def units(key, value, smalls):
        pre, dsq = mm(key, mct[...]), mm(value, gyt[...])
        rows = key.shape[0] // len(smalls)
        hqs, dps, grads = [], [], []
        for b, small in enumerate(smalls):
            s = slice(b * rows, (b + 1) * rows)
            down_f, up_c = small[:RANK], small[RANK:]
            active = jnp.maximum(pre[s] + SCALE * mm_tn(up_c, h_c[...]), 0.0)
            hq = (active * active).astype(BF)
            dpre = ((dsq[s] + mm_tn(down_f, dh_f[...])) * (2.0 * active)).astype(BF)
            grads.append((mm_nt(dh_f[...], hq), SCALE * mm_nt(h_c[...], dpre)))
            acc_f[...] += mm(down_f, hq)
            acc_c[...] += mm(up_c, dpre)
            hqs.append(hq)
            dps.append(dpre)
        ffo[...] += mm_tn(jnp.concatenate(hqs, 0), value)
        dmc[...] += mm_tn(jnp.concatenate(dps, 0), key)
        return grads

    @pl.when(step < last + (0 if late else 1))
    def _():
        key = jnp.concatenate([kv[b, :ff] for b in range(per)], 0)
        value = jnp.concatenate([kv[b, ff:] for b in range(per)], 0)
        grads = units(key, value, [hidden[b, :, :ff] for b in range(per)])
        for b, (low, high) in enumerate(grads):
            if late:
                g_hidden[b] = jnp.zeros(g_hidden.shape[1:], F32)
            g_hidden[b, :RANK, :ff], g_hidden[b, RANK:, :ff] = low, high

    @pl.when(step == last)
    def _():
        if late:
            g.finish()
            flat = lambda ref: ref[...].reshape(-1, ref.shape[-1])
            ((low, high),) = units(flat(key_late), flat(value_late), [hidden_late[...]])
            part = low.shape[1] // 8
            for p in range(8):
                at = slice(p * part, (p + 1) * part)
                g_late[p, :, :part], g_late[p, :, part:] = low[:, at], high[:, at]
        h_f = acc_f[...].astype(BF)
        out[...] = (middle[...] + ffo[...] + SCALE * mm_tn(h_f, up_f[...])).astype(BF)
        g_up_f[...] = SCALE * mm(h_f, gy[...])
        dh_c = (SCALE * acc_c[...]).astype(BF)
        d = dmc[...] + mm_tn(dh_c, down_c[...])
        dmc[...] = d
        first[...] = d[:8] * norm[17:18, :]
        if late:
            mine[1] = first[...]
            trade(1, jnp.logical_not(ends), jnp.logical_not(starts), -1)
            d_edge[...] = came[1]
        g_down_c[...] = mm(dh_c, mc[...])


def late_units(n_seq, n_dp, ff):
    return ff // 8 if (n_seq, n_dp) == (8, 4) and ff % 128 == 0 else 0


def channel(n2, edge, norm, gy, middle, down_c, up_f, kv, hidden, key_shard, value_shard):
    n, both, width = kv.shape
    ff, length, late = hidden.shape[2], n2.shape[0], key_shard.shape[0]
    per = max(1, min(n, 512 // ff))
    steps = n // per
    block = lambda shape: pl.BlockSpec(
        (per,) + tuple(shape[1:]), lambda i: (jnp.minimum(i, steps - 1), 0, 0)
    )
    far = lambda shape: pl.BlockSpec(memory_space=pl.ANY)
    shape = jax.ShapeDtypeStruct
    rank = shape((RANK, width), F32)
    ins = [(whole, a) for a in (n2, edge, norm, gy, middle, down_c, up_f)] + [(block, kv), (block, hidden)]
    outs = [
        (result, shape((length, width), BF)),
        (result, shape((length, width), F32)),
        (result, shape((8, width), F32)),
        (block, shape((n, 2 * RANK, ff), F32)),
        (result, rank),
        (result, rank),
    ]
    scratch = [
        pltpu.VMEM((length, width), BF),
        pltpu.VMEM((width, length), BF),
        pltpu.VMEM((width, length), BF),
        pltpu.VMEM((length, width), F32),
        pltpu.VMEM((RANK, length), BF),
        pltpu.VMEM((RANK, length), BF),
        pltpu.VMEM((RANK, length), F32),
        pltpu.VMEM((RANK, length), F32),
    ]
    params = {}
    if late:
        hidden_late = jnp.swapaxes(hidden[:, :, ff - late :], 0, 1).reshape(2 * RANK, n * late)
        ins += [(far, key_shard), (far, value_shard), (whole, hidden_late)]
        outs += [(result, shape((8, RANK, 2 * n * late // 8), F32)), (result, shape((8, width), F32))]
        scratch += [pltpu.VMEM((n, late, width), BF)] * 2
        scratch += [pltpu.VMEM((2, 8, width), F32)] * 2 + [pltpu.SemaphoreType.DMA((2, 2))]
        scratch += gather_scratch(2)
        params = dict(collective_id=4, has_side_effects=True)
    return over_tiles(
        functools.partial(channel_kernel, late), steps + (1 if late else 0), ins, outs, "channel", scratch, **params
    )


HALF = 512


def branch_masks(shape):
    lane = iota(shape, 1)
    lo, hi = DECAY_INNER, DECAY_INNER + RATE_INNER
    return lane < lo, (lane >= lo) & (lane < hi), (lane >= hi) & (lane < hi + GATE_INNER)


def project_kernel(
    hat, hat_prev, valid, vec, first, chosen, second, w_r, w_k, w_v, up,
    rr, kr, vr, wl, al, gg, m_r, m_k, m_v, hs, act, act_low,
):
    @pl.when(pl.program_id(0) == 0)
    def _():
        n1 = hat[...] * vec[0:1, :] + vec[1:2, :]
        change = (hat_prev[...] * vec[0:1, :] + vec[1:2, :]) * valid[...] - n1
        mixed = lambda i: (n1 + change * vec[2 + i : 3 + i, :]).astype(BF)
        m_r[...], m_k[...], m_v[...] = mixed(0), mixed(2), mixed(3)
        for i, m in enumerate((m_r, m_k, m_v)):
            hs[i] = mm_nt(m[...], chosen[i * RANK : (i + 1) * RANK, :]).astype(BF)
        t_w = mm(mixed(1), first[...])
        t_a = mm(mixed(4), first[...])
        t_g = mm(mixed(5), first[...])
        is_w, is_a, is_g = branch_masks(t_w.shape)
        zero = jnp.zeros_like(t_w)
        t_w = jnp.where(is_w, jnp.tanh(t_w), zero)
        t_a = jnp.where(is_a, t_a, zero)
        t_g = jnp.where(is_g, jax.nn.sigmoid(t_g), zero)
        act[...] = t_w + t_a + t_g
        act_low[0], act_low[1], act_low[2] = t_w.astype(BF), t_a.astype(BF), t_g.astype(BF)

    for i, (m, w, out) in enumerate(((m_r, w_r, rr), (m_k, w_k, kr), (m_v, w_v, vr))):
        out[...] = mm_nt(m[...], w[...]) + SCALE * mm(hs[i], up[(5 + i) * RANK : (6 + i) * RANK, :])
    for i, out in enumerate((wl, al, gg)):
        out[...] = mm_nt(act_low[i], second[...])


def final_kernel(
    n, drr, dkr, dvr, dwl, dal, dgg, m_r, m_k, m_v, hs, act, chosen, second, down_o, up_o, hat, rstd, d_mid, vecs,
    w_r, w_k, w_v, down, first, vec,
    grad, summed, stay, go, dhs, d_act, parts, here, came, send_sem, recv_sem, edge_sem,
):
    step, last = pl.program_id(0), pl.num_programs(0) - 1
    me, dp = lax.axis_index("seq"), lax.axis_index("dp")

    def copy(k):
        peer = lax.rem(me + k, n)
        return pltpu.make_async_remote_copy(
            src_ref=parts.at[peer],
            dst_ref=here.at[k - 1],
            send_sem=send_sem.at[k - 1],
            recv_sem=recv_sem.at[k - 1],
            device_id=(peer, dp),
            device_id_type=MESH,
        )

    def edge(to):
        return pltpu.make_async_remote_copy(
            src_ref=go.at[0:8],
            dst_ref=came,
            send_sem=edge_sem.at[0],
            recv_sem=edge_sem.at[1],
            device_id=(to, dp),
            device_id_type=MESH,
        )

    @pl.when(step == 0)
    def _():
        came[...] = jnp.zeros_like(came)
        barrier = pltpu.get_barrier_semaphore()
        for k in range(1, n):
            pl.semaphore_signal(
                barrier, inc=1, device_id=(lax.rem(me + k, n), dp), device_id_type=MESH
            )
        rows = [None] * 6 + [down_o[...], up_o[...]]
        for i, (d, m) in enumerate(((drr, m_r), (dkr, m_k), (dvr, m_v))):
            dh = (SCALE * mm_nt(d[...], chosen[(5 + i) * RANK : (6 + i) * RANK, :])).astype(BF)
            dhs[i] = dh
            rows[i], rows[3 + i] = mm_tn(dh, m[...]), SCALE * mm_tn(hs[i], d[...])
        wide = parts.shape[2]
        for i, r in enumerate(rows):
            for p in range(n):
                parts[p, i * RANK : (i + 1) * RANK, :] = r[:, p * wide : (p + 1) * wide].astype(BF)
        pl.semaphore_wait(barrier, n - 1)
        for k in range(1, n):
            copy(k).start()
        is_w, is_a, is_g = branch_masks(act.shape)
        a = act[...]
        zero = jnp.zeros_like(a)
        d_act[0] = jnp.where(is_w, mm(dwl[...], second[...]) * (1.0 - a * a), zero).astype(BF)
        d_act[1] = jnp.where(is_a, mm(dal[...], second[...]), zero).astype(BF)
        d_act[2] = jnp.where(is_g, mm(dgg[...], second[...]) * a * (1.0 - a), zero).astype(BF)

    total, moved = None, None
    for i, (d, w, at) in enumerate(((drr, w_r, 2), (dkr, w_k, 4), (dvr, w_v, 5))):
        g = mm(d[...], w[...]) + mm(dhs[i], down[i * RANK : (i + 1) * RANK, :])
        move = g * vec[at : at + 1, :]
        total, moved = (g, move) if total is None else (total + g, moved + move)
    for i, at in enumerate((3, 6, 7)):
        g = mm_nt(d_act[i], first[...])
        total, moved = total + g, moved + g * vec[at : at + 1, :]
    tile = pl.ds(pl.multiple_of(step * TILE, TILE), TILE)
    stay[:, tile] = total - moved
    go[:, tile] = moved

    @pl.when(step == last)
    def _():
        pl.when(me > 0)(lambda: edge(me - 1).start())
        for k in range(1, n):
            copy(k).wait()
        t = parts[me].astype(F32)
        for k in range(1, n):
            t = t + here[k - 1].astype(F32)
        summed[...] = t
        pl.when(me < n - 1)(lambda: edge(me + 1).wait_recv())
        size = go.shape[0]
        g = pltpu.roll(go[...], size - 1, axis=0)
        g = stay[...] + jnp.where(iota(g.shape, 0) == size - 1, came[0:1, :], g)
        dhat = g * vecs[0:1, :]
        grad[...] = d_mid[...] + rstd[...] * (
            dhat
            - jnp.mean(dhat, axis=-1, keepdims=True)
            - hat[...] * jnp.mean(dhat * hat[...], axis=-1, keepdims=True)
        )
        pl.when(me > 0)(lambda: edge(me - 1).wait_send())


def shifted(block, axis, distance):
    devices = range(lax.axis_size(axis))
    route = [(i - distance, i) for i in devices if i - distance in devices]
    return lax.ppermute(block, axis, route)


def mm(a, b):
    return lax.dot_general(a, b, DIMS["nn"], preferred_element_type=F32)


def mm_nt(a, b):
    return lax.dot_general(a, b, DIMS["nt"], preferred_element_type=F32)


def mm_tn(a, b):
    return lax.dot_general(a, b, DIMS["tn"], preferred_element_type=F32)


def body(tokens, output_gradient, index, proj, first, second, vectors, ckey, cvalue, model_rows, hidden_rows):
    axes = ("seq", "dp")
    n_seq, n_dp = lax.axis_size("seq"), lax.axis_size("dp")
    n = n_seq * n_dp
    tokens, gy = tokens[0], output_gradient[0]
    length, width = tokens.shape
    nc, tiles = length // C, width // TILE
    adapters, kinds, cols = model_rows.shape
    ff, inner, nvec = ckey.shape[1], first.shape[1], vectors.shape[0]

    key_shard, soon = ckey.T, ff - late_units(n_seq, n_dp, ff)
    kv = lax.all_gather(jnp.concatenate([key_shard[:soon], cvalue[:soon]], 0), axes, axis=0)

    index_all = lax.all_gather(index, "dp", axis=0, tiled=True)
    pick = index_all[:, None] == jnp.arange(adapters, dtype=jnp.int32)[None, :]
    few = jnp.concatenate([model_rows.reshape(adapters, -1), hidden_rows.reshape(adapters, -1)], 1)
    few = jnp.einsum("sa,ax->sx", pick.astype(BF), few, preferred_element_type=F32).astype(BF)
    pad = lambda k: jnp.zeros((cols, k), BF)
    misc = jnp.concatenate(
        [first, pad(HALF - inner), second.T, vectors.T, pad(HALF - inner - nvec)], axis=1
    )
    turned = jnp.swapaxes(proj, 1, 2)

    wide = tokens.astype(F32)
    ahead = shifted(tokens[-1:], "seq", 1).astype(F32)
    rows = jnp.concatenate([ahead, wide], 0)
    centre = rows - jnp.mean(rows, axis=-1, keepdims=True)
    rstd = lax.rsqrt(jnp.mean(centre * centre, axis=-1, keepdims=True) + NORM_EPS)
    hat = centre * rstd
    start = (jnp.arange(length)[:, None] == 0) & (lax.axis_index("seq") == 0)
    valid = jnp.where(start, 0.0, 1.0).astype(F32)
    hat_prev, hat, rstd = hat[:-1], hat[1:], rstd[1:]

    *mats, misc, few_all = gather([turned[0], turned[1], turned[2], turned[3], misc, few.reshape(-1, 128)])
    mats = [m.reshape(width, width) for m in mats]
    misc = misc.reshape(width, -1)
    vec = misc[:, HALF + inner : HALF + inner + nvec].T.astype(F32)
    own = lax.dynamic_index_in_dim(few_all.reshape(n, n_dp, -1, 128), lax.axis_index("dp"), 1, False)
    own = own.reshape(n, -1)
    chosen = own[:, : kinds * cols].reshape(n, kinds, cols).transpose(1, 0, 2).reshape(kinds, width)
    hidden = own[:, kinds * cols :].reshape(n, 2 * RANK, ff)
    down = lambda i: chosen[i * RANK : (i + 1) * RANK]
    up = lambda i: chosen[(5 + i) * RANK : (6 + i) * RANK]

    shape = jax.ShapeDtypeStruct
    full, low = shape((length, width), F32), shape((length, width), BF)
    small, rank = shape((D, width), F32), shape((RANK, width), F32)
    firsts = pl.BlockSpec((width, HALF), lambda i: (0, 0))
    seconds = pl.BlockSpec((width, HALF), lambda i: (0, 1))
    first_rows = pl.BlockSpec((TILE, HALF), lambda i: (i, 0))
    second_rows = pl.BlockSpec((TILE, HALF), lambda i: (i, 1))
    rr, kr, vr, wl, al, gg, m_r, m_k, m_v, hs, act = over_tiles(
        project_kernel, tiles,
        [
            (whole, hat), (whole, hat_prev), (whole, valid), (whole, vec), (firsts, misc), (whole, chosen),
            (second_rows, misc), (tile_rows, mats[0]), (tile_rows, mats[1]), (tile_rows, mats[2]), (cut, chosen),
        ],
        [(cut, full)] * 6
        + [(result, low)] * 3
        + [(result, shape((3, length, RANK), BF)), (result, shape((length, HALF), F32))],
        "project",
        [pltpu.VMEM((3, length, HALF), BF)],
    )
    one, two, each = in_turn(tiles, "first"), in_turn(tiles, "second"), in_turn(tiles, "both")
    keep = pltpu.VMEM((tiles, length, TILE), F32)
    keep_small = pltpu.VMEM((tiles, D, TILE), F32)
    reff, xs, mt, turned, gated, o, us, zs, middle, n2, h_o = over_tiles(
        functools.partial(rec_forward, nc, n_seq, tiles), 2 * tiles,
        [
            (each, rr), (each, kr), (each, vr), (one, wl), (each, al), (two, gg), (each, vec),
            (whole, tokens), (two, mats[3]), (two, down(3)), (whole, up(3)), (whole, vec),
        ],
        [(one, full), (one, full), (one, full), (one, small), (two, low), (two, full), (two, full), (two, full)]
        + [(result, full), (result, full), (result, shape((length, RANK), BF))],
        "rec_forward",
        [keep] * 6 + [keep_small] * 2 + [pltpu.VMEM((length, RANK), F32)] + hand_scratch(tiles),
        collective_id=0, has_side_effects=True,
    )
    soon_only = soon == ff
    row = shifted(n2[-1:], "seq", 1) if soon_only else n2[-1:]
    out, d_mc, moved, g_hidden, up_f, down_c, *more = channel(
        n2, row, vec, gy, middle, down(4), up(4), kv, hidden,
        key_shard[soon:], cvalue[soon:],
    )
    wide = n_dp * cols
    by_piece = lambda rows: jnp.swapaxes(rows.reshape(-1, n_seq, wide), 0, 1)
    parts = [by_piece(jnp.concatenate([down_c, up_f], 0)), g_hidden.reshape(n_seq, -1, wide)]
    if soon_only:
        edge = jnp.broadcast_to(shifted(moved[:1], "seq", -1), (8, width))
    else:
        g_late, edge = more
        parts.append(g_late)
    early, edge = lax.optimization_barrier((jnp.concatenate(parts, 1), edge))
    early = lax.psum_scatter(early, "seq", scatter_dimension=0, tiled=True)[0]
    d_mid, dgg, down_o, up_o, drr, dkr, dvr, dwl, dal = over_tiles(
        functools.partial(rec_backward, nc, n_seq, tiles), 2 * tiles,
        [
            (whole, d_mc), (whole, edge), (whole, gy), (whole, middle), (whole, vec), (one, mats[3]),
            (one, down(3)), (whole, up(3)), (whole, h_o), (one, gated), (one, gg), (one, o),
            (each, rr), (each, kr), (each, vr), (two, wl), (each, al), (each, vec),
            (one, reff), (each, mt), (one, turned), (two, xs), (two, us), (two, zs),
        ],
        [(result, full), (one, low), (one, rank), (result, rank)] + [(two, low)] * 5,
        "rec_backward",
        [pltpu.VMEM((length, width), BF), pltpu.VMEM((length, RANK), BF)]
        + [keep] * 3 + [keep_small] * 2 + hand_scratch(tiles),
        collective_id=1, has_side_effects=True,
    )
    early, drr = lax.optimization_barrier((early, drr))
    grad_tokens, late = over_tiles(
        functools.partial(final_kernel, n_seq), tiles,
        [(whole, a) for a in (drr, dkr, dvr, dwl, dal, dgg, m_r, m_k, m_v, hs, act, chosen)]
        + [(pl.BlockSpec((width, HALF), lambda i: (0, 1), pipeline_mode=pl.Buffered(1)), misc)]
        + [(whole, a) for a in (down_o, up_o, hat, rstd, d_mid, vec)]
        + [(cut, mats[0]), (cut, mats[1]), (cut, mats[2]), (cut, chosen), (first_rows, misc), (cut, vec)],
        [(result, full), (result, shape((8 * RANK, wide), F32))], "final",
        [
            pltpu.VMEM((length, width), F32),
            pltpu.VMEM((length, width), F32),
            pltpu.VMEM((3, length, RANK), BF),
            pltpu.VMEM((3, length, HALF), BF),
            pltpu.VMEM((n_seq, 8 * RANK, wide), BF),
            pltpu.VMEM((n_seq - 1, 8 * RANK, wide), BF),
            pltpu.VMEM((8, width), F32),
            pltpu.SemaphoreType.DMA((n_seq - 1,)),
            pltpu.SemaphoreType.DMA((n_seq - 1,)),
            pltpu.SemaphoreType.DMA((2,)),
        ],
        collective_id=3, has_side_effects=True,
    )

    mine = early[2 * RANK : 2 * RANK + 2 * RANK * ff // cols].reshape(n_dp, 2 * RANK, ff)
    if not soon_only:
        tail = early[2 * RANK + 2 * RANK * ff // cols :].reshape(RANK, 2, n_dp, ff - soon)
        tail = tail.transpose(2, 1, 0, 3).reshape(n_dp, 2 * RANK, ff - soon)
        mine = jnp.concatenate([mine[:, :, :soon], tail], 2)
    columns = jnp.concatenate([early[: 2 * RANK], late], 0).reshape(10 * RANK, n_dp, cols)
    both = jnp.concatenate(
        [jnp.swapaxes(columns, 0, 1).reshape(n_dp, -1), mine.reshape(n_dp, -1)], 1
    )
    both = lax.all_to_all(both, "dp", split_axis=0, concat_axis=0, tiled=True)
    both = jnp.einsum("sa,sx->ax", pick.astype(F32), both, precision=PRECISE)
    at = 10 * RANK * cols
    a = both[:, :at].reshape(adapters, 10 * RANK, cols)
    h = both[:, at:].reshape(adapters, 2 * RANK, ff)
    block = lambda i, k: a[:, i * RANK : (i + k) * RANK]
    grad_model = jnp.concatenate(
        [block(2, 3), block(8, 1), block(0, 1), block(5, 3), block(9, 1), block(1, 1)], axis=1
    )
    return out[None], grad_tokens[None], grad_model, h


def solution(mesh):
    cols = P(None, ("seq", "dp"))
    rows = P(("seq", "dp"), None)
    deep = P(None, None, ("seq", "dp"))
    act = P("dp", "seq", None)
    return jax.shard_map(
        body,
        mesh=mesh,
        in_specs=(act, act, P("dp"), deep, rows, cols, cols, cols, rows, deep, deep),
        out_specs=(act, act, deep, deep),
        check_vma=False,
    )
```

time: 739 us -> 692 us (0.936)
  waiting for transfers between devices: 50.2 us -> 24.2 us
  Pallas kernels: 583 us -> 569 us
  starting transfers between devices: 22.6 us -> 13.5 us
  local copies, waits for them, and re-layouts: 39.5 us -> 47.8 us
    pallas_call x2 -> x0, Pallas kernels: 66 us -> none  [pass_states(): pl.pallas_call(functools.partial(pass_kernel, n, groups, back), out_shape...]
    pallas_call x8 -> x5, Pallas kernels: 248 us -> 303 us  [over_tiles(): pl.pallas_call(body, grid=(steps,), in_specs=[made(spec, x.shape) for spe...]
    all_gather x1, waiting for transfers between devices: 46.5 us -> 18.6 us  [body(): lax.all_gather(jnp.concatenate([key_shard[:soon], cvalue[:soon]], 0), axe...]
    ppermute x4 -> x1, starting transfers between devices: 12.6 us -> 3.94 us  [shifted(): return lax.ppermute(block, axis, route)]
  transfers between devices with their start and end apart: 7 -> 4, of which waited for: 3 -> 2; matrix products, arithmetic and copies ran while one was open for 5% -> 5% of each run, Pallas kernels for 65% -> 65%
where the time goes in v3:
time: 692 us; the launch traced here: 684 us
  Pallas kernels  569 us (82%)
  local copies, waits for them, and re-layouts  47.8 us (7%)
  waiting for transfers between devices  24.2 us (3%)
  between operations  15.6 us (2%)
  starting transfers between devices  13.5 us (2%)
  other arithmetic  8.94 us (1%)
    pallas_call x5, Pallas kernels, over_tiles(): pl.pallas_call(body, grid=(steps,), in_specs=[made(spec, x.shape) for spe...  303 us
    pallas_call x1, Pallas kernels, gather(): pl.pallas_call(functools.partial(gather_kernel, [ORDERS[i % len(ORDERS)]...  266 us
    all_gather x1, waiting for transfers between devices, body(): lax.all_gather(jnp.concatenate([key_shard[:soon], cvalue[:soon]], 0), axe...  18.6 us
  transfers between devices with their start and end apart: 4, of which 2 were waited for; matrix products, arithmetic and copies ran while one was open for 5% of the time, Pallas kernels for 65%

profile of v3, /device:TPU:1, one launch (start us, length us, event | category | flops | bytes accessed | tf_op | source)
XLA Modules:
  0.0 684.1 jit_solution(8204917823418116815)
XLA Ops:
  7.2 1.5 copy.55
  8.8 1.1 slice-done
  9.9 1.4 pad_maximum_fusion
  12.1 0.6 dynamic-slice
  12.6 0.8 dynamic-update-slice
  13.4 3.9 collective-permute-start
  17.4 4.6 all-reduce
  21.9 0.2 copy.48
  22.2 0.3 reshape.131
  22.6 0.3 convolution_convert_fusion
  22.9 0.7 reshape.133.refs_5_
  23.8 0.8 concatenate.35.refs_4_
  24.5 2.2 slice_bitcast_fusion.1
  26.7 266.0 %gather_time.1 = (bf16[32,64,2048]{2,1,0:T(8,128)(2,1)}, bf16[32,64,2048]{2,1,0:T(8,128)(2,1)}, bf16[32,64,2048]{2,1,0:T(8,128)(2,1)}, bf16[32,64,2048]{2,1,0:T(...) custom-call(bf16[64,2048]{1,0:T(8,128)(2,1)} %get-tuple-element.125.refs_0_, ...), custom_call_target="tpu_custom_call" | custom-call | tf_op jit(solution)/shard_map/gather_time/pallas_call | solution.py:695
  292.8 1.4 constant_dynamic-slice_fusion
  294.1 0.3 copy.78
  294.4 0.9 slice.165
  295.3 0.8 slice.171
  296.2 2.5 reshape.137
  298.7 2.0 slice.164
  300.8 2.1 copy.66
  302.8 1.2 copy.70
  304.0 0.9 slice_bitcast_fusion
  304.9 0.7 fusion.15
  305.7 0.7 convert_bitcast_fusion.vec.norm.vecs
  306.4 0.7 fusion.10.valid
  307.0 1.6 copy.50
  308.6 0.7 slice.172.refs_0_
  309.2 0.6 slice.142.refs_1_
  309.9 3.0 reshape.138.chosen.up.down
  312.9 0.8 slice.130.down
  313.7 0.8 slice.132.up
  314.6 0.8 slice.135.down_c
  315.4 0.8 slice.137.up_f
  316.3 0.9 reshape.144.refs_2_
  317.2 0.4 convert_reduce_fusion
  317.6 0.7 fusion.2
  318.3 0.5 fusion
  318.9 2.4 fusion.14
  321.3 24.9 %project.1 = (f32[256,2048]{1,0:T(8,128)}, f32[256,2048]{1,0:T(8,128)}, f32[256,2048]{1,0:T(8,128)}, f32[256,2048]{1,0:T(8,128)}, f32[256,2048]{1,0:T(8,128)}, /...) custom-call(f32[256,2048]{1,0:T(8,128)} %get-tuple-element.117.hat, ...), custom_call_target="tpu_custom_call" | custom-call | tf_op jit(solution)/shard_map/project/pallas_call | solution.py:531
  346.1 66.0 %rec_forward.1 = (f32[256,2048]{1,0:T(8,128)}, f32[256,2048]{1,0:T(8,128)}, f32[256,2048]{1,0:T(8,128)}, f32[64,2048]{1,0:T(8,128)}, bf16[256,2048]{1,0:T(8,128)...) custom-call(f32[256,2048]{1,0:T(8,128)} %get-tuple-element.59.rr, ...), custom_call_target="tpu_custom_call" | custom-call | tf_op jit(solution)/shard_map/rec_forward/pallas_call | solution.py:531
  412.2 1.4 slice.133.edge
  413.6 18.6 %all-gather.3.cloned.1.call-done = bf16[14336,2048]{1,0:T(8,128)(2,1)} async-done(((bf16[448,2048]{1,0:T(8,128)(2,1)}), bf16[14336,2048]{1,0:T(8,128)(2,1)}) %all-gather.3.cloned.1.call-update) | async-done | bytes 58720272 | tf_op jit(solution)/shard_map/all_gather | solution.py:1039
  432.2 93.5 %channel.1 = (bf16[256,2048]{1,0:T(8,128)(2,1)}, f32[256,2048]{1,0:T(8,128)}, f32[8,2048]{1,0:T(8,128)}, f32[32,32,256]{2,1,0:T(8,128)}, f32[16,2048]{1,0:T(8,12...) custom-call(f32[256,2048]{1,0:T(8,128)} %get-tuple-element.66.n2, f32[1,2048]{1,0:T(1,128)} %slice.133.edge, ...), custom_call_target="tpu_custom_call" | custom-call | tf_op jit(solution)/shard_map/channel/pallas_call | solution.py:531
  525.8 1.0 pad_maximum_fusion.3
  526.8 2.5 pad_maximum_fusion.1
  529.4 0.8 copy.58.rstd
  530.2 85.8 %rec_backward.1 = (f32[256,2048]{1,0:T(8,128)}, bf16[256,2048]{1,0:T(8,128)(2,1)}, f32[16,2048]{1,0:T(8,128)}, f32[16,2048]{1,0:T(8,128)}, bf16[256,2048]{1,0:T(...) custom-call(f32[256,2048]{1,0:T(8,128)} %get-tuple-element.75.d_mc, ...), custom_call_target="tpu_custom_call" | custom-call | tf_op jit(solution)/shard_map/rec_backward/pallas_call | solution.py:531
  616.0 0.8 slice.146
  616.8 0.7 slice.149
  617.5 0.9 slice.147
  618.4 32.4 %final.1 = (f32[256,2048]{1,0:T(8,128)}, f32[128,256]{1,0:T(8,128)}) custom-call(bf16[256,2048]{1,0:T(8,128)(2,1)} %get-tuple-element.87.drr, bf16[256,2048]{1,0:T(8,128)(2,1)} %get-tuple-element.88.dkr, bf16[256,2048]{1,0:T(8,128)(2,1)} %get-tuple-element.89.dvr, bf16[256,2048]{1,0:T(8,128)(2,1)} %get-tuple-element.90.dwl, ...), custom_call_target="tpu_custom_call" | custom-call | tf_op jit(solution)/shard_map/final/pallas_call | solution.py:531
  650.8 0.9 pad_maximum_fusion.4
  651.9 0.2 copy.60
  652.6 1.0 copy.62
  653.6 9.5 %all-to-all-start = ((f32[4,1,18432]{2,1,0:T(1,128)}), f32[4,1,18432]{2,1,0:T(1,128)S(1)}, u32[]{:S(2)}, u32[]{:S(2)}) async-start(f32[4,1,18432]{2,1,0:T(1,128)} %copy.62), calls=%async_computation.1 | async-start | bytes 589824 | tf_op jit(solution)/shard_map/all_to_all | solution.py:1168
  663.1 5.5 all-to-all-done
  668.6 0.6 fusion.6
  669.2 0.7 slice.182
  669.9 0.2 reshape.153
  670.3 1.1 copy.63
  671.4 1.7 copy.64
  673.2 2.3 copy.89
  675.5 1.3 copy.90
  (71 shorter events, 1.6 us)
Async XLA Ops:
  7.2 425.0 %all-gather.3.cloned.1.call-start = ((), (), s32[]{:S(2)}) async-start(), calls=%async_computation.3 | async-start | bytes 60555264 | tf_op jit(solution)/shard_map/all_gather | solution.py:1039
  8.7 1.2 slice-start
  9.9 2.2 copy-start.16
  9.9 3.5 copy-start
  9.9 12.0 %copy-start.9 = (bf16[8,160,64]{1,2,0:T(8,128)(2,1)S(1)}, bf16[8,160,64]{1,2,0:T(8,128)(2,1)}, u32[]{:S(2)}) copy-start(bf16[8,160,64]{1,2,0:T(8,128)(2,1)} %param.20) | copy-start | bytes 491524
  11.3 11.2 %copy-start.10 = (bf16[8,32,256]{2,1,0:T(8,128)(2,1)S(1)}, bf16[8,32,256]{2,1,0:T(8,128)(2,1)}, u32[]{:S(2)}) copy-start(bf16[8,32,256]{2,1,0:T(8,128)(2,1)} %param.21) | copy-start | bytes 393220
  11.3 12.3 %copy-start.13 = (bf16[18,64]{1,0:T(8,128)(2,1)S(1)}, bf16[18,64]{1,0:T(8,128)(2,1)}, u32[]{:S(2)}) copy-start(bf16[18,64]{1,0:T(8,128)(2,1)} %param.17) | copy-start | bytes 6916
  11.3 12.5 %copy-start.11 = (bf16[64,448]{1,0:T(8,128)(2,1)S(1)}, bf16[64,448]{1,0:T(8,128)(2,1)}, u32[]{:S(2)}) copy-start(bf16[64,448]{1,0:T(8,128)(2,1)} %param.15) | copy-start | bytes 172036
  11.3 12.5 %copy-start.12 = (bf16[448,64]{0,1:T(8,128)(2,1)S(1)}, bf16[448,64]{0,1:T(8,128)(2,1)}, u32[]{:S(2)}) copy-start(bf16[448,64]{0,1:T(8,128)(2,1)} %param.16) | copy-start | bytes 172036
  11.3 604.7 %reduce-scatter.2.cloned.1.call-start = ((), (), s32[]{:S(2)}) async-start(), calls=%async_computation.2 | async-start | bytes 1622016 | tf_op jit(solution)/shard_map/reduce_scatter | solution.py:1121
  13.4 303.8 %collective-permute-start = (bf16[1,2048]{1,0:T(2,128)(2,1)S(1)}, bf16[1,2048]{1,0:T(2,128)(2,1)S(1)}, u32[]{:S(2)}, u32[]{:S(2)}) collective-permute-start(bf16[1,2048]{1,0:T(2,128)(2,1)S(1)} %slice_bitcast_fusion.5), channel_id=1, source_target_pairs={{0,4},{4,8},{8,12},{12,16},{16,20},{20,24},{24,28},{1,5},{5,9},{9,... | collective-permute-start | bytes 12296 | tf_op jit(solution)/shard_map/ppermute | solution.py:1013
  21.9 4.8 copy-start.14
  302.8 2.8 copy-start.8
  304.0 0.9 copy-start.2
  304.9 4.3 copy-start.1
  308.6 4.3 copy-start.7
  308.6 5.1 copy-start.6
  308.6 6.0 copy-start.5
  309.2 7.0 %copy-start.4 = (bf16[32,32,32]{2,0,1:T(8,128)(2,1)S(1)}, bf16[32,32,32]{2,0,1:T(8,128)(2,1)}, u32[]{:S(2)}) copy-start(bf16[32,32,32]{2,0,1:T(8,128)(2,1)} %slice_bitcast_fusion) | copy-start | bytes 196612
  651.7 16.9 %copy-start.15 = (s32[4]{0:T(128)S(1)}, s32[4]{0:T(128)}, u32[]{:S(2)}) copy-start(s32[4]{0:T(128)} %copy-done.14) | copy-start | bytes 52
  653.6 15.0 %all-to-all-start = ((f32[4,1,18432]{2,1,0:T(1,128)}), f32[4,1,18432]{2,1,0:T(1,128)S(1)}, u32[]{:S(2)}, u32[]{:S(2)}) async-start(f32[4,1,18432]{2,1,0:T(1,128)} %copy.62), calls=%async_computation.1 | async-start | bytes 589824 | tf_op jit(solution)/shard_map/all_to_all | solution.py:1168
  670.3 5.2 copy-start.3
Sparse Core Ops, SparseCore 0:
  11.4 420.7 all-gather.2
  529.5 68.0 reduce-scatter.1

commit v4 on v3

--- a/solution.py
+++ b/solution.py
@@ -45,7 +45,8 @@
     return r[:, :n] + r[:, n:]
 
 
-dot_inv = dot_a = dot_w = dot_b = dot_g = dot3
+dot_inv = dot_a = dot_w = dot_b = dot3
+dot_g = dot1
 
 
 def iota(shape, axis):
@@ -540,7 +541,7 @@
     )(*[x for _, x in ins])
 
 
-ORDERS = ("zxy", "zyx", "xzy", "yzx")
+ORDERS = ("zxy", "zyx", "xzy", "yzx", "zxy", "yzx")
 DIRS = "xyuds"
 
 
@@ -581,7 +582,7 @@
         self.shards, self.whole, self.send, self.recv, self.near = shards, whole, send, recv, near
         seq, dp = lax.axis_index("seq"), lax.axis_index("dp")
         z, x, y, self.c = seq // 2, seq % 2, dp // 2, dp % 2
-        self.z = z
+        self.y, self.z = y, z
         self.to = {
             "x": (z * 2 + 1 - x, dp),
             "y": (seq, (1 - y) * 2 + self.c),
@@ -617,10 +618,16 @@
     def chip(self, b):
         return b[0] * 4 + b[1] * 2 + b[2]
 
+    def shard(self, t, k=None):
+        ref = self.shards[t]
+        if len(ref.shape) == 2:
+            return ref
+        return ref.at[1 - self.y if k == "y" else self.y]
+
     def copy(self, t, own, b, k):
         slot = self.whole[t].at[self.chip(b) * 2 + self.c]
         return pltpu.make_async_remote_copy(
-            src_ref=self.shards[t] if own else slot,
+            src_ref=self.shard(t, k) if own else slot,
             dst_ref=slot,
             send_sem=self.send.at[DIRS.index(k), t, self.chip(b)],
             recv_sem=self.recv.at[1 if k == "s" else 0, t, self.chip(b)],
@@ -630,7 +637,7 @@
 
     def local(self, t, b):
         return pltpu.make_async_copy(
-            self.shards[t], self.whole[t].at[self.chip(b) * 2 + self.c], self.near.at[t]
+            self.shard(t), self.whole[t].at[self.chip(b) * 2 + self.c], self.near.at[t]
         )
 
     def goes(self, event):
@@ -657,7 +664,7 @@
         for t in range(len(self.shards)):
             for i in range(16):
                 pltpu.make_async_remote_copy(
-                    src_ref=self.shards[t],
+                    src_ref=self.shard(t),
                     dst_ref=self.whole[t].at[i * 2 + 1 - self.c],
                     send_sem=self.send.at[4, t, i],
                     recv_sem=self.recv.at[1, t, i],
@@ -688,19 +695,64 @@
     g.finish()
 
 
+def own_gather():
+    return (lax.axis_size("seq"), lax.axis_size("dp")) == (8, 4)
+
+
 def gather(shards):
-    n_seq, n_dp, n = lax.axis_size("seq"), lax.axis_size("dp"), len(shards)
-    if (n_seq, n_dp) != (8, 4):
+    if not own_gather():
         return [lax.all_gather(s, ("seq", "dp"), axis=0) for s in shards]
+    n, devices = len(shards), 32
     return pl.pallas_call(
-        functools.partial(gather_kernel, [ORDERS[i % len(ORDERS)] for i in range(n)]),
-        out_shape=[jax.ShapeDtypeStruct((n_seq * n_dp,) + s.shape, s.dtype) for s in shards],
+        functools.partial(gather_kernel, ORDERS[:n]),
+        out_shape=[jax.ShapeDtypeStruct((devices,) + s.shape[-2:], s.dtype) for s in shards],
         in_specs=[pl.BlockSpec(memory_space=pl.ANY)] * n,
         out_specs=[pl.BlockSpec(memory_space=pl.ANY)] * n,
         scratch_shapes=gather_scratch(n),
         compiler_params=pltpu.CompilerParams(collective_id=2, has_side_effects=True),
         name="gather_time",
     )(*shards)
+
+
+def sort_kernel(kinds, late, few, small, chosen, hidden, hidden_late, vec):
+    half = kinds // 2
+    base = (lax.axis_index("dp") % 2) * (half + 4 * RANK)
+    rows = lambda o, at, n: few[o, pl.ds(pl.multiple_of(base + at, 16), n), :]
+    left = iota((half, PW), 1) < D
+    for p in range(few.shape[0] // 2):
+        one, two = rows(2 * p, 0, half).astype(F32), rows(2 * p + 1, 0, half).astype(F32)
+        at = slice(p * PW, (p + 1) * PW)
+        chosen[:half, at] = jnp.where(left, one, pltpu.roll(two, D, axis=1)).astype(BF)
+        chosen[half:, at] = jnp.where(left, pltpu.roll(one, D, axis=1), two).astype(BF)
+    per = PW // late
+    lane = iota((2 * RANK, PW), 1) // late
+    for g in range(few.shape[0] // per):
+        tail = None
+        for j in range(per):
+            o = g * per + j
+            low, high = rows(o, half, 2 * RANK), rows(o, half + 2 * RANK, 2 * RANK)
+            hidden[o, :, :PW], hidden[o, :, PW:] = low, high
+            shift = (j + 1) * late % PW
+            end = pltpu.roll(high.astype(F32), shift, axis=1) if shift else high.astype(F32)
+            tail = end if tail is None else jnp.where(lane == j, end, tail)
+        hidden_late[:, g * PW : (g + 1) * PW] = tail.astype(BF)
+    vec[...] = small[...].astype(F32).T[D : D + vec.shape[0]]
+
+
+def sort_small(kinds, late, nvec, few, misc):
+    n, width = few.shape[0], misc.shape[0]
+    shape = jax.ShapeDtypeStruct
+    return over_tiles(
+        functools.partial(sort_kernel, kinds, late), 1,
+        [(whole, few), (pl.BlockSpec((width, PW), lambda i: (0, 7)), misc)],
+        [
+            (whole, shape((kinds, width), BF)),
+            (whole, shape((n, 2 * RANK, 2 * PW), BF)),
+            (whole, shape((2 * RANK, n * late), BF)),
+            (whole, shape((nvec, width), F32)),
+        ],
+        "sort_small",
+    )
 
 
 LATE_ORDERS = ("zxy", "yzx")
@@ -835,7 +887,7 @@
     return ff // 8 if (n_seq, n_dp) == (8, 4) and ff % 128 == 0 else 0
 
 
-def channel(n2, edge, norm, gy, middle, down_c, up_f, kv, hidden, key_shard, value_shard):
+def channel(n2, edge, norm, gy, middle, down_c, up_f, kv, hidden, key_shard, value_shard, hidden_late):
     n, both, width = kv.shape
     ff, length, late = hidden.shape[2], n2.shape[0], key_shard.shape[0]
     per = max(1, min(n, 512 // ff))
@@ -867,7 +919,6 @@
     ]
     params = {}
     if late:
-        hidden_late = jnp.swapaxes(hidden[:, :, ff - late :], 0, 1).reshape(2 * RANK, n * late)
         ins += [(far, key_shard), (far, value_shard), (whole, hidden_late)]
         outs += [(result, shape((8, RANK, 2 * n * late // 8), F32)), (result, shape((8, width), F32))]
         scratch += [pltpu.VMEM((n, late, width), BF)] * 2
@@ -918,12 +969,29 @@
 
 
 def final_kernel(
-    n, drr, dkr, dvr, dwl, dal, dgg, m_r, m_k, m_v, hs, act, chosen, second, down_o, up_o, hat, rstd, d_mid, vecs,
-    w_r, w_k, w_v, down, first, vec,
-    grad, summed, stay, go, dhs, d_act, parts, here, came, send_sem, recv_sem, edge_sem,
+    n, fast, drr, dkr, dvr, dwl, dal, dgg, m_r, m_k, m_v, hs, act, chosen, second, down_o, up_o, hat, rstd, d_mid, vecs,
+    w_r, w_k, w_v, down, first, vec, *refs,
 ):
     step, last = pl.program_id(0), pl.num_programs(0) - 1
     me, dp = lax.axis_index("seq"), lax.axis_index("dp")
+    if fast:
+        early, picks, grad, g_model, g_hidden, *refs = refs
+        stage_m, stage_h, from_m, from_h, own_send, own_recv, *refs = refs
+    else:
+        grad, summed, *refs = refs
+    stay, go, dhs, d_act, parts, here, came, send_sem, recv_sem, edge_sem = refs
+
+    def to_owner(k, i):
+        peer = lax.rem(dp + k, 4)
+        stage, slots = ((stage_m, from_m), (stage_h, from_h))[i]
+        return pltpu.make_async_remote_copy(
+            src_ref=stage.at[peer],
+            dst_ref=slots.at[k - 1],
+            send_sem=own_send.at[i, k - 1],
+            recv_sem=own_recv.at[i, k - 1],
+            device_id=(me, peer),
+            device_id_type=MESH,
+        )
 
     def copy(k):
         peer = lax.rem(me + k, n)
@@ -954,6 +1022,11 @@
             pl.semaphore_signal(
                 barrier, inc=1, device_id=(lax.rem(me + k, n), dp), device_id_type=MESH
             )
+        if fast:
+            for k in range(1, 4):
+                pl.semaphore_signal(
+                    barrier, inc=1, device_id=(me, lax.rem(dp + k, 4)), device_id_type=MESH
+                )
         rows = [None] * 6 + [down_o[...], up_o[...]]
         for i, (d, m) in enumerate(((drr, m_r), (dkr, m_k), (dvr, m_v))):
             dh = (SCALE * mm_nt(d[...], chosen[(5 + i) * RANK : (6 + i) * RANK, :])).astype(BF)
@@ -963,7 +1036,7 @@
         for i, r in enumerate(rows):
             for p in range(n):
                 parts[p, i * RANK : (i + 1) * RANK, :] = r[:, p * wide : (p + 1) * wide].astype(BF)
-        pl.semaphore_wait(barrier, n - 1)
+        pl.semaphore_wait(barrier, n - 1 + (3 if fast else 0))
         for k in range(1, n):
             copy(k).start()
         is_w, is_a, is_g = branch_masks(act.shape)
@@ -993,7 +1066,28 @@
         t = parts[me].astype(F32)
         for k in range(1, n):
             t = t + here[k - 1].astype(F32)
-        summed[...] = t
+        if fast:
+            e = early[...]
+            r = lambda x, i, k: x[i * RANK : (i + k) * RANK]
+            rows = jnp.concatenate(
+                [r(t, 0, 3), r(t, 6, 1), r(e, 0, 1), r(t, 3, 3), r(t, 7, 1), r(e, 1, 1)], 0
+            )
+            tails = e[10 * RANK : 11 * RANK]
+            lane = iota((2 * RANK, PW), 1)
+            for j in range(4):
+                two = rows[:, (j // 2) * PW : (j // 2 + 1) * PW]
+                stage_m[j] = pltpu.roll(two, D, axis=1) if j % 2 else two
+                mine = e[(2 + 2 * j) * RANK : (4 + 2 * j) * RANK]
+                tail = jnp.concatenate([tails[:, :PW], tails[:, PW:]], 0)
+                shift = (3 - j) * (PW // 4)
+                tail = pltpu.roll(tail, shift, axis=1) if shift else tail
+                stage_h[j, :, :PW] = mine[:, :PW]
+                stage_h[j, :, PW:] = jnp.where(lane >= 3 * PW // 4, tail, mine[:, PW:])
+            for k in range(1, 4):
+                to_owner(k, 0).start()
+                to_owner(k, 1).start()
+        else:
+            summed[...] = t
         pl.when(me < n - 1)(lambda: edge(me + 1).wait_recv())
         size = go.shape[0]
         g = pltpu.roll(go[...], size - 1, axis=0)
@@ -1005,6 +1099,21 @@
             - hat[...] * jnp.mean(dhat * hat[...], axis=-1, keepdims=True)
         )
         pl.when(me > 0)(lambda: edge(me - 1).wait_send())
+        if fast:
+            for k in range(1, 4):
+                to_owner(k, 0).wait()
+                to_owner(k, 1).wait()
+            found = [(dp, stage_m[dp], stage_h[dp])]
+            found += [(lax.rem(dp + 4 - k, 4), from_m[k - 1], from_h[k - 1]) for k in range(1, 4)]
+            adapters = g_model.shape[0]
+            weights = [picks[pl.ds(pl.multiple_of(q * adapters, 8), adapters), :] for q, _, _ in found]
+            for a in range(adapters):
+                m, h = None, None
+                for w, (_, x, y) in zip(weights, found):
+                    w = w[a : a + 1, :]
+                    x, y = x * w, y * jnp.concatenate([w, w], 1)
+                    m, h = (x, y) if m is None else (m + x, h + y)
+                g_model[a], g_hidden[a] = m[:, :D], h
 
 
 def shifted(block, axis, distance):
@@ -1040,8 +1149,22 @@
 
     index_all = lax.all_gather(index, "dp", axis=0, tiled=True)
     pick = index_all[:, None] == jnp.arange(adapters, dtype=jnp.int32)[None, :]
-    few = jnp.concatenate([model_rows.reshape(adapters, -1), hidden_rows.reshape(adapters, -1)], 1)
-    few = jnp.einsum("sa,ax->sx", pick.astype(BF), few, preferred_element_type=F32).astype(BF)
+    pick_low = pick.astype(BF)
+    fast = own_gather() and (cols, ff, 2 * inner + nvec) == (D, 2 * PW, 914)
+    if fast:
+        half = kinds // 2
+        few = jnp.concatenate(
+            [
+                jnp.concatenate([model_rows[:, :half], model_rows[:, half:]], 2),
+                hidden_rows[:, :, :PW],
+                hidden_rows[:, :, PW:],
+            ],
+            1,
+        )
+    else:
+        few = jnp.concatenate([model_rows.reshape(adapters, -1), hidden_rows.reshape(adapters, -1)], 1)
+        few = few.reshape(adapters, -1, 128)
+    few = jnp.einsum("sa,arx->srx", pick_low, few, preferred_element_type=F32).astype(BF)
     pad = lambda k: jnp.zeros((cols, k), BF)
     misc = jnp.concatenate(
         [first, pad(HALF - inner), second.T, vectors.T, pad(HALF - inner - nvec)], axis=1
@@ -1058,14 +1181,18 @@
     valid = jnp.where(start, 0.0, 1.0).astype(F32)
     hat_prev, hat, rstd = hat[:-1], hat[1:], rstd[1:]
 
-    *mats, misc, few_all = gather([turned[0], turned[1], turned[2], turned[3], misc, few.reshape(-1, 128)])
+    few = few.reshape((2, -1, 128) if fast else (-1, 128))
+    *mats, misc, few_all = gather([turned[0], turned[1], turned[2], turned[3], misc, few])
     mats = [m.reshape(width, width) for m in mats]
     misc = misc.reshape(width, -1)
-    vec = misc[:, HALF + inner : HALF + inner + nvec].T.astype(F32)
-    own = lax.dynamic_index_in_dim(few_all.reshape(n, n_dp, -1, 128), lax.axis_index("dp"), 1, False)
-    own = own.reshape(n, -1)
-    chosen = own[:, : kinds * cols].reshape(n, kinds, cols).transpose(1, 0, 2).reshape(kinds, width)
-    hidden = own[:, kinds * cols :].reshape(n, 2 * RANK, ff)
+    if fast:
+        chosen, hidden, hidden_late, vec = sort_small(kinds, ff - soon, nvec, few_all, misc)
+    else:
+        vec = misc[:, HALF + inner : HALF + inner + nvec].T.astype(F32)
+        own = lax.dynamic_index_in_dim(few_all.reshape(n, n_dp, -1, 128), lax.axis_index("dp"), 1, False)
+        own = own.reshape(n, -1)
+        chosen = own[:, : kinds * cols].reshape(n, kinds, cols).transpose(1, 0, 2).reshape(kinds, width)
+        hidden, hidden_late = own[:, kinds * cols :].reshape(n, 2 * RANK, ff), None
     down = lambda i: chosen[i * RANK : (i + 1) * RANK]
     up = lambda i: chosen[(5 + i) * RANK : (6 + i) * RANK]
 
@@ -1107,7 +1234,7 @@
     row = shifted(n2[-1:], "seq", 1) if soon_only else n2[-1:]
     out, d_mc, moved, g_hidden, up_f, down_c, *more = channel(
         n2, row, vec, gy, middle, down(4), up(4), kv, hidden,
-        key_shard[soon:], cvalue[soon:],
+        key_shard[soon:], cvalue[soon:], hidden_late,
     )
     wide = n_dp * cols
     by_piece = lambda rows: jnp.swapaxes(rows.reshape(-1, n_seq, wide), 0, 1)
@@ -1134,28 +1261,39 @@
         collective_id=1, has_side_effects=True,
     )
     early, drr = lax.optimization_barrier((early, drr))
-    grad_tokens, late = over_tiles(
-        functools.partial(final_kernel, n_seq), tiles,
-        [(whole, a) for a in (drr, dkr, dvr, dwl, dal, dgg, m_r, m_k, m_v, hs, act, chosen)]
-        + [(pl.BlockSpec((width, HALF), lambda i: (0, 1), pipeline_mode=pl.Buffered(1)), misc)]
-        + [(whole, a) for a in (down_o, up_o, hat, rstd, d_mid, vec)]
-        + [(cut, mats[0]), (cut, mats[1]), (cut, mats[2]), (cut, chosen), (first_rows, misc), (cut, vec)],
-        [(result, full), (result, shape((8 * RANK, wide), F32))], "final",
-        [
-            pltpu.VMEM((length, width), F32),
-            pltpu.VMEM((length, width), F32),
-            pltpu.VMEM((3, length, RANK), BF),
-            pltpu.VMEM((3, length, HALF), BF),
-            pltpu.VMEM((n_seq, 8 * RANK, wide), BF),
-            pltpu.VMEM((n_seq - 1, 8 * RANK, wide), BF),
-            pltpu.VMEM((8, width), F32),
-            pltpu.SemaphoreType.DMA((n_seq - 1,)),
-            pltpu.SemaphoreType.DMA((n_seq - 1,)),
-            pltpu.SemaphoreType.DMA((2,)),
-        ],
+    ins = [(whole, a) for a in (drr, dkr, dvr, dwl, dal, dgg, m_r, m_k, m_v, hs, act, chosen)]
+    ins += [(pl.BlockSpec((width, HALF), lambda i: (0, 1), pipeline_mode=pl.Buffered(1)), misc)]
+    ins += [(whole, a) for a in (down_o, up_o, hat, rstd, d_mid, vec)]
+    ins += [(cut, mats[0]), (cut, mats[1]), (cut, mats[2]), (cut, chosen), (first_rows, misc), (cut, vec)]
+    scratch = [
+        pltpu.VMEM((length, width), F32),
+        pltpu.VMEM((length, width), F32),
+        pltpu.VMEM((3, length, RANK), BF),
+        pltpu.VMEM((3, length, HALF), BF),
+        pltpu.VMEM((n_seq, 8 * RANK, wide), BF),
+        pltpu.VMEM((n_seq - 1, 8 * RANK, wide), BF),
+        pltpu.VMEM((8, width), F32),
+        pltpu.SemaphoreType.DMA((n_seq - 1,)),
+        pltpu.SemaphoreType.DMA((n_seq - 1,)),
+        pltpu.SemaphoreType.DMA((2,)),
+    ]
+    ready = fast and adapters == 8 and not soon_only
+    call = lambda ins, outs, scratch: over_tiles(
+        functools.partial(final_kernel, n_seq, ready), tiles, ins, [(result, full)] + outs, "final", scratch,
         collective_id=3, has_side_effects=True,
     )
-
+    if ready:
+        picks = jnp.broadcast_to(pick.astype(F32).reshape(-1, 1), (n_dp * adapters, PW))
+        grad_tokens, grad_model, h = call(
+            ins + [(whole, early), (whole, picks)],
+            [(result, shape((adapters, kinds, cols), F32)), (result, shape((adapters, 2 * RANK, ff), F32))],
+            [pltpu.VMEM((4, kinds, PW), F32), pltpu.VMEM((4, 2 * RANK, ff), F32)]
+            + [pltpu.VMEM((3, kinds, PW), F32), pltpu.VMEM((3, 2 * RANK, ff), F32)]
+            + [pltpu.SemaphoreType.DMA((2, 3))] * 2
+            + scratch,
+        )
+        return out[None], grad_tokens[None], grad_model, h
+    grad_tokens, late = call(ins, [(result, shape((8 * RANK, wide), F32))], scratch)
     mine = early[2 * RANK : 2 * RANK + 2 * RANK * ff // cols].reshape(n_dp, 2 * RANK, ff)
     if not soon_only:
         tail = early[2 * RANK + 2 * RANK * ff // cols :].reshape(RANK, 2, n_dp, ff - soon)

time: 692 us -> 659 us (0.952)
  local copies, waits for them, and re-layouts: 47.8 us -> 24.5 us
  waiting for transfers between devices: 24.2 us -> 44.3 us
  Pallas kernels: 569 us -> 550 us
  starting transfers between devices: 13.5 us -> 4.02 us
    all_gather x1, waiting for transfers between devices: 18.6 us -> 44.2 us  [body(): lax.all_gather(jnp.concatenate([key_shard[:soon], cvalue[:soon]], 0), axe...]
    pallas_call x5 -> x6, Pallas kernels: 303 us -> 292 us  [over_tiles(): pl.pallas_call(body, grid=(steps,), in_specs=[made(spec, x.shape) for spe...]
    all_to_all x1 -> x0, starting transfers between devices: 9.5 us -> none  [body(): both = lax.all_to_all(both, 'dp', split_axis=0, concat_axis=0, tiled=True)]
    reshape x9 -> x0, local copies, waits for them, and re-layouts: 7.98 us -> none  [the longest x2 5.52 us: body(): own[:, :kinds * cols].reshape(n, kinds, cols).transpose(1, 0, 2)]
    pallas_call x1, Pallas kernels: 266 us -> 258 us  [gather(): pl.pallas_call(functools.partial(gather_kernel, ORDERS[:n]), out_shape=[j...]
  transfers between devices with their start and end apart: 4 -> 3, of which waited for: 2 -> 1; matrix products, arithmetic and copies ran while one was open for 5% -> 3% of each run, Pallas kernels for 65% -> 66%
where the time goes in v4:
time: 659 us; the launch traced here: 651 us
  Pallas kernels  550 us (83%)
  waiting for transfers between devices  44.3 us (7%)
  local copies, waits for them, and re-layouts  24.5 us (4%)
  between operations  15.2 us (2%)
  other arithmetic  7.25 us (1%)
    pallas_call x6, Pallas kernels, over_tiles(): pl.pallas_call(body, grid=(steps,), in_specs=[made(spec, x.shape) for spe...  292 us
    pallas_call x1, Pallas kernels, gather(): pl.pallas_call(functools.partial(gather_kernel, ORDERS[:n]), out_shape=[j...  258 us
    all_gather x1, waiting for transfers between devices, body(): lax.all_gather(jnp.concatenate([key_shard[:soon], cvalue[:soon]], 0), axe...  44.2 us
  transfers between devices with their start and end apart: 3, of which 1 were waited for; matrix products, arithmetic and copies ran while one was open for 3% of the time, Pallas kernels for 66%

profile of v4, /device:TPU:1, one launch (start us, length us, event | category | flops | bytes accessed | tf_op | source)
XLA Modules:
  0.0 651.4 jit_solution(14978245825444576845)
XLA Ops:
  7.2 0.0 all-gather.3.cloned.1.call-start
  7.2 1.5 copy.29
  8.7 0.0 slice-start
  8.7 0.1 slice.100
  8.8 1.1 slice-done
  9.9 1.4 pad_maximum_fusion
  11.3 0.0 all-gather.3.cloned.1.call-update
  11.3 0.0 copy-start.3
  11.3 0.0 reduce-scatter.2.cloned.1.call-start
  12.1 0.0 copy-done.8
  12.1 0.6 dynamic-slice
  12.7 0.8 dynamic-update-slice
  13.4 0.0 copy-done
  13.5 3.9 collective-permute-start
  17.4 4.6 all-reduce
  22.0 1.2 fusion.19
  23.2 0.8 copy.33
  24.0 0.2 copy.34
  24.2 0.9 fusion.20
  25.2 1.3 convolution_convert_fusion
  26.4 0.7 copy.28
  27.2 0.0 copy-done.7
  27.2 0.1 copy.23
  27.3 0.0 copy-done.6
  27.3 1.6 concatenate.26.refs_4_
  28.9 0.0 copy-done.3
  28.9 1.0 slice_bitcast_fusion
  29.9 258.2 %gather_time.1 = (bf16[32,64,2048]{2,1,0:T(8,128)(2,1)}, bf16[32,64,2048]{2,1,0:T(8,128)(2,1)}, bf16[32,64,2048]{2,1,0:T(8,128)(2,1)}, bf16[32,64,2048]{2,1,0:T(...) custom-call(bf16[64,2048]{1,0:T(8,128)(2,1)} %get-tuple-element.127.refs_0_, ...), custom_call_target="tpu_custom_call" | custom-call | tf_op jit(solution)/shard_map/gather_time/pallas_call | solution.py:706
  288.0 0.0 copy-start.1
  288.1 3.2 sort_small.1
  291.3 1.6 fusion.18
  292.9 0.7 fusion.11.valid
  293.6 0.7 slice.101.refs_0_
  294.3 0.0 copy-done.1
  294.3 0.7 slice.91.refs_1_
  294.9 0.0 collective-permute-done
  294.9 0.4 convert_reduce_fusion
  295.3 0.7 fusion.2
  296.0 0.5 fusion
  296.6 2.5 fusion.17
  299.0 25.1 %project.1 = (f32[256,2048]{1,0:T(8,128)}, f32[256,2048]{1,0:T(8,128)}, f32[256,2048]{1,0:T(8,128)}, f32[256,2048]{1,0:T(8,128)}, f32[256,2048]{1,0:T(8,128)}, /...) custom-call(f32[256,2048]{1,0:T(8,128)} %get-tuple-element.123.hat, ...), custom_call_target="tpu_custom_call" | custom-call | tf_op jit(solution)/shard_map/project/pallas_call | solution.py:532
  324.1 65.8 %rec_forward.1 = (f32[256,2048]{1,0:T(8,128)}, f32[256,2048]{1,0:T(8,128)}, f32[256,2048]{1,0:T(8,128)}, f32[64,2048]{1,0:T(8,128)}, bf16[256,2048]{1,0:T(8,128)...) custom-call(f32[256,2048]{1,0:T(8,128)} %get-tuple-element.66.rr, ...), custom_call_target="tpu_custom_call" | custom-call | tf_op jit(solution)/shard_map/rec_forward/pallas_call | solution.py:532
  390.0 1.4 slice.85.edge
  391.4 44.2 %all-gather.3.cloned.1.call-done = bf16[14336,2048]{1,0:T(8,128)(2,1)} async-done(((bf16[448,2048]{1,0:T(8,128)(2,1)}), bf16[14336,2048]{1,0:T(8,128)(2,1)}) %all-gather.3.cloned.1.call-update) | async-done | bytes 58720272 | tf_op jit(solution)/shard_map/all_gather | solution.py:1148
  435.6 84.7 %channel.1 = (bf16[256,2048]{1,0:T(8,128)(2,1)}, f32[256,2048]{1,0:T(8,128)}, f32[8,2048]{1,0:T(8,128)}, f32[32,32,256]{2,1,0:T(8,128)}, f32[16,2048]{1,0:T(8,12...) custom-call(f32[256,2048]{1,0:T(8,128)} %get-tuple-element.73.n2, f32[1,2048]{1,0:T(1,128)} %slice.85.edge, ...), custom_call_target="tpu_custom_call" | custom-call | tf_op jit(solution)/shard_map/channel/pallas_call | solution.py:532
  520.4 1.0 pad_maximum_fusion.3
  521.4 2.5 pad_maximum_fusion.1
  523.9 0.0 reduce-scatter.2.cloned.1.call-update
  523.9 0.1 fusion.12
  524.0 0.1 reshape.102
  524.1 0.1 slice.92
  524.2 0.8 copy.31.rstd
  525.0 75.2 %rec_backward.1 = (f32[256,2048]{1,0:T(8,128)}, bf16[256,2048]{1,0:T(8,128)(2,1)}, f32[16,2048]{1,0:T(8,128)}, f32[16,2048]{1,0:T(8,128)}, bf16[256,2048]{1,0:T(...) custom-call(f32[256,2048]{1,0:T(8,128)} %get-tuple-element.84.d_mc, ...), custom_call_target="tpu_custom_call" | custom-call | tf_op jit(solution)/shard_map/rec_backward/pallas_call | solution.py:532
  600.2 0.0 reduce-scatter.2.cloned.1.call-done
  600.2 0.7 broadcast_in_dim.35.refs_1_
  600.9 38.2 %final.1 = (f32[256,2048]{1,0:T(8,128)}, f32[8,160,64]{2,1,0:T(8,128)}, f32[8,32,256]{2,1,0:T(8,128)}) custom-call(bf16[256,2048]{1,0:T(8,128)(2,1)} %get-tuple-element.96.drr, bf16[256,2048]{1,0:T(8,128)(2,1)} %get-tuple-element.97.dkr, bf16[256,2048]{1,0:T(8,128)(2,1)} %get-tuple-element.98.dvr, bf16[256,2048]{1,0:T(8,128)(2,1)} %get-tuple-element.99.dwl, ...), custom_call_target="tpu_custom_call" | custom-call | tf_op jit(solution)/shard_map/final/pallas_call | solution.py:532
  639.0 0.0 copy-start.2
  639.0 2.3 copy.32
  641.4 0.0 copy-done.4
  641.4 1.0 copy.45
  642.4 0.0 copy-done.2
  642.4 1.3 copy.46
  643.7 0.0 copy-done.5
  643.7 0.7 copy.47
  (15 shorter events, 0.1 us)
Async XLA Ops:
  7.2 428.5 %all-gather.3.cloned.1.call-start = ((), (), s32[]{:S(2)}) async-start(), calls=%async_computation.2 | async-start | bytes 60555264 | tf_op jit(solution)/shard_map/all_gather | solution.py:1148
  8.7 1.2 slice-start
  9.9 2.2 copy-start.8
  9.9 3.6 copy-start
  11.3 15.9 %copy-start.7 = (bf16[18,64]{1,0:T(8,128)(2,1)S(1)}, bf16[18,64]{1,0:T(8,128)(2,1)}, u32[]{:S(2)}) copy-start(bf16[18,64]{1,0:T(8,128)(2,1)} %param.17) | copy-start | bytes 6916
  11.3 16.0 %copy-start.6 = (bf16[64,448]{1,0:T(8,128)(2,1)S(1)}, bf16[64,448]{1,0:T(8,128)(2,1)}, u32[]{:S(2)}) copy-start(bf16[64,448]{1,0:T(8,128)(2,1)} %param.15) | copy-start | bytes 172036
  11.3 17.6 %copy-start.3 = (bf16[4,2048,64]{1,2,0:T(8,128)(2,1)S(1)}, bf16[4,2048,64]{1,2,0:T(8,128)(2,1)}, u32[]{:S(2)}) copy-start(bf16[4,2048,64]{1,2,0:T(8,128)(2,1)} %param.14) | copy-start | bytes 3145732
  11.3 588.9 %reduce-scatter.2.cloned.1.call-start = ((), (), s32[]{:S(2)}) async-start(), calls=%async_computation.1 | async-start | bytes 1622016 | tf_op jit(solution)/shard_map/reduce_scatter | solution.py:1248
  13.5 281.5 %collective-permute-start = (bf16[1,2048]{1,0:T(2,128)(2,1)S(1)}, bf16[1,2048]{1,0:T(2,128)(2,1)S(1)}, u32[]{:S(2)}, u32[]{:S(2)}) collective-permute-start(bf16[1,2048]{1,0:T(2,128)(2,1)S(1)} %slice_bitcast_fusion.4), channel_id=1, source_target_pairs={{0,4},{4,8},{8,12},{12,16},{16,20},{20,24},{24,28},{1,5},{5,9},{9,... | collective-permute-start | bytes 12296 | tf_op jit(solution)/shard_map/ppermute | solution.py:1122
  288.0 6.2 copy-start.1
  600.9 40.5 %copy-start.4 = (bf16[256,2048]{1,0:T(8,128)(2,1)S(1)}, bf16[256,2048]{1,0:T(8,128)(2,1)}, u32[]{:S(2)}) copy-start(bf16[256,2048]{1,0:T(8,128)(2,1)} %get-tuple-element.77) | copy-start | bytes 3145732
  639.0 3.3 copy-start.2
  642.4 1.3 copy-start.5
Sparse Core Ops, SparseCore 0:
  11.4 424.1 all-gather.2
  524.1 68.1 reduce-scatter.1

commit v5 on v4

--- a/solution.py
+++ b/solution.py
@@ -45,8 +45,8 @@
     return r[:, :n] + r[:, n:]
 
 
-dot_inv = dot_a = dot_w = dot_b = dot3
-dot_g = dot1
+dot_inv = dot_a = dot3
+dot_w = dot_b = dot_g = dot1
 
 
 def iota(shape, axis):
@@ -541,7 +541,7 @@
     )(*[x for _, x in ins])
 
 
-ORDERS = ("zxy", "zyx", "xzy", "yzx", "zxy", "yzx")
+ORDERS = ("zxy", "zyx", "xzy", "yzx", "zxy", "yzx", "zyx")
 DIRS = "xyuds"
 
 
@@ -703,7 +703,7 @@
     if not own_gather():
         return [lax.all_gather(s, ("seq", "dp"), axis=0) for s in shards]
     n, devices = len(shards), 32
-    return pl.pallas_call(
+    made = pl.pallas_call(
         functools.partial(gather_kernel, ORDERS[:n]),
         out_shape=[jax.ShapeDtypeStruct((devices,) + s.shape[-2:], s.dtype) for s in shards],
         in_specs=[pl.BlockSpec(memory_space=pl.ANY)] * n,
@@ -712,6 +712,7 @@
         compiler_params=pltpu.CompilerParams(collective_id=2, has_side_effects=True),
         name="gather_time",
     )(*shards)
+    return list(made)
 
 
 def sort_kernel(kinds, late, few, small, chosen, hidden, hidden_late, vec):
@@ -755,6 +756,8 @@
     )
 
 
+UNITS = 512
+EARLY_UNITS = 16
 LATE_ORDERS = ("zxy", "yzx")
 LATE_STEPS = (
     (0, 2, 2, 4, 4, 7, 7, 11, 9, 4, 2, 5, 9, 11, 9, 13, 7, 11, 4, 8, 2, 6, 5, 9, 7, 11, 9, 13),
@@ -766,14 +769,17 @@
     late, n2, edge, norm, gy, middle, down_c, up_f, kv, hidden, *refs,
 ):
     if late:
-        key_shard, value_shard, hidden_late, *refs = refs
+        kv2, key_shard, value_shard, hidden_late, *refs = refs
     out, dmc, first, g_hidden, g_up_f, g_down_c, *refs = refs
     if late:
         g_late, d_edge, *refs = refs
     mc, mct, gyt, ffo, h_c, dh_f, acc_f, acc_c, *refs = refs
     step, last = pl.program_id(0), pl.num_programs(0) - 1
     per, ff = kv.shape[0], kv.shape[1] // 2
+    blocks = [(kv, ff)]
     if late:
+        blocks.append((kv2, kv2.shape[1] // 2))
+        ff += kv2.shape[1] // 2
         key_late, value_late, mine, came, edge_sem, *sems = refs
         g = Gathering(LATE_ORDERS, LATE_STEPS, (key_shard, value_shard), (key_late, value_late), *sems)
         seq, dp = lax.axis_index("seq"), lax.axis_index("dp")
@@ -851,8 +857,8 @@
 
     @pl.when(step < last + (0 if late else 1))
     def _():
-        key = jnp.concatenate([kv[b, :ff] for b in range(per)], 0)
-        value = jnp.concatenate([kv[b, ff:] for b in range(per)], 0)
+        key = jnp.concatenate([a[b, :h] for b in range(per) for a, h in blocks], 0)
+        value = jnp.concatenate([a[b, h:] for b in range(per) for a, h in blocks], 0)
         grads = units(key, value, [hidden[b, :, :ff] for b in range(per)])
         for b, (low, high) in enumerate(grads):
             if late:
@@ -887,10 +893,10 @@
     return ff // 8 if (n_seq, n_dp) == (8, 4) and ff % 128 == 0 else 0
 
 
-def channel(n2, edge, norm, gy, middle, down_c, up_f, kv, hidden, key_shard, value_shard, hidden_late):
+def channel(n2, edge, norm, gy, middle, down_c, up_f, kv, hidden, kv2, key_shard, value_shard, hidden_late):
     n, both, width = kv.shape
     ff, length, late = hidden.shape[2], n2.shape[0], key_shard.shape[0]
-    per = max(1, min(n, 512 // ff))
+    per = max(1, min(n, UNITS // ff))
     steps = n // per
     block = lambda shape: pl.BlockSpec(
         (per,) + tuple(shape[1:]), lambda i: (jnp.minimum(i, steps - 1), 0, 0)
@@ -919,7 +925,7 @@
     ]
     params = {}
     if late:
-        ins += [(far, key_shard), (far, value_shard), (whole, hidden_late)]
+        ins += [(block, kv2), (far, key_shard), (far, value_shard), (whole, hidden_late)]
         outs += [(result, shape((8, RANK, 2 * n * late // 8), F32)), (result, shape((8, width), F32))]
         scratch += [pltpu.VMEM((n, late, width), BF)] * 2
         scratch += [pltpu.VMEM((2, 8, width), F32)] * 2 + [pltpu.SemaphoreType.DMA((2, 2))]
@@ -1145,7 +1151,8 @@
     ff, inner, nvec = ckey.shape[1], first.shape[1], vectors.shape[0]
 
     key_shard, soon = ckey.T, ff - late_units(n_seq, n_dp, ff)
-    kv = lax.all_gather(jnp.concatenate([key_shard[:soon], cvalue[:soon]], 0), axes, axis=0)
+    most = soon - EARLY_UNITS if soon < ff else soon
+    kv = lax.all_gather(jnp.concatenate([key_shard[:most], cvalue[:most]], 0), axes, axis=0)
 
     index_all = lax.all_gather(index, "dp", axis=0, tiled=True)
     pick = index_all[:, None] == jnp.arange(adapters, dtype=jnp.int32)[None, :]
@@ -1171,6 +1178,12 @@
     )
     turned = jnp.swapaxes(proj, 1, 2)
 
+    few = few.reshape((2, -1, 128) if fast else (-1, 128))
+    more = [jnp.concatenate([key_shard[most:soon], cvalue[most:soon]], 0)] if most < soon else []
+    *mats, misc, few_all, kv2 = gather([turned[0], turned[1], turned[2], turned[3], misc, few] + more) + [None] * (
+        most == soon
+    )
+    mats[0], tokens = lax.optimization_barrier((mats[0], tokens))
     wide = tokens.astype(F32)
     ahead = shifted(tokens[-1:], "seq", 1).astype(F32)
     rows = jnp.concatenate([ahead, wide], 0)
@@ -1181,8 +1194,6 @@
     valid = jnp.where(start, 0.0, 1.0).astype(F32)
     hat_prev, hat, rstd = hat[:-1], hat[1:], rstd[1:]
 
-    few = few.reshape((2, -1, 128) if fast else (-1, 128))
-    *mats, misc, few_all = gather([turned[0], turned[1], turned[2], turned[3], misc, few])
     mats = [m.reshape(width, width) for m in mats]
     misc = misc.reshape(width, -1)
     if fast:
@@ -1234,7 +1245,7 @@
     row = shifted(n2[-1:], "seq", 1) if soon_only else n2[-1:]
     out, d_mc, moved, g_hidden, up_f, down_c, *more = channel(
         n2, row, vec, gy, middle, down(4), up(4), kv, hidden,
-        key_shard[soon:], cvalue[soon:], hidden_late,
+        kv2, key_shard[soon:], cvalue[soon:], hidden_late,
     )
     wide = n_dp * cols
     by_piece = lambda rows: jnp.swapaxes(rows.reshape(-1, n_seq, wide), 0, 1)

time: 659 us -> 654 us (level)
  waiting for transfers between devices: 44.3 us -> 0.77 us
  Pallas kernels: 550 us -> 593 us
    pallas_call x1, Pallas kernels: 258 us -> 302 us  [gather(): pl.pallas_call(functools.partial(gather_kernel, ORDERS[:n]), out_shape=[j...]
    all_gather x1, waiting for transfers between devices: 44.2 us -> 0.71 us  [body(): lax.all_gather(jnp.concatenate([key_shard[:most], cvalue[:most]], 0), axe...]
  transfers between devices with their start and end apart: 3 -> 3, of which waited for: 1 -> 1; matrix products, arithmetic and copies ran while one was open for 3% -> 2% of each run, Pallas kernels for 66% -> 71%
where the time goes in v5:
time: 654 us; the launch traced here: 646 us
  Pallas kernels  593 us (91%)
  local copies, waits for them, and re-layouts  21 us (3%)
  between operations  15.6 us (2%)
  other arithmetic  7.85 us (1%)
    pallas_call x1, Pallas kernels, gather(): pl.pallas_call(functools.partial(gather_kernel, ORDERS[:n]), out_shape=[j...  302 us
    pallas_call x6, Pallas kernels, over_tiles(): pl.pallas_call(body, grid=(steps,), in_specs=[made(spec, x.shape) for spe...  291 us
  transfers between devices with their start and end apart: 3, of which 1 were waited for; matrix products, arithmetic and copies ran while one was open for 2% of the time, Pallas kernels for 71%

profile of v5, /device:TPU:1, one launch (start us, length us, event | category | flops | bytes accessed | tf_op | source)
XLA Modules:
  0.0 645.5 jit_solution(2097202653135787725)
XLA Ops:
  7.2 0.0 all-gather.3.cloned.1.call-start
  7.2 1.5 copy.29
  8.7 0.0 slice-start
  8.7 0.1 slice.105
  8.8 1.1 slice-done
  9.9 1.3 pad_maximum_fusion
  11.2 0.0 all-gather.3.cloned.1.call-update
  11.2 0.0 copy-start.8
  11.3 0.0 copy-start.9
  11.3 0.0 slice-start.1
  11.3 0.0 copy-start.3
  11.3 0.0 reduce-scatter.2.cloned.1.call-start
  12.1 0.0 copy-done.11
  12.1 0.6 dynamic-slice
  12.7 0.8 dynamic-update-slice
  13.5 5.1 all-reduce
  18.6 0.0 copy-done.5
  18.6 0.1 fusion.19
  18.7 0.2 copy.33
  18.8 0.2 copy.34
  19.0 0.0 copy-done.7
  19.1 0.3 convolution_convert_fusion
  19.4 0.7 copy.28
  20.1 0.0 copy-done.10
  20.1 0.1 copy.23
  20.2 0.8 concatenate.27.refs_4_
  21.0 0.7 pad_maximum_fusion.4.refs_6_
  21.6 0.0 copy-done.3
  21.7 1.0 slice_bitcast_fusion
  22.6 302.1 %gather_time.1 = (bf16[32,64,2048]{2,1,0:T(8,128)(2,1)}, bf16[32,64,2048]{2,1,0:T(8,128)(2,1)}, bf16[32,64,2048]{2,1,0:T(8,128)(2,1)}, bf16[32,64,2048]{2,1,0:T(...) custom-call(bf16[64,2048]{1,0:T(8,128)(2,1)} %get-tuple-element.133.refs_0_, ...), custom_call_target="tpu_custom_call" | custom-call | tf_op jit(solution)/shard_map/gather_time/pallas_call | solution.py:706
  324.7 2.2 collective-permute-start
  326.9 0.0 copy-start.1
  327.0 3.3 sort_small.1
  330.2 1.7 fusion.18
  331.9 0.7 fusion.11.valid
  332.6 0.6 slice.106.refs_1_
  333.2 0.0 copy-done.1
  333.2 0.7 slice.95.refs_2_
  333.9 0.0 collective-permute-done
  333.9 0.4 convert_reduce_fusion
  334.3 0.7 fusion.2
  335.0 0.5 fusion
  335.5 2.5 fusion.17
  338.0 25.1 %project.1 = (f32[256,2048]{1,0:T(8,128)}, f32[256,2048]{1,0:T(8,128)}, f32[256,2048]{1,0:T(8,128)}, f32[256,2048]{1,0:T(8,128)}, f32[256,2048]{1,0:T(8,128)}, /...) custom-call(f32[256,2048]{1,0:T(8,128)} %get-tuple-element.129.hat, ...), custom_call_target="tpu_custom_call" | custom-call | tf_op jit(solution)/shard_map/project/pallas_call | solution.py:532
  363.1 57.1 %rec_forward.1 = (f32[256,2048]{1,0:T(8,128)}, f32[256,2048]{1,0:T(8,128)}, f32[256,2048]{1,0:T(8,128)}, f32[64,2048]{1,0:T(8,128)}, bf16[256,2048]{1,0:T(8,128)...) custom-call(f32[256,2048]{1,0:T(8,128)} %get-tuple-element.71.rr, ...), custom_call_target="tpu_custom_call" | custom-call | tf_op jit(solution)/shard_map/rec_forward/pallas_call | solution.py:532
  420.2 1.4 slice.89.edge
  421.6 0.7 all-gather.3.cloned.1.call-done
  422.4 92.0 %channel.1 = (bf16[256,2048]{1,0:T(8,128)(2,1)}, f32[256,2048]{1,0:T(8,128)}, f32[8,2048]{1,0:T(8,128)}, f32[32,32,256]{2,1,0:T(8,128)}, f32[16,2048]{1,0:T(8,12...) custom-call(f32[256,2048]{1,0:T(8,128)} %get-tuple-element.78.n2, f32[1,2048]{1,0:T(1,128)} %slice.89.edge, ...), custom_call_target="tpu_custom_call" | custom-call | tf_op jit(solution)/shard_map/channel/pallas_call | solution.py:532
  514.4 1.0 pad_maximum_fusion.3
  515.4 2.5 pad_maximum_fusion.1
  518.0 0.0 reduce-scatter.2.cloned.1.call-update
  518.0 0.1 fusion.12
  518.1 0.1 reshape.101
  518.1 0.1 slice.96
  518.2 0.8 copy.31.rstd
  519.0 70.7 %rec_backward.1 = (f32[256,2048]{1,0:T(8,128)}, bf16[256,2048]{1,0:T(8,128)(2,1)}, f32[16,2048]{1,0:T(8,128)}, f32[16,2048]{1,0:T(8,128)}, bf16[256,2048]{1,0:T(...) custom-call(f32[256,2048]{1,0:T(8,128)} %get-tuple-element.90.d_mc, ...), custom_call_target="tpu_custom_call" | custom-call | tf_op jit(solution)/shard_map/rec_backward/pallas_call | solution.py:532
  589.7 0.0 reduce-scatter.2.cloned.1.call-done
  589.7 0.7 broadcast_in_dim.35.refs_1_
  590.4 42.4 %final.1 = (f32[256,2048]{1,0:T(8,128)}, f32[8,160,64]{2,1,0:T(8,128)}, f32[8,32,256]{2,1,0:T(8,128)}) custom-call(bf16[256,2048]{1,0:T(8,128)(2,1)} %get-tuple-element.102.drr, bf16[256,2048]{1,0:T(8,128)(2,1)} %get-tuple-element.103.dkr, bf16[256,2048]{1,0:T(8,128)(2,1)} %get-tuple-element.104.dvr, bf16[256,2048]{1,0:T(8,128)(2,1)} %get-tuple-element.105.dwl, ...), custom_call_target="tpu_custom_call" | custom-call | tf_op jit(solution)/shard_map/final/pallas_call | solution.py:532
  632.8 2.3 copy.32
  635.2 1.0 copy.45
  636.1 1.3 copy.46
  637.5 0.0 copy-done.6
  637.5 0.7 copy.47
  (25 shorter events, 0.2 us)
Async XLA Ops:
  7.2 415.2 %all-gather.3.cloned.1.call-start = ((), (), s32[]{:S(2)}) async-start(), calls=%async_computation.2 | async-start | bytes 56229888 | tf_op jit(solution)/shard_map/all_gather | solution.py:1155
  8.7 1.2 slice-start
  9.9 2.3 copy-start.11
  9.9 8.7 %copy-start.5 = (bf16[8,160,64]{1,2,0:T(8,128)(2,1)S(1)}, bf16[8,160,64]{1,2,0:T(8,128)(2,1)}, u32[]{:S(2)}) copy-start(bf16[8,160,64]{1,2,0:T(8,128)(2,1)} %param.20) | copy-start | bytes 491524
  11.2 7.8 %copy-start.7 = (bf16[8,32,256]{2,1,0:T(8,128)(2,1)S(1)}, bf16[8,32,256]{2,1,0:T(8,128)(2,1)}, u32[]{:S(2)}) copy-start(bf16[8,32,256]{2,1,0:T(8,128)(2,1)} %param.21) | copy-start | bytes 393220
  11.2 8.9 %copy-start.10 = (bf16[18,64]{1,0:T(8,128)(2,1)S(1)}, bf16[18,64]{1,0:T(8,128)(2,1)}, u32[]{:S(2)}) copy-start(bf16[18,64]{1,0:T(8,128)(2,1)} %param.17) | copy-start | bytes 6916
  11.2 9.0 %copy-start.8 = (bf16[64,448]{1,0:T(8,128)(2,1)S(1)}, bf16[64,448]{1,0:T(8,128)(2,1)}, u32[]{:S(2)}) copy-start(bf16[64,448]{1,0:T(8,128)(2,1)} %param.15) | copy-start | bytes 172036
  11.3 9.0 %copy-start.9 = (bf16[448,64]{0,1:T(8,128)(2,1)S(1)}, bf16[448,64]{0,1:T(8,128)(2,1)}, u32[]{:S(2)}) copy-start(bf16[448,64]{0,1:T(8,128)(2,1)} %param.16) | copy-start | bytes 172036
  11.3 9.7 %slice-start.1 = ((bf16[256,2048]{1,0:T(8,128)(2,1)}), bf16[16,2048]{1,0:T(8,128)(2,1)S(1)}, s32[]{:S(2)}) async-start(bf16[256,2048]{1,0:T(8,128)(2,1)} %param.19), calls=%async_computation.4 | async-start | bytes 131072 | tf_op jit(solution)/shard_map/slice | solution.py:1182
  11.3 10.4 %copy-start.3 = (bf16[4,2048,64]{1,2,0:T(8,128)(2,1)S(1)}, bf16[4,2048,64]{1,2,0:T(8,128)(2,1)}, u32[]{:S(2)}) copy-start(bf16[4,2048,64]{1,2,0:T(8,128)(2,1)} %param.14) | copy-start | bytes 3145732
  11.3 578.4 %reduce-scatter.2.cloned.1.call-start = ((), (), s32[]{:S(2)}) async-start(), calls=%async_computation.1 | async-start | bytes 1622016 | tf_op jit(solution)/shard_map/reduce_scatter | solution.py:1259
  20.1 304.6 %copy-start = (bf16[1,256,2048]{2,1,0:T(8,128)(2,1)S(1)}, bf16[1,256,2048]{2,1,0:T(8,128)(2,1)}, u32[]{:S(2)}) copy-start(bf16[1,256,2048]{2,1,0:T(8,128)(2,1)} %param.11) | copy-start | bytes 3145732
  324.7 9.1 %collective-permute-start = (bf16[1,2048]{1,0:T(2,128)(2,1)S(1)}, bf16[1,2048]{1,0:T(2,128)(2,1)S(1)}, u32[]{:S(2)}, u32[]{:S(2)}) collective-permute-start(bf16[1,2048]{1,0:T(2,128)(2,1)S(1)} %slice.84), channel_id=1, source_target_pairs={{0,4},{4,8},{8,12},{12,16},{16,20},{20,24},{24,28},{1,5},{5,9},{9,... | collective-permute-start | bytes 12296 | tf_op jit(solution)/shard_map/ppermute | solution.py:1128
  326.9 6.3 copy-start.1
  590.4 44.7 %copy-start.4 = (bf16[256,2048]{1,0:T(8,128)(2,1)S(1)}, bf16[256,2048]{1,0:T(8,128)(2,1)}, u32[]{:S(2)}) copy-start(bf16[256,2048]{1,0:T(8,128)(2,1)} %get-tuple-element.83) | copy-start | bytes 3145732
  632.8 3.3 copy-start.2
  636.1 1.3 copy-start.6
Sparse Core Ops, SparseCore 0:
  11.4 410.9 all-gather.2
  518.1 67.2 reduce-scatter.1

commit v6 on v5

--- a/solution.py
+++ b/solution.py
@@ -946,13 +946,14 @@
 
 
 def project_kernel(
-    hat, hat_prev, valid, vec, first, chosen, second, w_r, w_k, w_v, up,
+    hat, edge, valid, vec, first, chosen, second, w_r, w_k, w_v, up,
     rr, kr, vr, wl, al, gg, m_r, m_k, m_v, hs, act, act_low,
 ):
     @pl.when(pl.program_id(0) == 0)
     def _():
         n1 = hat[...] * vec[0:1, :] + vec[1:2, :]
-        change = (hat_prev[...] * vec[0:1, :] + vec[1:2, :]) * valid[...] - n1
+        before = jnp.where(iota(hat.shape, 0) == 0, edge[...], pltpu.roll(hat[...], 1, axis=0))
+        change = (before * vec[0:1, :] + vec[1:2, :]) * valid[...] - n1
         mixed = lambda i: (n1 + change * vec[2 + i : 3 + i, :]).astype(BF)
         m_r[...], m_k[...], m_v[...] = mixed(0), mixed(2), mixed(3)
         for i, m in enumerate((m_r, m_k, m_v)):
@@ -1186,13 +1187,15 @@
     mats[0], tokens = lax.optimization_barrier((mats[0], tokens))
     wide = tokens.astype(F32)
     ahead = shifted(tokens[-1:], "seq", 1).astype(F32)
-    rows = jnp.concatenate([ahead, wide], 0)
-    centre = rows - jnp.mean(rows, axis=-1, keepdims=True)
-    rstd = lax.rsqrt(jnp.mean(centre * centre, axis=-1, keepdims=True) + NORM_EPS)
-    hat = centre * rstd
+    def normal(rows):
+        centre = rows - jnp.mean(rows, axis=-1, keepdims=True)
+        rstd = lax.rsqrt(jnp.mean(centre * centre, axis=-1, keepdims=True) + NORM_EPS)
+        return centre * rstd, rstd
+
+    hat, rstd = normal(wide)
+    row, _ = normal(ahead)
     start = (jnp.arange(length)[:, None] == 0) & (lax.axis_index("seq") == 0)
     valid = jnp.where(start, 0.0, 1.0).astype(F32)
-    hat_prev, hat, rstd = hat[:-1], hat[1:], rstd[1:]
 
     mats = [m.reshape(width, width) for m in mats]
     misc = misc.reshape(width, -1)
@@ -1217,7 +1220,7 @@
     rr, kr, vr, wl, al, gg, m_r, m_k, m_v, hs, act = over_tiles(
         project_kernel, tiles,
         [
-            (whole, hat), (whole, hat_prev), (whole, valid), (whole, vec), (firsts, misc), (whole, chosen),
+            (whole, hat), (whole, row), (whole, valid), (whole, vec), (firsts, misc), (whole, chosen),
             (second_rows, misc), (tile_rows, mats[0]), (tile_rows, mats[1]), (tile_rows, mats[2]), (cut, chosen),
         ],
         [(cut, full)] * 6

time: 654 us -> 653 us (level)
  no operation moved by 1% of the time
where the time goes in v6:
time: 653 us; the launch traced here: 646 us
  Pallas kernels  592 us (91%)
  local copies, waits for them, and re-layouts  18.5 us (3%)
  between operations  16.9 us (3%)
  other arithmetic  10.4 us (2%)
    pallas_call x1, Pallas kernels, gather(): pl.pallas_call(functools.partial(gather_kernel, ORDERS[:n]), out_shape=[j...  302 us
    pallas_call x6, Pallas kernels, over_tiles(): pl.pallas_call(body, grid=(steps,), in_specs=[made(spec, x.shape) for spe...  290 us
  transfers between devices with their start and end apart: 3, of which 1 were waited for; matrix products, arithmetic and copies ran while one was open for 2% of the time, Pallas kernels for 71%

profile of v6, /device:TPU:1, one launch (start us, length us, event | category | flops | bytes accessed | tf_op | source)
XLA Modules:
  0.0 646.1 jit_solution(15473057002540039850)
XLA Ops:
  7.2 0.0 all-gather.3.cloned.1.call-start
  7.2 1.5 copy.29
  8.7 0.0 slice-start
  8.7 0.1 slice.87
  8.8 1.1 slice-done
  9.9 1.3 pad_maximum_fusion
  11.2 0.0 all-gather.3.cloned.1.call-update
  11.2 0.0 copy-start.8
  11.2 0.0 copy-start.9
  11.3 0.0 slice-start.1
  11.3 0.0 copy-start.3
  11.3 0.0 reduce-scatter.2.cloned.1.call-start
  12.1 0.0 copy-done.11
  12.1 0.6 dynamic-slice
  12.7 0.8 dynamic-update-slice
  13.5 5.1 all-reduce
  18.6 0.0 copy-done.5
  18.6 0.1 fusion.19
  18.7 0.2 copy.33
  18.8 0.2 copy.34
  19.1 0.3 convolution_convert_fusion
  19.4 0.7 copy.28
  20.1 0.1 copy.23
  20.2 0.8 concatenate.21.refs_4_
  21.0 0.7 pad_maximum_fusion.3.refs_6_
  21.7 1.0 slice_bitcast_fusion
  22.6 302.1 %gather_time.1 = (bf16[32,64,2048]{2,1,0:T(8,128)(2,1)}, bf16[32,64,2048]{2,1,0:T(8,128)(2,1)}, bf16[32,64,2048]{2,1,0:T(8,128)(2,1)}, bf16[32,64,2048]{2,1,0:T(...) custom-call(bf16[64,2048]{1,0:T(8,128)(2,1)} %get-tuple-element.131.refs_0_, ...), custom_call_target="tpu_custom_call" | custom-call | tf_op jit(solution)/shard_map/gather_time/pallas_call | solution.py:706
  324.8 2.2 collective-permute-start
  326.9 3.2 sort_small.1
  330.2 0.2 convert_reduce_fusion
  330.4 0.4 fusion.2
  330.8 0.0 copy-start.1
  330.8 1.7 fusion.18
  332.6 1.6 fusion.hat
  334.2 0.7 fusion.11.valid
  334.9 0.7 slice.88.refs_1_
  335.5 0.0 copy-done.1
  335.5 0.7 slice.81.refs_2_
  336.2 0.0 collective-permute-done
  336.2 0.6 convert_reduce_fusion.1
  337.4 0.6 multiply_reduce_fusion
  338.7 0.6 fusion.12.edge
  339.3 24.8 %project.1 = (f32[256,2048]{1,0:T(8,128)}, f32[256,2048]{1,0:T(8,128)}, f32[256,2048]{1,0:T(8,128)}, f32[256,2048]{1,0:T(8,128)}, f32[256,2048]{1,0:T(8,128)}, /...) custom-call(f32[256,2048]{1,0:T(8,128)} %fusion.hat, ...), custom_call_target="tpu_custom_call" | custom-call | tf_op jit(solution)/shard_map/project/pallas_call | solution.py:532
  364.1 56.2 %rec_forward.1 = (f32[256,2048]{1,0:T(8,128)}, f32[256,2048]{1,0:T(8,128)}, f32[256,2048]{1,0:T(8,128)}, f32[64,2048]{1,0:T(8,128)}, bf16[256,2048]{1,0:T(8,128)...) custom-call(f32[256,2048]{1,0:T(8,128)} %get-tuple-element.71.rr, ...), custom_call_target="tpu_custom_call" | custom-call | tf_op jit(solution)/shard_map/rec_forward/pallas_call | solution.py:532
  420.3 1.4 slice.75.edge
  421.8 0.6 all-gather.3.cloned.1.call-done
  422.4 92.1 %channel.1 = (bf16[256,2048]{1,0:T(8,128)(2,1)}, f32[256,2048]{1,0:T(8,128)}, f32[8,2048]{1,0:T(8,128)}, f32[32,32,256]{2,1,0:T(8,128)}, f32[16,2048]{1,0:T(8,12...) custom-call(f32[256,2048]{1,0:T(8,128)} %get-tuple-element.78.n2, f32[1,2048]{1,0:T(1,128)} %slice.75.edge, ...), custom_call_target="tpu_custom_call" | custom-call | tf_op jit(solution)/shard_map/channel/pallas_call | solution.py:532
  514.4 1.0 pad_maximum_fusion.2
  515.4 2.6 pad_maximum_fusion.1
  518.0 0.0 reduce-scatter.2.cloned.1.call-update
  518.0 0.8 copy.31.rstd
  518.8 0.1 fusion.13
  518.9 0.1 reshape.117
  519.0 71.9 %rec_backward.1 = (f32[256,2048]{1,0:T(8,128)}, bf16[256,2048]{1,0:T(8,128)(2,1)}, f32[16,2048]{1,0:T(8,128)}, f32[16,2048]{1,0:T(8,128)}, bf16[256,2048]{1,0:T(...) custom-call(f32[256,2048]{1,0:T(8,128)} %get-tuple-element.90.d_mc, ...), custom_call_target="tpu_custom_call" | custom-call | tf_op jit(solution)/shard_map/rec_backward/pallas_call | solution.py:532
  590.9 0.0 reduce-scatter.2.cloned.1.call-done
  590.9 0.7 broadcast_in_dim.37.refs_1_
  591.6 41.8 %final.1 = (f32[256,2048]{1,0:T(8,128)}, f32[8,160,64]{2,1,0:T(8,128)}, f32[8,32,256]{2,1,0:T(8,128)}) custom-call(bf16[256,2048]{1,0:T(8,128)(2,1)} %get-tuple-element.102.drr, bf16[256,2048]{1,0:T(8,128)(2,1)} %get-tuple-element.103.dkr, bf16[256,2048]{1,0:T(8,128)(2,1)} %get-tuple-element.104.dvr, bf16[256,2048]{1,0:T(8,128)(2,1)} %get-tuple-element.105.dwl, ...), custom_call_target="tpu_custom_call" | custom-call | tf_op jit(solution)/shard_map/final/pallas_call | solution.py:532
  633.4 0.0 copy-start.2
  633.4 2.3 copy.32
  635.7 0.0 copy-done.4
  635.7 1.0 copy.45
  636.7 0.0 copy-done.2
  636.7 1.3 copy.46
  638.0 0.7 copy.47
  (26 shorter events, 0.2 us)
Async XLA Ops:
  7.2 415.2 %all-gather.3.cloned.1.call-start = ((), (), s32[]{:S(2)}) async-start(), calls=%async_computation.2 | async-start | bytes 56229888 | tf_op jit(solution)/shard_map/all_gather | solution.py:1156
  8.7 1.2 slice-start
  9.9 2.3 copy-start.11
  9.9 8.7 %copy-start.5 = (bf16[8,160,64]{1,2,0:T(8,128)(2,1)S(1)}, bf16[8,160,64]{1,2,0:T(8,128)(2,1)}, u32[]{:S(2)}) copy-start(bf16[8,160,64]{1,2,0:T(8,128)(2,1)} %param.20) | copy-start | bytes 491524
  11.2 7.8 %copy-start.7 = (bf16[8,32,256]{2,1,0:T(8,128)(2,1)S(1)}, bf16[8,32,256]{2,1,0:T(8,128)(2,1)}, u32[]{:S(2)}) copy-start(bf16[8,32,256]{2,1,0:T(8,128)(2,1)} %param.21) | copy-start | bytes 393220
  11.2 8.9 %copy-start.10 = (bf16[18,64]{1,0:T(8,128)(2,1)S(1)}, bf16[18,64]{1,0:T(8,128)(2,1)}, u32[]{:S(2)}) copy-start(bf16[18,64]{1,0:T(8,128)(2,1)} %param.17) | copy-start | bytes 6916
  11.2 9.0 %copy-start.8 = (bf16[64,448]{1,0:T(8,128)(2,1)S(1)}, bf16[64,448]{1,0:T(8,128)(2,1)}, u32[]{:S(2)}) copy-start(bf16[64,448]{1,0:T(8,128)(2,1)} %param.15) | copy-start | bytes 172036
  11.2 9.0 %copy-start.9 = (bf16[448,64]{0,1:T(8,128)(2,1)S(1)}, bf16[448,64]{0,1:T(8,128)(2,1)}, u32[]{:S(2)}) copy-start(bf16[448,64]{0,1:T(8,128)(2,1)} %param.16) | copy-start | bytes 172036
  11.3 9.7 %slice-start.1 = ((bf16[256,2048]{1,0:T(8,128)(2,1)}), bf16[16,2048]{1,0:T(8,128)(2,1)S(1)}, s32[]{:S(2)}) async-start(bf16[256,2048]{1,0:T(8,128)(2,1)} %param.19), calls=%async_computation.4 | async-start | bytes 131072 | tf_op jit(solution)/shard_map/slice | solution.py:1183
  11.3 10.4 %copy-start.3 = (bf16[4,2048,64]{1,2,0:T(8,128)(2,1)S(1)}, bf16[4,2048,64]{1,2,0:T(8,128)(2,1)}, u32[]{:S(2)}) copy-start(bf16[4,2048,64]{1,2,0:T(8,128)(2,1)} %param.14) | copy-start | bytes 3145732
  11.3 579.6 %reduce-scatter.2.cloned.1.call-start = ((), (), s32[]{:S(2)}) async-start(), calls=%async_computation.1 | async-start | bytes 1622016 | tf_op jit(solution)/shard_map/reduce_scatter | solution.py:1262
  20.1 304.6 %copy-start = (bf16[1,256,2048]{2,1,0:T(8,128)(2,1)S(1)}, bf16[1,256,2048]{2,1,0:T(8,128)(2,1)}, u32[]{:S(2)}) copy-start(bf16[1,256,2048]{2,1,0:T(8,128)(2,1)} %param.11) | copy-start | bytes 3145732
  324.8 11.4 %collective-permute-start = (bf16[1,2048]{1,0:T(2,128)(2,1)S(1)}, bf16[1,2048]{1,0:T(2,128)(2,1)S(1)}, u32[]{:S(2)}, u32[]{:S(2)}) collective-permute-start(bf16[1,2048]{1,0:T(2,128)(2,1)S(1)} %slice.72), channel_id=1, source_target_pairs={{0,4},{4,8},{8,12},{12,16},{16,20},{20,24},{24,28},{1,5},{5,9},{9,... | collective-permute-start | bytes 12296 | tf_op jit(solution)/shard_map/ppermute | solution.py:1129
  330.8 4.7 copy-start.1
  591.6 44.1 %copy-start.4 = (bf16[256,2048]{1,0:T(8,128)(2,1)S(1)}, bf16[256,2048]{1,0:T(8,128)(2,1)}, u32[]{:S(2)}) copy-start(bf16[256,2048]{1,0:T(8,128)(2,1)} %get-tuple-element.83) | copy-start | bytes 3145732
  633.4 3.3 copy-start.2
  636.7 1.3 copy-start.6
Sparse Core Ops, SparseCore 0:
  11.4 410.9 all-gather.2
  518.2 67.5 reduce-scatter.1
